TPU v7x, 32 devices: a whole 2x2x4 slice. The times are simulated.
32 devices in a mesh: det: 4 (over y, x), tm: 8 (over z, core).
Axes of the slice: x: 2, y: 2, z: 4, core: 2. Of those that a mesh axis runs over, the one named last changes fastest.
Arguments:
- detector_data: float32 [128, 65536], P('det', 'tm'), may hold values from -250 to 250
- templates: bfloat16 [8, 16, 65536], P(None, None, 'tm'), may hold values from -5 to 5
- wafer_of: int32 [128], P('det'), may hold values from 0 to 7, as said below
- knee_freq: float32 [128], P(('det', 'tm')), may hold values from 0.1 to 5
- white_level: float32 [128], P(('det', 'tm')), may hold values from 0.5 to 5
- tile_id: int32 [128, 65536], P(('det', 'tm')), may hold values from 0 to 15
- pixel_id: int32 [128, 65536], P(('det', 'tm')), may hold values from 0 to 127
- tile_order: int32 [16], replicated, may hold values from 0 to 15, each once
Outputs:
- fit_amps: float32 [16, 128], P(None, 'det')
- weighted_data: bfloat16 [128, 65536], P(('det', 'tm'))
- sky_map: float32 [2048], P('tm')
- weight_map: float32 [2048], P('tm')
Inputs may be any that keep to these rules, and one draw needn't show every extreme that they name: `wafer_of`: the detectors of each aligned run of 16 share one wafer, and each wafer has exactly one such run.
All inputs are finite; a program needn't handle non-finite values.
Results may differ from a plain program's by a relative error of at most 0.0016.
Values sent between devices are 32-bit elements; how exact they have to be, the bound alone decides.
No kernel may reach another device: no remote copies, remote signals or barrier semaphores. Data moves between devices by JAX's collectives and lax.ppermute only.
A program may use at most 64 MiB of HBM per device.

v0:
```python
import functools
import math

import jax
import jax.numpy as jnp
import numpy as np
from jax import lax
from jax.experimental import pallas as pl
from jax.experimental.pallas import tpu as pltpu
from jax.sharding import PartitionSpec as P

PIX = 128
COLS = 256
LANES = 128
HALVES = COLS // LANES
LOW = 64
SAMPLE_RATE = 200.0
MIB = 1024 * 1024
NT = (((1,), (1,)), ((), ()))
f32 = jnp.float32
bf16 = jnp.bfloat16


def split2(x):
    high = x.astype(bf16)
    return high, (x - high.astype(f32)).astype(bf16)


def split3(x):
    high = x.astype(bf16)
    rest = x - high.astype(f32)
    mid = rest.astype(bf16)
    return high, mid, (rest - mid.astype(f32)).astype(bf16)


def host_split(x):
    high = x.astype(np.float32).astype(bf16)
    low = (x - high.astype(np.float64)).astype(np.float32).astype(bf16)
    return high, low


@functools.lru_cache(maxsize=None)
def tables(rows):
    total = rows * COLS
    half = rows // 2
    slots = np.arange(half)
    slots[0] = half
    ramp = np.arange(rows)
    angle = 2.0 * np.pi * (slots[:, None] * ramp[None, :] % rows) / rows
    first = np.concatenate([np.cos(angle), -np.sin(angle)], axis=0)
    first[half] = 1.0
    weight = np.full((half,), 2.0)
    weight[0] = 1.0
    last = np.concatenate([weight[:, None] * np.cos(angle), -2.0 * np.sin(angle)], axis=0)
    last[half] = 1.0
    last = last.T / total
    col = np.arange(COLS)
    phase = 2.0 * np.pi * (col[:, None] * col[None, :] % COLS) / COLS
    side = np.concatenate([np.cos(phase), np.sin(phase)], axis=1)
    turn = 2.0 * np.pi * (slots[:, None] * col[None, :] % total) / total
    bins = np.concatenate([slots, np.zeros((16,), np.int64)])[:, None] + rows * col[None, :]
    freq = np.minimum(bins, total - bins).astype(np.float32) * np.float32(SAMPLE_RATE / total)
    return (
        *host_split(first),
        *host_split(side),
        *host_split(last),
        np.cos(turn).astype(np.float32),
        np.sin(turn).astype(np.float32),
        (freq * freq).astype(np.float32),
    )


def dot3(left, right, lhs_const):
    (lh, ll), (rh, rl) = left, right
    return jnp.dot(
        jnp.concatenate([lh, ll, lh], axis=1),
        jnp.concatenate([rh, rh, rl], axis=0),
        preferred_element_type=f32,
    )


def fit_kernel(runs, run_len, wafer_ref, *refs):
    data_ref, template_refs, out_ref = refs[0], refs[1:-1], refs[-1]
    parts = []
    for run in range(runs):
        temp = template_refs[run][0]
        modes = temp.shape[0]
        high, mid, low = split3(data_ref[run * run_len : (run + 1) * run_len, :])
        both = lax.dot_general(
            temp, jnp.concatenate([temp, high, mid, low], axis=0), NT, preferred_element_type=f32
        )
        ends = [modes + i * run_len for i in range(4)]
        parts.append(both[:, :modes])
        parts.append(
            both[:, ends[0] : ends[1]] + both[:, ends[1] : ends[2]] + both[:, ends[2] : ends[3]]
        )
    part = jnp.concatenate(parts, axis=1)

    @pl.when(pl.program_id(0) == 0)
    def _():
        out_ref[...] = part

    @pl.when(pl.program_id(0) > 0)
    def _():
        out_ref[...] += part


def residual_kernel(runs, run_len, owners, split_out, scalar_ref, sums_ref, data_ref, *refs):
    template_refs = refs[:runs]
    amps_ref, out_refs, rows_ref = refs[runs], refs[runs + 1 : -1], refs[-1]
    modes = template_refs[0].shape[1]
    row_count, time_local = data_ref.shape
    pieces = time_local // COLS
    width = modes + run_len
    row_index = lax.broadcasted_iota(jnp.int32, (modes, width), 0)
    joined = [sums_ref[:, run * width : (run + 1) * width] for run in range(runs)]
    for column in range(modes):
        for run in range(runs):
            now = joined[run]
            pivot_row = now[column : column + 1, :] / now[column : column + 1, column : column + 1]
            rest = now - now[:, column : column + 1] * pivot_row
            joined[run] = jnp.where(row_index == column, pivot_row, rest)
    amps = [now[:, modes:] for now in joined]
    amps_ref[...] = jnp.concatenate(amps, axis=1)
    for run in range(runs):
        temp = template_refs[run][0]
        left = jnp.concatenate(split3(amps[run].T), axis=1)
        fitted = jnp.dot(left, jnp.concatenate([temp] * 3, axis=0), preferred_element_type=f32)
        rows = slice(run * run_len, (run + 1) * run_len)
        for lane in range(time_local // LANES):
            cols = slice(lane * LANES, (lane + 1) * LANES)
            start = (lane % HALVES * pieces + lane // HALVES) * row_count + run * run_len
            rows_ref[start : start + run_len, :] = data_ref[rows, cols] - fitted[:, cols]
    local_dets = row_count // owners
    me = scalar_ref[row_count]
    for step in range(owners):
        owner = jnp.bitwise_xor(me, step) if split_out else step
        for det in range(local_dets):
            block = take_rows(rows_ref, owner * local_dets + det, pieces, row_count)
            if split_out:
                out_refs[step][det] = block
            else:
                out_refs[0][step, det] = block


def take_rows(ref, start, count, stride):
    return jnp.concatenate(
        [
            ref[pl.ds(side * count * stride + start, count, stride=stride), :]
            for side in range(HALVES)
        ],
        axis=1,
    )


def one_hot_pair(high_rows, low_rows, value_rows, tall):
    high_ramp = lax.broadcasted_iota(jnp.int32, (tall, COLS), 0).astype(f32).astype(bf16)
    low_ramp = lax.broadcasted_iota(jnp.int32, (LOW, COLS), 0).astype(f32).astype(bf16)
    lefts, rights = [], []
    for row in range(high_rows.shape[0]):
        high = jnp.broadcast_to(high_rows[row : row + 1], (tall, COLS)).astype(bf16)
        low = jnp.broadcast_to(low_rows[row : row + 1], (LOW, COLS)).astype(bf16)
        if value_rows.shape[0] == 1:
            value = jnp.broadcast_to(value_rows, (tall, COLS)).astype(bf16)
        else:
            value = jnp.broadcast_to(value_rows[row : row + 1], (tall, COLS)).astype(bf16)
        lefts.append(jnp.where(high == high_ramp, value, jnp.zeros_like(value)))
        rights.append(jnp.where(low == low_ramp, jnp.ones_like(low), jnp.zeros_like(low)))
    return lax.dot_general(
        jnp.concatenate(lefts, axis=1),
        jnp.concatenate(rights, axis=1),
        NT,
        preferred_element_type=f32,
    )


def weight_kernel(tall, white_ref, after_ref, tile_ref, pixel_ref, high_ref, low_ref, out_ref, hi_s, lo_s):
    local_dets, rows = high_ref.shape[0], high_ref.shape[1]
    cell = tile_ref[...] * PIX + pixel_ref[...]
    high = jnp.right_shift(cell, LOW.bit_length() - 1).astype(f32)
    low = jnp.bitwise_and(cell, LOW - 1).astype(f32)
    for lane in range(rows * HALVES):
        cols = slice(lane * LANES, (lane + 1) * LANES)
        start = (lane % HALVES * rows + lane // HALVES) * local_dets
        hi_s[start : start + local_dets, :] = high[:, cols]
        lo_s[start : start + local_dets, :] = low[:, cols]
    for det in range(local_dets):
        high_ref[det] = take_rows(hi_s, det, rows, local_dets)
        low_ref[det] = take_rows(lo_s, det, rows, local_dets)
    out_ref[...] = jnp.zeros_like(out_ref)
    chunk = min(64, rows)

    @pl.loop(0, local_dets)
    def _(det):
        value = jnp.full((1, COLS), white_ref[det], f32)

        @pl.loop(0, rows // chunk)
        def _(turn):
            here = pl.ds(pl.multiple_of(turn * chunk, chunk), chunk)
            out_ref[...] += one_hot_pair(high_ref[det, here], low_ref[det, here], value, tall)


def filter_kernel(parts, place_ref, order_ref, knee_ref, white_ref, *refs):
    part_refs = refs[:parts]
    (high_ref, low_ref, wsum_ref, f_h, f_l, s_h, s_l, l_h, l_l, tc_ref, ts_ref, sq_ref) = refs[
        parts : parts + 12
    ]
    out_ref, sky_ref, weight_ref, signal, stacked, totals = refs[parts + 12 :]
    det = pl.program_id(0)
    local_dets = pl.num_programs(0)
    dets = out_ref.shape[0]
    rows = signal.shape[0]
    half = rows // 2
    for part in range(parts):
        height = part_refs[part].shape[1]
        start = place_ref[part] * height if parts > 1 else 0
        if parts > 1:
            start = pl.multiple_of(start, height)
        signal[pl.ds(start, height), :] = part_refs[part][0]
    row_index = lax.broadcasted_iota(jnp.int32, (half, COLS), 0)
    turn_cos, turn_sin = tc_ref[...], ts_ref[...]
    side = (s_h[...], s_l[...])
    first = dot3((f_h[...], f_l[...]), split2(signal[...]), True)
    real_y, low_y = first[:half], first[half:]
    imag_y = jnp.where(row_index == 0, 0.0, low_y)
    zero_y = jnp.broadcast_to(low_y[0:1], (16, COLS))
    real_z = real_y * turn_cos + imag_y * turn_sin
    imag_z = imag_y * turn_cos - real_y * turn_sin
    forward = dot3(split2(jnp.concatenate([real_z, imag_z, zero_y], axis=0)), side, False)
    cos_f, sin_f = forward[:, :COLS], forward[:, COLS:]
    squared = sq_ref[...]
    knee = knee_ref[det]
    gain = squared / (white_ref[det] * (squared + knee * knee))
    gain_main, gain_zero = gain[:half], gain[half:]
    real_x = (cos_f[:half] + sin_f[half : 2 * half]) * gain_main
    imag_x = (cos_f[half : 2 * half] - sin_f[:half]) * gain_main
    zero_r = cos_f[2 * half :] * gain_zero
    zero_i = -sin_f[2 * half :] * gain_zero
    back = dot3(split2(jnp.concatenate([real_x, imag_x, zero_r, zero_i], axis=0)), side, False)
    cos_b, sin_b = back[:, :COLS], back[:, COLS:]
    real_u = cos_b[:half] - sin_b[half : 2 * half]
    imag_u = sin_b[:half] + cos_b[half : 2 * half]
    zero_o = cos_b[2 * half : 2 * half + 16] - sin_b[2 * half + 16 :]
    real_v = real_u * turn_cos - imag_u * turn_sin
    imag_v = real_u * turn_sin + imag_u * turn_cos
    imag_v = jnp.where(row_index == 0, zero_o[0:1], imag_v)
    result = dot3((l_h[...], l_l[...]), split2(jnp.concatenate([real_v, imag_v], axis=0)), True)
    signal[...] = result
    for side_half in range(HALVES):
        cols = slice(side_half * LANES, (side_half + 1) * LANES)
        stacked[pl.ds(side_half * rows * dets + det, rows, stride=dets), :] = result[:, cols]

    @pl.when(det == 0)
    def _():
        totals[...] = jnp.zeros_like(totals)

    chunk = min(64, rows)

    @pl.loop(0, rows // chunk)
    def _(turn):
        here = pl.ds(pl.multiple_of(turn * chunk, chunk), chunk)
        totals[...] += one_hot_pair(
            high_ref[0, here], low_ref[0, here], signal[here, :], totals.shape[0]
        )

    @pl.when(det == local_dets - 1)
    def _():
        for lane in range(rows * HALVES):
            start = (lane % HALVES * rows + lane // HALVES) * dets
            out_ref[:, lane * LANES : (lane + 1) * LANES] = stacked[
                start : start + dets, :
            ].astype(bf16)
        per_tile = PIX // LOW
        for tile in range(sky_ref.shape[0]):
            source = order_ref[tile] * per_tile
            for piece in range(per_tile):
                cols = slice(piece * LOW, (piece + 1) * LOW)
                sky_ref[tile : tile + 1, cols] = totals[pl.ds(source + piece, 1), :]
                weight_ref[tile : tile + 1, cols] = wsum_ref[pl.ds(source + piece, 1), :]


def swap(x, step, axis):
    size = lax.axis_size(axis)
    return lax.ppermute(x, axis, [(i, i ^ step) for i in range(size)])


def vmem(limit):
    return pltpu.CompilerParams(vmem_limit_bytes=limit * MIB)


def shards(
    detector_data, templates, wafer_of, knee_freq, white_level, tile_id, pixel_id, tile_order
):
    row_count, time_local = detector_data.shape
    wafer_count, modes, _ = templates.shape
    owners, groups = lax.axis_size("tm"), lax.axis_size("det")
    run_len = min(row_count, row_count * groups // wafer_count)
    runs = row_count // run_len
    width = runs * (modes + run_len)
    local_dets = row_count // owners
    full_length = time_local * owners
    rows = full_length // COLS
    pieces = time_local // COLS
    me = lax.axis_index("tm").astype(jnp.int32)
    power = owners & (owners - 1) == 0

    step_len = min(2048, time_local)

    def template_spec(run, blocked):
        length = step_len if blocked else time_local
        return pl.BlockSpec(
            (1, modes, length),
            lambda i, w, run=run: (w[run * run_len], 0, i if blocked else 0),
        )

    sums = pl.pallas_call(
        functools.partial(fit_kernel, runs, run_len),
        out_shape=jax.ShapeDtypeStruct((modes, width), f32),
        grid_spec=pltpu.PrefetchScalarGridSpec(
            num_scalar_prefetch=1,
            grid=(time_local // step_len,),
            in_specs=[pl.BlockSpec((row_count, step_len), lambda i, w: (0, i))]
            + [template_spec(run, True) for run in range(runs)],
            out_specs=pl.BlockSpec((modes, width), lambda i, w: (0, 0)),
        ),
        compiler_params=vmem(24),
        name="fit_sums",
    )(wafer_of, detector_data, *[templates] * runs)
    if power:
        step = 1
        while step < owners:
            sums = sums + swap(sums, step, "tm")
            step *= 2
    else:
        sums = lax.psum(sums, "tm")

    split_out = power and owners <= 8
    block_shape = (local_dets, pieces, COLS)
    if split_out:
        out_blocks = [jax.ShapeDtypeStruct(block_shape, f32)] * owners
        block_specs = [pl.BlockSpec(block_shape, lambda i, w: (0, 0, 0))] * owners
    else:
        out_blocks = [jax.ShapeDtypeStruct((owners, *block_shape), f32)]
        block_specs = [pl.BlockSpec((owners, *block_shape), lambda i, w: (0, 0, 0, 0))]
    fit_amps, *blocks = pl.pallas_call(
        functools.partial(residual_kernel, runs, run_len, owners, split_out),
        out_shape=[jax.ShapeDtypeStruct((modes, row_count), f32), *out_blocks],
        grid_spec=pltpu.PrefetchScalarGridSpec(
            num_scalar_prefetch=1,
            grid=(1,),
            in_specs=[
                pl.BlockSpec((modes, width), lambda i, w: (0, 0)),
                pl.BlockSpec((row_count, time_local), lambda i, w: (0, 0)),
            ]
            + [template_spec(run, False) for run in range(runs)],
            out_specs=[pl.BlockSpec((modes, row_count), lambda i, w: (0, 0)), *block_specs],
            scratch_shapes=[pltpu.VMEM((HALVES * pieces * row_count, LANES), f32)],
        ),
        compiler_params=vmem(32),
        name="residual",
    )(jnp.concatenate([wafer_of, me[None]]), sums, detector_data, *[templates] * runs)

    if split_out:
        received = [blocks[0]] + [None] * (owners - 1)
        for step in reversed(range(1, owners)):
            received[step] = swap(blocks[step], step, "tm")
        place = jnp.bitwise_xor(me, jnp.arange(owners, dtype=jnp.int32))
    else:
        moved = lax.all_to_all(blocks[0], "tm", split_axis=0, concat_axis=0, tiled=True)
        received = [jnp.swapaxes(moved, 0, 1).reshape(local_dets, rows, COLS)]
        place = jnp.zeros((1,), jnp.int32)

    tile_count = tile_order.shape[0]
    tall = tile_count * PIX // LOW
    inverse_white = (1.0 / white_level).astype(bf16).astype(f32)
    smem = pl.BlockSpec(memory_space=pltpu.SMEM)
    whole = pl.BlockSpec(memory_space=pltpu.VMEM)
    cells = local_dets * full_length
    high, low, weight_sum = pl.pallas_call(
        functools.partial(weight_kernel, tall),
        out_shape=[
            jax.ShapeDtypeStruct((local_dets, rows, COLS), f32),
            jax.ShapeDtypeStruct((local_dets, rows, COLS), f32),
            jax.ShapeDtypeStruct((tall, LOW), f32),
        ],
        in_specs=[smem, pl.BlockSpec(memory_space=pl.ANY), whole, whole],
        out_specs=[whole] * 3,
        scratch_shapes=[pltpu.VMEM((HALVES * rows * local_dets, LANES), f32)] * 2,
        compiler_params=vmem(32),
        cost_estimate=pl.CostEstimate(
            flops=2 * cells * tall * LOW * 8, bytes_accessed=16 * cells, transcendentals=0
        ),
        name="weights",
    )(inverse_white, fit_amps, tile_id, pixel_id)

    consts = [jnp.asarray(t) for t in tables(rows)]
    parts = len(received)
    fixed2 = lambda i, *_: (0, 0)
    by_det = lambda i, *_: (i, 0, 0)
    weighted_data, sky_part, weight_part = pl.pallas_call(
        functools.partial(filter_kernel, parts),
        out_shape=[
            jax.ShapeDtypeStruct((local_dets, full_length), bf16),
            jax.ShapeDtypeStruct((tile_count, PIX), f32),
            jax.ShapeDtypeStruct((tile_count, PIX), f32),
        ],
        grid_spec=pltpu.PrefetchScalarGridSpec(
            num_scalar_prefetch=4,
            grid=(local_dets,),
            in_specs=[pl.BlockSpec((1, *r.shape[1:]), by_det) for r in received]
            + [pl.BlockSpec((1, rows, COLS), by_det)] * 2
            + [pl.BlockSpec((tall, LOW), fixed2)]
            + [pl.BlockSpec(c.shape, fixed2) for c in consts],
            out_specs=[
                pl.BlockSpec((local_dets, full_length), fixed2),
                pl.BlockSpec((tile_count, PIX), fixed2),
                pl.BlockSpec((tile_count, PIX), fixed2),
            ],
            scratch_shapes=[
                pltpu.VMEM((rows, COLS), f32),
                pltpu.VMEM((HALVES * rows * local_dets, LANES), f32),
                pltpu.VMEM((tall, LOW), f32),
            ],
        ),
        compiler_params=vmem(48),
        name="filter_and_bin",
    )(place, tile_order, knee_freq, white_level, *received, high, low, weight_sum, *consts)

    owned = tile_count * PIX // owners
    both = jnp.concatenate(
        [sky_part.reshape(owners, owned), weight_part.reshape(owners, owned)], axis=1
    )
    spread = jnp.broadcast_to(both[None], (groups, *both.shape)).reshape(groups * owners, 2 * owned)
    spread = lax.all_to_all(spread, ("det", "tm"), split_axis=0, concat_axis=0, tiled=True)
    scale = float(tile_count * PIX) / float(local_dets * groups * owners * full_length)
    summed = jnp.sum(spread, axis=0) * scale
    return (fit_amps, weighted_data, summed[:owned], summed[owned:])


def solution(mesh):
    in_specs = (
        P("det", "tm"),
        P(None, None, "tm"),
        P("det"),
        P(("det", "tm")),
        P(("det", "tm")),
        P(("det", "tm"), None),
        P(("det", "tm"), None),
        P(),
    )
    out_specs = (P(None, "det"), P(("det", "tm"), None), P("tm"), P("tm"))
    return jax.shard_map(shards, mesh=mesh, in_specs=in_specs, out_specs=out_specs, check_vma=False)
```

profile of v0, /device:TPU:0, one launch (start us, length us, event | category | flops | bytes accessed | tf_op | source)
XLA Modules:
  0.0 81.4 jit_solution(1121110660010978551)
XLA Ops:
  0.6 1.6 %copy-done = bf16[8,16,8192]{2,1,0:T(8,128)(2,1)S(1)} copy-done((bf16[8,16,8192]{2,1,0:T(8,128)(2,1)S(1)}, bf16[8,16,8192]{2,1,0:T(8,128)(2,1)}, u32[]{:S(2)}) %copy-start) | copy-done | bytes 2097176
  2.2 1.2 %copy-done.2 = f32[32,8192]{1,0:T(8,128)S(1)} copy-done((f32[32,8192]{1,0:T(8,128)S(1)}, f32[32,8192]{1,0:T(8,128)}, u32[]{:S(2)}) %copy-start.2) | copy-done | bytes 1048600
  3.5 0.7 copy-done.16
  4.1 2.3 %fit_sums.1 = f32[16,64]{1,0:T(8,128)S(1)} custom-call(s32[32]{0:T(128)S(1)} %copy-done.16, f32[32,8192]{1,0:T(8,128)S(1)} %copy-done.2, bf16[8,16,8192]{2,1,0:T(8,128)(2,1)S(1)} %copy-done, bf16[8,16,8192]{2,1,0:T(8,128)(2,1)S(1)} %copy-done), custom_call_target="tpu_custom_call" | custom-call | tf_op jit(solution)/shard_map/fit_sums/pallas_call | solution.py:316
  6.4 0.5 collective-permute-start
  6.9 0.8 %collective-permute-done = f32[16,64]{1,0:T(8,128)S(1)} collective-permute-done((f32[16,64]{1,0:T(8,128)S(1)}, f32[16,64]{1,0:T(8,128)S(1)}, u32[]{:S(2)}, u32[]{:S(2)}) %collective-permute-start) | collective-permute-done | bytes 4128 | tf_op jit(solution)/shard_map/ppermute | solution.py:284
  7.7 2.9 %collective-permute-start.1 = (f32[16,64]{1,0:T(8,128)S(1)}, f32[16,64]{1,0:T(8,128)S(1)}, u32[]{:S(2)}, u32[]{:S(2)}) collective-permute-start(f32[16,64]{1,0:T(8,128)S(1)} %add.9), channel_id=1, source_target_pairs={{0,2},{1,3},{2,0},{3,1},{4,6},{5,7},{6,4},{7,5},{8,10},{9,11},{10,... | collective-permute-start | bytes 12296 | tf_op jit(solution)/shard_map/ppermute | solution.py:284
  10.6 1.6 %collective-permute-done.1 = f32[16,64]{1,0:T(8,128)S(1)} collective-permute-done((f32[16,64]{1,0:T(8,128)S(1)}, f32[16,64]{1,0:T(8,128)S(1)}, u32[]{:S(2)}, u32[]{:S(2)}) %collective-permute-start.1) | collective-permute-done | bytes 4128 | tf_op jit(solution)/shard_map/ppermute | solution.py:284
  12.3 3.0 %collective-permute-start.2 = (f32[16,64]{1,0:T(8,128)S(1)}, f32[16,64]{1,0:T(8,128)S(1)}, u32[]{:S(2)}, u32[]{:S(2)}) collective-permute-start(f32[16,64]{1,0:T(8,128)S(1)} %add.10), channel_id=1, source_target_pairs={{0,4},{1,5},{2,6},{3,7},{4,0},{5,1},{6,2},{7,3},{8,12},{9,13},{10,... | collective-permute-start | bytes 12296 | tf_op jit(solution)/shard_map/ppermute | solution.py:284
  15.3 0.1 pad_add_fusion.scalar_ref
  15.4 1.6 %collective-permute-done.2 = f32[16,64]{1,0:T(8,128)S(1)} collective-permute-done((f32[16,64]{1,0:T(8,128)S(1)}, f32[16,64]{1,0:T(8,128)S(1)}, u32[]{:S(2)}, u32[]{:S(2)}) %collective-permute-start.2) | collective-permute-done | bytes 4128 | tf_op jit(solution)/shard_map/ppermute | solution.py:284
  17.0 0.0 copy-start.18
  17.0 0.0 copy-start.19
  17.0 3.7 %residual.1 = (f32[16,32]{1,0:T(8,128)}, f32[4,32,256]{2,1,0:T(8,128)S(1)}, f32[4,32,256]{2,1,0:T(8,128)S(1)}, f32[4,32,256]{2,1,0:T(8,128)S(1)}, f32[4,32,256]{...) custom-call(s32[33]{0:T(128)S(1)} %pad_add_fusion.scalar_ref, ...), custom_call_target="tpu_custom_call" | custom-call | tf_op jit(solution)/shard_map/residual/pallas_call | solution.py:345
  20.7 1.9 %collective-permute-start.4 = (f32[4,32,256]{2,1,0:T(8,128)S(1)}, f32[4,32,256]{2,1,0:T(8,128)S(1)}, u32[]{:S(2)}, u32[]{:S(2)}) collective-permute-start(f32[4,32,256]{2,1,0:T(8,128)S(1)} %get-tuple-element.22), channel_id=1, source_target_pairs={{0,2},{1,3},{2,0},{3,1},{4,6},{5,7},{6,4},{7,5},{8,10},{9,11},{10,... | collective-permute-start | bytes 393224 | tf_op jit(solution)/shard_map/ppermute | solution.py:284
  22.6 0.2 collective-permute-start.5
  22.8 2.7 %collective-permute-start.6 = (f32[4,32,256]{2,1,0:T(8,128)S(1)}, f32[4,32,256]{2,1,0:T(8,128)S(1)}, u32[]{:S(2)}, u32[]{:S(2)}) collective-permute-start(f32[4,32,256]{2,1,0:T(8,128)S(1)} %get-tuple-element.24), channel_id=1, source_target_pairs={{0,4},{1,5},{2,6},{3,7},{4,0},{5,1},{6,2},{7,3},{8,12},{9,13},{10,... | collective-permute-start | bytes 393224 | tf_op jit(solution)/shard_map/ppermute | solution.py:284
  25.6 3.5 %collective-permute-start.8 = (f32[4,32,256]{2,1,0:T(8,128)S(1)}, f32[4,32,256]{2,1,0:T(8,128)S(1)}, u32[]{:S(2)}, u32[]{:S(2)}) collective-permute-start(f32[4,32,256]{2,1,0:T(8,128)S(1)} %get-tuple-element.26), channel_id=1, source_target_pairs={{0,6},{1,7},{2,4},{3,5},{4,2},{5,3},{6,0},{7,1},{8,14},{9,15},{10,... | collective-permute-start | bytes 393224 | tf_op jit(solution)/shard_map/ppermute | solution.py:284
  29.1 3.0 %collective-permute-done.4.refs_2_ = f32[4,32,256]{2,1,0:T(8,128)S(1)} collective-permute-done((f32[4,32,256]{2,1,0:T(8,128)S(1)}, f32[4,32,256]{2,1,0:T(8,128)S(1)}, u32[]{:S(2)}, u32[]{:S(2)}) %collective-permute-start.4) | collective-permute-done | bytes 131104 | tf_op jit(solution)/shard_map/ppermute | solution.py:284
  32.1 0.0 copy-start.20
  32.1 0.7 copy-done.20
  32.8 0.0 copy-start.8
  32.8 0.0 copy-start.9
  32.8 0.0 copy-start.10
  32.8 0.0 copy-start.11
  32.8 0.0 copy-start.12
  32.9 12.3 %weights.1 = (f32[4,256,256]{2,1,0:T(8,128)S(1)}, f32[4,256,256]{2,1,0:T(8,128)S(1)}, f32[32,64]{1,0:T(8,128)S(1)}) custom-call(f32[4]{0:T(128)S(1)} %convert_convert_fusion.white_ref, f32[16,32]{1,0:T(8,128)S(1)} %copy-done.20, s32[4,65536]{1,0:T(4,128)S(1)} %copy-done.18, s32[4,65536]{1,0:T(4,128)S(1)} %copy-done.19), custom_call_target="tpu_custom_call" | custom-call | flops 8589934592 | bytes 4194304 | tf_op jit(solution)/shard_map/weights/pallas_call | solution.py:379
  45.3 19.6 %filter_and_bin.1 = (bf16[4,65536]{1,0:T(4,128)(2,1)}, f32[16,128]{1,0:T(8,128)S(1)}, f32[16,128]{1,0:T(8,128)S(1)}) custom-call(s32[8]{0:T(128)S(1)} %iota_xor_fusion.place_ref, s32[16]{0:T(128)S(1)} %copy-done.13, f32[4]{0:T(128)S(1)} %copy-done.14, f32[4]{0:T(128)S(1)} %copy-done.15, f32[4,32,256]{2,1,0:T(8,128)S(1)} %get-tuple-element.20.refs_0_, ...), custom_call_target="tpu_custom_call" | custom-call | tf_op jit(solution)/shard_map/filter_and_bin/pallas_call | solution.py:400
  65.0 0.1 all_to_all.6
  65.1 15.6 %all_to_all.9 = f32[32,1,512]{2,1,0:T(1,128)S(1)} all-to-all(f32[32,1,512]{2,1,0:T(1,128)S(1)} %all_to_all.6), channel_id=1, replica_groups=mesh['det'=4,'tm'=8] {'det','tm'}, dimensions={0} | all-to-all | bytes 131072 | tf_op jit(solution)/shard_map/all_to_all | solution.py:434
  80.7 0.1 reduce_sum.9
  80.8 0.6 fusion
  (49 shorter events, 0.1 us)
Async XLA Ops:
  0.6 1.6 %copy-start = (bf16[8,16,8192]{2,1,0:T(8,128)(2,1)S(1)}, bf16[8,16,8192]{2,1,0:T(8,128)(2,1)}, u32[]{:S(2)}) copy-start(bf16[8,16,8192]{2,1,0:T(8,128)(2,1)} %refs_1_.3) | copy-start | bytes 6291460
  2.2 1.2 %copy-start.2 = (f32[32,8192]{1,0:T(8,128)S(1)}, f32[32,8192]{1,0:T(8,128)}, u32[]{:S(2)}) copy-start(f32[32,8192]{1,0:T(8,128)} %data_ref.1) | copy-start | bytes 3145732
  3.4 0.7 copy-start.16
  4.1 11.2 %copy-start.17 = (s32[32]{0:T(128)S(1)}, s32[32]{0:T(128)}, u32[]{:S(2)}) copy-start(s32[32]{0:T(128)} %wafer_ref.1) | copy-start | bytes 388
  4.1 12.8 %copy-start.1 = (bf16[8,16,8192]{2,1,0:T(8,128)(2,1)S(1)}, bf16[8,16,8192]{2,1,0:T(8,128)(2,1)}, u32[]{:S(2)}) copy-start(bf16[8,16,8192]{2,1,0:T(8,128)(2,1)} %refs_1_.3) | copy-start | bytes 6291460
  4.1 12.8 %copy-start.3 = (f32[32,8192]{1,0:T(8,128)S(1)}, f32[32,8192]{1,0:T(8,128)}, u32[]{:S(2)}) copy-start(f32[32,8192]{1,0:T(8,128)} %data_ref.1) | copy-start | bytes 3145732
  6.4 1.3 %collective-permute-start = (f32[16,64]{1,0:T(8,128)S(1)}, f32[16,64]{1,0:T(8,128)S(1)}, u32[]{:S(2)}, u32[]{:S(2)}) collective-permute-start(f32[16,64]{1,0:T(8,128)S(1)} %fit_sums.1), channel_id=1, source_target_pairs={{0,1},{1,0},{2,3},{3,2},{4,5},{5,4},{6,7},{7,6},{8,9},{9,8},{10,11... | collective-permute-start | bytes 12296 | tf_op jit(solution)/shard_map/ppermute | solution.py:284
  7.7 4.5 %collective-permute-start.1 = (f32[16,64]{1,0:T(8,128)S(1)}, f32[16,64]{1,0:T(8,128)S(1)}, u32[]{:S(2)}, u32[]{:S(2)}) collective-permute-start(f32[16,64]{1,0:T(8,128)S(1)} %add.9), channel_id=1, source_target_pairs={{0,2},{1,3},{2,0},{3,1},{4,6},{5,7},{6,4},{7,5},{8,10},{9,11},{10,... | collective-permute-start | bytes 12296 | tf_op jit(solution)/shard_map/ppermute | solution.py:284
  12.3 4.7 %collective-permute-start.2 = (f32[16,64]{1,0:T(8,128)S(1)}, f32[16,64]{1,0:T(8,128)S(1)}, u32[]{:S(2)}, u32[]{:S(2)}) collective-permute-start(f32[16,64]{1,0:T(8,128)S(1)} %add.10), channel_id=1, source_target_pairs={{0,4},{1,5},{2,6},{3,7},{4,0},{5,1},{6,2},{7,3},{8,12},{9,13},{10,... | collective-permute-start | bytes 12296 | tf_op jit(solution)/shard_map/ppermute | solution.py:284
  16.9 5.7 %copy-start.15 = (f32[4]{0:T(128)S(1)}, f32[4]{0:T(128)}, u32[]{:S(2)}) copy-start(f32[4]{0:T(128)} %white_ref.1) | copy-start | bytes 52
  17.0 15.1 %copy-start.18 = (s32[4,65536]{1,0:T(4,128)S(1)}, s32[4,65536]{1,0:T(4,128)}, u32[]{:S(2)}) copy-start(s32[4,65536]{1,0:T(4,128)} %tile_ref.1) | copy-start | bytes 3145732
  17.0 15.1 %copy-start.19 = (s32[4,65536]{1,0:T(4,128)S(1)}, s32[4,65536]{1,0:T(4,128)}, u32[]{:S(2)}) copy-start(s32[4,65536]{1,0:T(4,128)} %pixel_ref.1) | copy-start | bytes 3145732
  20.7 4.9 %collective-permute-start.3 = (f32[4,32,256]{2,1,0:T(8,128)S(1)}, f32[4,32,256]{2,1,0:T(8,128)S(1)}, u32[]{:S(2)}, u32[]{:S(2)}) collective-permute-start(f32[4,32,256]{2,1,0:T(8,128)S(1)} %get-tuple-element.21), channel_id=1, source_target_pairs={{0,1},{1,0},{2,3},{3,2},{4,5},{5,4},{6,7},{7,6},{8,9},{9,8},{10,11... | collective-permute-start | bytes 393224 | tf_op jit(solution)/shard_map/ppermute | solution.py:284
  20.7 11.4 %collective-permute-start.4 = (f32[4,32,256]{2,1,0:T(8,128)S(1)}, f32[4,32,256]{2,1,0:T(8,128)S(1)}, u32[]{:S(2)}, u32[]{:S(2)}) collective-permute-start(f32[4,32,256]{2,1,0:T(8,128)S(1)} %get-tuple-element.22), channel_id=1, source_target_pairs={{0,2},{1,3},{2,0},{3,1},{4,6},{5,7},{6,4},{7,5},{8,10},{9,11},{10,... | collective-permute-start | bytes 393224 | tf_op jit(solution)/shard_map/ppermute | solution.py:284
  22.6 22.6 %collective-permute-start.5 = (f32[4,32,256]{2,1,0:T(8,128)S(1)}, f32[4,32,256]{2,1,0:T(8,128)S(1)}, u32[]{:S(2)}, u32[]{:S(2)}) collective-permute-start(f32[4,32,256]{2,1,0:T(8,128)S(1)} %get-tuple-element.23), channel_id=1, source_target_pairs={{0,3},{1,2},{2,1},{3,0},{4,7},{5,6},{6,5},{7,4},{8,11},{9,10},{10,... | collective-permute-start | bytes 393224 | tf_op jit(solution)/shard_map/ppermute | solution.py:284
  22.8 22.4 %collective-permute-start.6 = (f32[4,32,256]{2,1,0:T(8,128)S(1)}, f32[4,32,256]{2,1,0:T(8,128)S(1)}, u32[]{:S(2)}, u32[]{:S(2)}) collective-permute-start(f32[4,32,256]{2,1,0:T(8,128)S(1)} %get-tuple-element.24), channel_id=1, source_target_pairs={{0,4},{1,5},{2,6},{3,7},{4,0},{5,1},{6,2},{7,3},{8,12},{9,13},{10,... | collective-permute-start | bytes 393224 | tf_op jit(solution)/shard_map/ppermute | solution.py:284
  25.5 19.7 %collective-permute-start.7 = (f32[4,32,256]{2,1,0:T(8,128)S(1)}, f32[4,32,256]{2,1,0:T(8,128)S(1)}, u32[]{:S(2)}, u32[]{:S(2)}) collective-permute-start(f32[4,32,256]{2,1,0:T(8,128)S(1)} %get-tuple-element.25), channel_id=1, source_target_pairs={{0,5},{1,4},{2,7},{3,6},{4,1},{5,0},{6,3},{7,2},{8,13},{9,12},{10,... | collective-permute-start | bytes 393224 | tf_op jit(solution)/shard_map/ppermute | solution.py:284
  25.6 19.7 %collective-permute-start.8 = (f32[4,32,256]{2,1,0:T(8,128)S(1)}, f32[4,32,256]{2,1,0:T(8,128)S(1)}, u32[]{:S(2)}, u32[]{:S(2)}) collective-permute-start(f32[4,32,256]{2,1,0:T(8,128)S(1)} %get-tuple-element.26), channel_id=1, source_target_pairs={{0,6},{1,7},{2,4},{3,5},{4,2},{5,3},{6,0},{7,1},{8,14},{9,15},{10,... | collective-permute-start | bytes 393224 | tf_op jit(solution)/shard_map/ppermute | solution.py:284
  32.1 13.2 %collective-permute-start.9 = (f32[4,32,256]{2,1,0:T(8,128)S(1)}, f32[4,32,256]{2,1,0:T(8,128)S(1)}, u32[]{:S(2)}, u32[]{:S(2)}) collective-permute-start(f32[4,32,256]{2,1,0:T(8,128)S(1)} %get-tuple-element.27), channel_id=1, source_target_pairs={{0,7},{1,6},{2,5},{3,4},{4,3},{5,2},{6,1},{7,0},{8,15},{9,14},{10,... | collective-permute-start | bytes 393224 | tf_op jit(solution)/shard_map/ppermute | solution.py:284
  32.1 0.7 copy-start.20
  32.8 12.5 %copy-start.4 = (bf16[256,512]{1,0:T(8,128)(2,1)S(1)}, bf16[256,512]{1,0:T(8,128)(2,1)}, u32[]{:S(2)}) copy-start(bf16[256,512]{1,0:T(8,128)(2,1)} %constant.31.clone.refs_14_) | copy-start | bytes 786436
  32.8 12.5 %copy-start.5 = (bf16[256,512]{1,0:T(8,128)(2,1)S(1)}, bf16[256,512]{1,0:T(8,128)(2,1)}, u32[]{:S(2)}) copy-start(bf16[256,512]{1,0:T(8,128)(2,1)} %constant.30.clone.refs_13_) | copy-start | bytes 786436
  32.8 12.5 %copy-start.6 = (f32[144,256]{1,0:T(8,128)S(1)}, f32[144,256]{1,0:T(8,128)}, u32[]{:S(2)}) copy-start(f32[144,256]{1,0:T(8,128)} %constant.36.clone.refs_19_) | copy-start | bytes 442372
  32.8 12.5 %copy-start.7 = (f32[128,256]{1,0:T(8,128)S(1)}, f32[128,256]{1,0:T(8,128)}, u32[]{:S(2)}) copy-start(f32[128,256]{1,0:T(8,128)} %constant.35.clone.refs_18_) | copy-start | bytes 393220
  32.8 12.5 %copy-start.8 = (f32[128,256]{1,0:T(8,128)S(1)}, f32[128,256]{1,0:T(8,128)}, u32[]{:S(2)}) copy-start(f32[128,256]{1,0:T(8,128)} %constant.34.clone.refs_17_) | copy-start | bytes 393220
  32.8 12.5 %copy-start.9 = (bf16[256,256]{1,0:T(8,128)(2,1)S(1)}, bf16[256,256]{1,0:T(8,128)(2,1)}, u32[]{:S(2)}) copy-start(bf16[256,256]{1,0:T(8,128)(2,1)} %constant.33.clone.refs_16_) | copy-start | bytes 393220
  32.8 12.5 %copy-start.10 = (bf16[256,256]{1,0:T(8,128)(2,1)S(1)}, bf16[256,256]{1,0:T(8,128)(2,1)}, u32[]{:S(2)}) copy-start(bf16[256,256]{1,0:T(8,128)(2,1)} %constant.32.clone.refs_15_) | copy-start | bytes 393220
  32.8 12.5 %copy-start.11 = (bf16[256,256]{1,0:T(8,128)(2,1)S(1)}, bf16[256,256]{1,0:T(8,128)(2,1)}, u32[]{:S(2)}) copy-start(bf16[256,256]{1,0:T(8,128)(2,1)} %constant.29.clone.refs_12_) | copy-start | bytes 393220
  32.8 12.5 %copy-start.12 = (bf16[256,256]{1,0:T(8,128)(2,1)S(1)}, bf16[256,256]{1,0:T(8,128)(2,1)}, u32[]{:S(2)}) copy-start(bf16[256,256]{1,0:T(8,128)(2,1)} %constant.28.clone.refs_11_) | copy-start | bytes 393220
  32.8 12.5 %copy-start.13 = (s32[16]{0:T(128)S(1)}, s32[16]{0:T(128)}, u32[]{:S(2)}) copy-start(s32[16]{0:T(128)} %order_ref.1) | copy-start | bytes 196
  32.9 12.5 %copy-start.14 = (f32[4]{0:T(128)S(1)}, f32[4]{0:T(128)}, u32[]{:S(2)}) copy-start(f32[4]{0:T(128)} %knee_ref.1) | copy-start | bytes 52
where the time goes:
time: 81.6 us; the launch traced here: 81.4 us
  Pallas kernels  37.9 us (46%)
  blocking collectives  15.6 us (19%)
  starting transfers between devices  14.9 us (18%)
  waiting for transfers between devices  6.98 us (9%)
  local copies, waits for them, and re-layouts  4.91 us (6%)
  between operations  0.9 us (1%)
    pallas_call x1, Pallas kernels, shards(): pl.pallas_call(functools.partial(filter_kernel, parts), out_shape=[jax.Sh...  19.6 us
    all_to_all x1, blocking collectives, shards(): lax.all_to_all(spread, ('det', 'tm'), split_axis=0, concat_axis=0, tiled=...  15.6 us
    ppermute x10, starting transfers between devices, swap(): return lax.ppermute(x, axis, [(i, i ^ step) for i in range(size)])  14.9 us
    pallas_call x1, Pallas kernels, shards(): pl.pallas_call(functools.partial(weight_kernel, tall), out_shape=[jax.Sha...  12.3 us
    ppermute x10, waiting for transfers between devices, swap(): return lax.ppermute(x, axis, [(i, i ^ step) for i in range(size)])  6.98 us
    unnamed x42, local copies, waits for them, and re-layouts  4.25 us
    pallas_call x1, Pallas kernels, shards(): pl.pallas_call(functools.partial(residual_kernel, runs, run_len, owners,...  3.7 us
    pallas_call x1, Pallas kernels, shards(): pl.pallas_call(functools.partial(fit_kernel, runs, run_len), out_shape=ja...  2.27 us
  transfers between devices with their start and end apart: 10, of which 4 were waited for; matrix products, arithmetic and copies ran while one was open for 0% of the time, Pallas kernels for 15%

commit v1 on v0

v1 whole, which is shorter than its diff:
```python
import functools
import math

import jax
import jax.numpy as jnp
import numpy as np
from jax import lax
from jax.experimental import pallas as pl
from jax.experimental.pallas import tpu as pltpu
from jax.sharding import PartitionSpec as P

PIX = 128
COLS = 256
LANES = 128
HALVES = COLS // LANES
LOW = 64
SAMPLE_RATE = 200.0
MIB = 1024 * 1024
NT = (((1,), (1,)), ((), ()))
f32 = jnp.float32
bf16 = jnp.bfloat16


def split2(x):
    high = x.astype(bf16)
    return high, (x - high.astype(f32)).astype(bf16)


def split3(x):
    high = x.astype(bf16)
    rest = x - high.astype(f32)
    mid = rest.astype(bf16)
    return high, mid, (rest - mid.astype(f32)).astype(bf16)


def host_split(x):
    high = x.astype(np.float32).astype(bf16)
    low = (x - high.astype(np.float64)).astype(np.float32).astype(bf16)
    return high, low


@functools.lru_cache(maxsize=None)
def tables(rows):
    total = rows * COLS
    half = rows // 2
    slots = np.arange(half)
    slots[0] = half
    ramp = np.arange(rows)
    angle = 2.0 * np.pi * (slots[:, None] * ramp[None, :] % rows) / rows
    first = np.concatenate([np.cos(angle), -np.sin(angle)], axis=0)
    first[half] = 1.0
    weight = np.full((half,), 2.0)
    weight[0] = 1.0
    last = np.concatenate([weight[:, None] * np.cos(angle), -2.0 * np.sin(angle)], axis=0)
    last[half] = 1.0
    last = last.T / total
    col = np.arange(COLS)
    phase = 2.0 * np.pi * (col[:, None] * col[None, :] % COLS) / COLS
    side = np.concatenate([np.cos(phase), np.sin(phase)], axis=1)
    turn = 2.0 * np.pi * (slots[:, None] * col[None, :] % total) / total
    bins = np.concatenate([slots, np.zeros((16,), np.int64)])[:, None] + rows * col[None, :]
    freq = np.minimum(bins, total - bins).astype(np.float32) * np.float32(SAMPLE_RATE / total)
    return (
        *host_split(first),
        *host_split(side),
        *host_split(last),
        np.cos(turn).astype(np.float32),
        np.sin(turn).astype(np.float32),
        (freq * freq).astype(np.float32),
    )


def dot3(left, right):
    (lh, ll), (rh, rl) = left, right
    return jnp.dot(
        jnp.concatenate([lh, ll, lh], axis=1),
        jnp.concatenate([rh, rh, rl], axis=0),
        preferred_element_type=f32,
    )


def pick(core, first, second):
    return jnp.where(core == 0, first, second)


def fit_kernel(runs, run_len, local_dets, paired, scalar_ref, data_ref, *refs):
    template_refs, out_ref = refs[:runs], refs[runs]
    parts, wide = [], []
    for run in range(runs):
        temp = template_refs[run][0]
        modes = temp.shape[0]
        high, mid, low = split3(data_ref[run * run_len : (run + 1) * run_len, :])
        both = lax.dot_general(
            temp, jnp.concatenate([temp, high, mid, low], axis=0), NT, preferred_element_type=f32
        )
        ends = [modes + i * run_len for i in range(4)]
        parts.append(both[:, :modes])
        parts.append(
            both[:, ends[0] : ends[1]] + both[:, ends[1] : ends[2]] + both[:, ends[2] : ends[3]]
        )
        wide.append(temp.astype(f32))
    part = jnp.concatenate(parts, axis=1)

    @pl.when(pl.program_id(0) == 0)
    def _():
        out_ref[...] = part

    @pl.when(pl.program_id(0) > 0)
    def _():
        out_ref[...] += part

    if paired:
        mine_ref, send_ref = refs[runs + 1 :]
        row_count = data_ref.shape[0]
        core = jnp.bitwise_and(scalar_ref[row_count], 1)
        groups = [
            data_ref[start : start + local_dets, :] for start in range(0, row_count, local_dets)
        ]
        even = jnp.concatenate(groups[0::2], axis=0)
        odd = jnp.concatenate(groups[1::2], axis=0)
        mine_ref[...] = pick(core, even, odd)
        send_ref[: row_count // 2, :] = pick(core, odd, even)
        send_ref[row_count // 2 :, :] = jnp.concatenate(wide, axis=0)


def eliminate(sums_ref, runs, run_len, modes):
    width = modes + run_len
    row_index = lax.broadcasted_iota(jnp.int32, (modes, width), 0)
    joined = [sums_ref[:, run * width : (run + 1) * width] for run in range(runs)]
    for column in range(modes):
        for run in range(runs):
            now = joined[run]
            pivot_row = now[column : column + 1, :] / now[column : column + 1, column : column + 1]
            rest = now - now[:, column : column + 1] * pivot_row
            joined[run] = jnp.where(row_index == column, pivot_row, rest)
    return [now[:, modes:] for now in joined]


def paired_kernel(runs, run_len, local_dets, chunks, scalar_ref, sums_ref, mine_ref, got_ref, *refs):
    template_refs, amps_ref = refs[:runs], refs[runs]
    out_refs, rows_ref = refs[runs + 1 : -1], refs[-1]
    modes = template_refs[0].shape[1]
    kept, time_local = mine_ref.shape
    pieces = time_local // COLS
    amps = eliminate(sums_ref, runs, run_len, modes)
    amps_ref[...] = jnp.concatenate(amps, axis=1)
    me = scalar_ref[2 * kept]
    core, chip = jnp.bitwise_and(me, 1), jnp.right_shift(me, 1)
    per_run = run_len // 2
    shard_rows = HALVES * pieces * kept
    for run in range(runs):
        turned = amps[run].T
        groups = [turned[start : start + local_dets] for start in range(0, run_len, local_dets)]
        turned = pick(
            core, jnp.concatenate(groups[0::2], axis=0), jnp.concatenate(groups[1::2], axis=0)
        )
        left = jnp.concatenate(split3(turned), axis=1)
        rows = slice(run * per_run, (run + 1) * per_run)
        other = got_ref[kept + run * modes : kept + (run + 1) * modes, :].astype(bf16)
        for side, (temp, data_ref) in enumerate([(template_refs[run][0], mine_ref), (other, got_ref)]):
            fitted = jnp.dot(left, jnp.concatenate([temp] * 3, axis=0), preferred_element_type=f32)
            for lane in range(time_local // LANES):
                cols = slice(lane * LANES, (lane + 1) * LANES)
                start = side * shard_rows + run * per_run
                start += (lane % HALVES * pieces + lane // HALVES) * kept
                rows_ref[start : start + per_run, :] = data_ref[rows, cols] - fitted[:, cols]
    chips = kept // local_dets
    per_chunk = local_dets // chunks
    for chunk in range(chunks):
        for step in range(chips):
            base = jnp.bitwise_xor(chip, step) * local_dets + chunk * per_chunk
            for det in range(per_chunk):
                for side in range(2):
                    place = pl.multiple_of(jnp.bitwise_xor(core, side) * pieces, pieces)
                    out_refs[chunk * chips + step][det, pl.ds(place, pieces), :] = take_rows(
                        rows_ref, side * shard_rows + base + det, pieces, kept
                    )


def residual_kernel(runs, run_len, owners, scalar_ref, sums_ref, data_ref, *refs):
    template_refs = refs[:runs]
    amps_ref, out_ref, rows_ref = refs[runs:]
    modes = template_refs[0].shape[1]
    row_count, time_local = data_ref.shape
    pieces = time_local // COLS
    amps = eliminate(sums_ref, runs, run_len, modes)
    amps_ref[...] = jnp.concatenate(amps, axis=1)
    for run in range(runs):
        temp = template_refs[run][0]
        left = jnp.concatenate(split3(amps[run].T), axis=1)
        fitted = jnp.dot(left, jnp.concatenate([temp] * 3, axis=0), preferred_element_type=f32)
        rows = slice(run * run_len, (run + 1) * run_len)
        for lane in range(time_local // LANES):
            cols = slice(lane * LANES, (lane + 1) * LANES)
            start = (lane % HALVES * pieces + lane // HALVES) * row_count + run * run_len
            rows_ref[start : start + run_len, :] = data_ref[rows, cols] - fitted[:, cols]
    local_dets = row_count // owners
    for owner in range(owners):
        for det in range(local_dets):
            out_ref[owner, det] = take_rows(rows_ref, owner * local_dets + det, pieces, row_count)


def take_rows(ref, start, count, stride):
    return jnp.concatenate(
        [
            ref[pl.ds(side * count * stride + start, count, stride=stride), :]
            for side in range(HALVES)
        ],
        axis=1,
    )


def binned(high_rows, low_rows, value_rows, weight_row, tall):
    high_ramp = lax.broadcasted_iota(jnp.int32, (tall, COLS), 0).astype(f32).astype(bf16)
    low_ramp = lax.broadcasted_iota(jnp.int32, (LOW, COLS), 0).astype(f32).astype(bf16)
    weight = jnp.broadcast_to(weight_row, (tall, COLS)).astype(bf16)
    zero, one = jnp.zeros((tall, COLS), bf16), jnp.ones((LOW, COLS), bf16)
    lefts, rights = [], []
    for row in range(high_rows.shape[0]):
        high = jnp.broadcast_to(high_rows[row : row + 1], (tall, COLS)).astype(bf16)
        low = jnp.broadcast_to(low_rows[row : row + 1], (LOW, COLS)).astype(bf16)
        value = jnp.broadcast_to(value_rows[row : row + 1], (tall, COLS)).astype(bf16)
        hot = high == high_ramp
        lefts.append(
            jnp.concatenate([jnp.where(hot, value, zero), jnp.where(hot, weight, zero)], axis=0)
        )
        rights.append(jnp.where(low == low_ramp, one, jnp.zeros_like(one)))
    return lax.dot_general(
        jnp.concatenate(lefts, axis=1),
        jnp.concatenate(rights, axis=1),
        NT,
        preferred_element_type=f32,
    )


def cell_kernel(after_ref, tile_ref, pixel_ref, high_ref, low_ref, hi_s, lo_s):
    local_dets, rows = high_ref.shape[0], high_ref.shape[1]
    cell = tile_ref[...] * PIX + pixel_ref[...]
    high = jnp.right_shift(cell, LOW.bit_length() - 1).astype(f32)
    low = jnp.bitwise_and(cell, LOW - 1).astype(f32)
    for lane in range(rows * HALVES):
        cols = slice(lane * LANES, (lane + 1) * LANES)
        start = (lane % HALVES * rows + lane // HALVES) * local_dets
        hi_s[start : start + local_dets, :] = high[:, cols]
        lo_s[start : start + local_dets, :] = low[:, cols]
    for det in range(local_dets):
        high_ref[det] = take_rows(hi_s, det, rows, local_dets)
        low_ref[det] = take_rows(lo_s, det, rows, local_dets)


def filter_kernel(parts, first_det, dets, final, place_ref, order_ref, knee_ref, white_ref, inverse_ref, *refs):
    part_refs = refs[:parts]
    (high_ref, low_ref, f_h, f_l, s_h, s_l, l_h, l_l, tc_ref, ts_ref, sq_ref) = refs[
        parts : parts + 11
    ]
    refs = refs[parts + 11 :]
    if first_det > 0:
        before_ref, sums_ref, refs = refs[0], refs[1], refs[2:]
    if final:
        out_ref, sky_ref, weight_ref, signal, stacked, totals = refs
    else:
        stacked, totals, signal = refs
    turn = pl.program_id(0)
    det = turn + first_det
    rows = signal.shape[0]
    half = rows // 2
    for part in range(parts):
        height = part_refs[part].shape[1]
        start = place_ref[part] * height if parts > 1 else 0
        if parts > 1:
            start = pl.multiple_of(start, height)
        signal[pl.ds(start, height), :] = part_refs[part][0]
    row_index = lax.broadcasted_iota(jnp.int32, (half, COLS), 0)
    turn_cos, turn_sin = tc_ref[...], ts_ref[...]
    side = (s_h[...], s_l[...])
    first = dot3((f_h[...], f_l[...]), split2(signal[...]))
    real_y, low_y = first[:half], first[half:]
    imag_y = jnp.where(row_index == 0, 0.0, low_y)
    zero_y = jnp.broadcast_to(low_y[0:1], (16, COLS))
    real_z = real_y * turn_cos + imag_y * turn_sin
    imag_z = imag_y * turn_cos - real_y * turn_sin
    forward = dot3(split2(jnp.concatenate([real_z, imag_z, zero_y], axis=0)), side)
    cos_f, sin_f = forward[:, :COLS], forward[:, COLS:]
    squared = sq_ref[...]
    knee = knee_ref[det]
    gain = squared / (white_ref[det] * (squared + knee * knee))
    gain_main, gain_zero = gain[:half], gain[half:]
    real_x = (cos_f[:half] + sin_f[half : 2 * half]) * gain_main
    imag_x = (cos_f[half : 2 * half] - sin_f[:half]) * gain_main
    zero_r = cos_f[2 * half :] * gain_zero
    zero_i = -sin_f[2 * half :] * gain_zero
    back = dot3(split2(jnp.concatenate([real_x, imag_x, zero_r, zero_i], axis=0)), side)
    cos_b, sin_b = back[:, :COLS], back[:, COLS:]
    real_u = cos_b[:half] - sin_b[half : 2 * half]
    imag_u = sin_b[:half] + cos_b[half : 2 * half]
    zero_o = cos_b[2 * half : 2 * half + 16] - sin_b[2 * half + 16 :]
    real_v = real_u * turn_cos - imag_u * turn_sin
    imag_v = real_u * turn_sin + imag_u * turn_cos
    imag_v = jnp.where(row_index == 0, zero_o[0:1], imag_v)
    result = dot3((l_h[...], l_l[...]), split2(jnp.concatenate([real_v, imag_v], axis=0)))
    signal[...] = result
    for half_index in range(HALVES):
        cols = slice(half_index * LANES, (half_index + 1) * LANES)
        stacked[pl.ds(half_index * rows * dets + det, rows, stride=dets), :] = result[:, cols]

    @pl.when(turn == 0)
    def _():
        totals[...] = sums_ref[...] if first_det > 0 else jnp.zeros_like(totals)

    tall = totals.shape[0] // 2
    weight_row = jnp.full((1, COLS), inverse_ref[det], f32)
    chunk = min(128, rows)

    @pl.loop(0, rows // chunk)
    def _(step):
        here = pl.ds(pl.multiple_of(step * chunk, chunk), chunk)
        totals[...] += binned(
            high_ref[0, here], low_ref[0, here], signal[here, :], weight_row, tall
        )

    if final:

        @pl.when(turn == pl.num_programs(0) - 1)
        def _():
            det_index = lax.broadcasted_iota(jnp.int32, (dets, LANES), 0)
            for lane in range(rows * HALVES):
                start = (lane % HALVES * rows + lane // HALVES) * dets
                here = stacked[start : start + dets, :]
                if first_det > 0:
                    here = jnp.where(
                        det_index < first_det, before_ref[start : start + dets, :], here
                    )
                out_ref[:, lane * LANES : (lane + 1) * LANES] = here.astype(bf16)
            per_tile = PIX // LOW
            for tile in range(sky_ref.shape[0]):
                source = order_ref[tile] * per_tile
                for piece in range(per_tile):
                    cols = slice(piece * LOW, (piece + 1) * LOW)
                    sky_ref[tile : tile + 1, cols] = totals[pl.ds(source + piece, 1), :]
                    weight_ref[tile : tile + 1, cols] = totals[pl.ds(tall + source + piece, 1), :]


def swap(x, step, axis):
    size = lax.axis_size(axis)
    return lax.ppermute(x, axis, [(i, i ^ step) for i in range(size)])


def vmem(limit):
    return pltpu.CompilerParams(vmem_limit_bytes=limit * MIB)


def shards(
    detector_data, templates, wafer_of, knee_freq, white_level, tile_id, pixel_id, tile_order
):
    row_count, time_local = detector_data.shape
    wafer_count, modes, _ = templates.shape
    owners, groups = lax.axis_size("tm"), lax.axis_size("det")
    run_len = min(row_count, row_count * groups // wafer_count)
    runs = row_count // run_len
    width = runs * (modes + run_len)
    local_dets = row_count // owners
    full_length = time_local * owners
    rows = full_length // COLS
    pieces = time_local // COLS
    me = lax.axis_index("tm").astype(jnp.int32)
    scalars = jnp.concatenate([wafer_of, me[None]])
    power = owners & (owners - 1) == 0
    paired = power and 4 <= owners <= 8 and run_len % (2 * local_dets) == 0
    step_len = min(2048, time_local)

    def template_spec(run, blocked):
        length = step_len if blocked else time_local
        return pl.BlockSpec(
            (1, modes, length),
            lambda i, w, run=run: (w[run * run_len], 0, i if blocked else 0),
        )

    def fixed(*shape):
        return pl.BlockSpec(shape, lambda i, *_: (0,) * len(shape))

    def by_step(height):
        return pl.BlockSpec((height, step_len), lambda i, w: (0, i))

    kept = row_count // 2
    sent = kept + runs * modes
    sums, *packed = pl.pallas_call(
        functools.partial(fit_kernel, runs, run_len, local_dets, paired),
        out_shape=[jax.ShapeDtypeStruct((modes, width), f32)]
        + [jax.ShapeDtypeStruct((n, time_local), f32) for n in (kept, sent) if paired],
        grid_spec=pltpu.PrefetchScalarGridSpec(
            num_scalar_prefetch=1,
            grid=(time_local // step_len,),
            in_specs=[by_step(row_count)] + [template_spec(run, True) for run in range(runs)],
            out_specs=[fixed(modes, width)] + [by_step(n) for n in (kept, sent) if paired],
        ),
        compiler_params=vmem(60),
        name="fit_sums",
    )(scalars, detector_data, *[templates] * runs)
    if paired:
        got = swap(packed[1], 1, "tm")
    if power:
        step = owners // 2
        while step > 0:
            sums = sums + swap(sums, step, "tm")
            step //= 2
    else:
        sums = lax.psum(sums, "tm")

    chunks = 2 if paired and local_dets % 2 == 0 else 1
    per_chunk = local_dets // chunks
    if paired:
        block_shape = (per_chunk, 2 * pieces, COLS)
        chips = owners // 2
        blocks_out = [block_shape] * (chunks * chips)
        kernel = functools.partial(paired_kernel, runs, run_len, local_dets, chunks)
        operands = [packed[0], got]
        operand_specs = [fixed(kept, time_local), fixed(sent, time_local)]
        scratch = pltpu.VMEM((2 * HALVES * pieces * kept, LANES), f32)
    else:
        blocks_out = [(owners, local_dets, pieces, COLS)]
        kernel = functools.partial(residual_kernel, runs, run_len, owners)
        operands = [detector_data]
        operand_specs = [fixed(row_count, time_local)]
        scratch = pltpu.VMEM((HALVES * pieces * row_count, LANES), f32)
    fit_amps, *blocks = pl.pallas_call(
        kernel,
        out_shape=[jax.ShapeDtypeStruct(shape, f32) for shape in [(modes, row_count), *blocks_out]],
        grid_spec=pltpu.PrefetchScalarGridSpec(
            num_scalar_prefetch=1,
            grid=(1,),
            in_specs=[fixed(modes, width), *operand_specs]
            + [template_spec(run, False) for run in range(runs)],
            out_specs=[fixed(modes, row_count)] + [fixed(*shape) for shape in blocks_out],
            scratch_shapes=[scratch],
        ),
        compiler_params=vmem(32),
        name="residual",
    )(scalars, sums, *operands, *[templates] * runs)

    if paired:
        received = []
        for chunk in range(chunks):
            here = blocks[chunk * chips : (chunk + 1) * chips]
            for step in reversed(range(1, chips)):
                here[step] = swap(here[step], 2 * step, "tm")
            received.append(here)
        place = jnp.bitwise_xor(me // 2, jnp.arange(chips, dtype=jnp.int32))
    else:
        moved = lax.all_to_all(blocks[0], "tm", split_axis=0, concat_axis=0, tiled=True)
        received = [[jnp.swapaxes(moved, 0, 1).reshape(local_dets, rows, COLS)]]
        place = jnp.zeros((1,), jnp.int32)

    tile_count = tile_order.shape[0]
    tall = tile_count * PIX // LOW
    inverse_white = (1.0 / white_level).astype(bf16).astype(f32)
    whole = pl.BlockSpec(memory_space=pltpu.VMEM)
    high, low = pl.pallas_call(
        cell_kernel,
        out_shape=[jax.ShapeDtypeStruct((local_dets, rows, COLS), f32)] * 2,
        in_specs=[pl.BlockSpec(memory_space=pl.ANY), whole, whole],
        out_specs=[whole] * 2,
        scratch_shapes=[pltpu.VMEM((HALVES * rows * local_dets, LANES), f32)] * 2,
        compiler_params=vmem(32),
        cost_estimate=pl.CostEstimate(
            flops=0, bytes_accessed=32 * local_dets * full_length, transcendentals=0
        ),
        name="cells",
    )(fit_amps, tile_id, pixel_id)

    consts = [jnp.asarray(t) for t in tables(rows)]
    stacked_shape = (HALVES * rows * local_dets, LANES)
    carried = []
    for chunk in range(chunks):
        final = chunk == chunks - 1
        first_det = chunk * per_chunk
        parts = len(received[chunk])
        if final:
            outs = [((local_dets, full_length), bf16)] + [((tile_count, PIX), f32)] * 2
            scratch = [pltpu.VMEM(s, f32) for s in ((rows, COLS), stacked_shape, (2 * tall, LOW))]
        else:
            outs = [(stacked_shape, f32), ((2 * tall, LOW), f32)]
            scratch = [pltpu.VMEM((rows, COLS), f32)]
        carried = pl.pallas_call(
            functools.partial(filter_kernel, parts, first_det, local_dets, final),
            out_shape=[jax.ShapeDtypeStruct(*o) for o in outs],
            grid_spec=pltpu.PrefetchScalarGridSpec(
                num_scalar_prefetch=5,
                grid=(per_chunk,),
                in_specs=[
                    pl.BlockSpec((1, *r.shape[1:]), lambda i, *_: (i, 0, 0))
                    for r in received[chunk]
                ]
                + [
                    pl.BlockSpec((1, rows, COLS), lambda i, *_, f=first_det: (i + f, 0, 0)),
                ]
                * 2
                + [fixed(*c.shape) for c in [*consts, *carried]],
                out_specs=[fixed(*shape) for shape, _ in outs],
                scratch_shapes=scratch,
            ),
            compiler_params=vmem(48),
            cost_estimate=pl.CostEstimate(
                flops=80000 * per_chunk * full_length,
                bytes_accessed=16 * per_chunk * full_length,
                transcendentals=0,
            ),
            name="filter_and_bin",
        )(
            place,
            tile_order,
            knee_freq,
            white_level,
            inverse_white,
            *received[chunk],
            high,
            low,
            *consts,
            *carried,
        )
    weighted_data, sky_part, weight_part = carried

    owned = tile_count * PIX // owners
    both = jnp.concatenate(
        [sky_part.reshape(owners, owned), weight_part.reshape(owners, owned)], axis=1
    )
    spread = jnp.broadcast_to(both[None], (groups, *both.shape)).reshape(groups * owners, 2 * owned)
    spread = lax.all_to_all(spread, ("det", "tm"), split_axis=0, concat_axis=0, tiled=True)
    scale = float(tile_count * PIX) / float(local_dets * groups * owners * full_length)
    summed = jnp.sum(spread, axis=0) * scale
    return (fit_amps, weighted_data, summed[:owned], summed[owned:])


def solution(mesh):
    in_specs = (
        P("det", "tm"),
        P(None, None, "tm"),
        P("det"),
        P(("det", "tm")),
        P(("det", "tm")),
        P(("det", "tm"), None),
        P(("det", "tm"), None),
        P(),
    )
    out_specs = (P(None, "det"), P(("det", "tm"), None), P("tm"), P("tm"))
    return jax.shard_map(shards, mesh=mesh, in_specs=in_specs, out_specs=out_specs, check_vma=False)
```

time: 81.6 us -> 87 us (1.066)
  Pallas kernels: 37.9 us -> 29.5 us
  local copies, waits for them, and re-layouts: 4.91 us -> 11.9 us
  blocking collectives: 15.6 us -> 19.5 us
  other arithmetic: 0.17 us -> 2.03 us
  starting transfers between devices: 14.9 us -> 15.9 us
    pallas_call x4 -> x5, Pallas kernels: 37.9 us -> 29.5 us  [the longest x2 19.5 us: shards(): pl.pallas_call(functools.partial(filter_kernel, parts, first_det, local_d...]
    unnamed x42 -> x46, local copies, waits for them, and re-layouts: 4.25 us -> 11.2 us
    all_to_all x1, blocking collectives: 15.6 us -> 19.5 us  [shards(): lax.all_to_all(spread, ('det', 'tm'), split_axis=0, concat_axis=0, tiled=...]
    concatenate x1, other arithmetic: 0.07 us -> 1.24 us  [shards(): scalars = jnp.concatenate([wafer_of, me[None]])]
    ppermute x10, starting transfers between devices: 14.9 us -> 15.9 us  [swap(): return lax.ppermute(x, axis, [(i, i ^ step) for i in range(size)])]
  transfers between devices with their start and end apart: 10 -> 10, of which waited for: 4 -> 4; matrix products, arithmetic and copies ran while one was open for 0% -> 1% of each run, Pallas kernels for 15% -> 12%
where the time goes in v1:
time: 87 us; the launch traced here: 86.4 us
  Pallas kernels  29.5 us (34%)
  blocking collectives  19.5 us (22%)
  starting transfers between devices  15.9 us (18%)
  local copies, waits for them, and re-layouts  11.9 us (14%)
  waiting for transfers between devices  6.82 us (8%)
  other arithmetic  2.03 us (2%)
    pallas_call x2, Pallas kernels, shards(): pl.pallas_call(functools.partial(filter_kernel, parts, first_det, local_d...  19.5 us
    all_to_all x1, blocking collectives, shards(): lax.all_to_all(spread, ('det', 'tm'), split_axis=0, concat_axis=0, tiled=...  19.5 us
    ppermute x10, starting transfers between devices, swap(): return lax.ppermute(x, axis, [(i, i ^ step) for i in range(size)])  15.9 us
    unnamed x46, local copies, waits for them, and re-layouts  11.2 us
    ppermute x10, waiting for transfers between devices, swap(): return lax.ppermute(x, axis, [(i, i ^ step) for i in range(size)])  6.82 us
    pallas_call x1, Pallas kernels, shards(): pl.pallas_call(functools.partial(fit_kernel, runs, run_len, local_dets, p...  5.3 us
    pallas_call x1, Pallas kernels, shards(): pl.pallas_call(kernel, out_shape=[jax.ShapeDtypeStruct(shape, f32) for sh...  3.86 us
  transfers between devices with their start and end apart: 10, of which 4 were waited for; matrix products, arithmetic and copies ran while one was open for 1% of the time, Pallas kernels for 12%

profile of v1, /device:TPU:0, one launch (start us, length us, event | category | flops | bytes accessed | tf_op | source)
XLA Modules:
  0.0 86.4 jit_solution(17403359254316119227)
XLA Ops:
  0.6 1.2 %pad_add_fusion.scalar_ref = s32[33]{0:T(128)} fusion(s32[1]{0:T(128)} %bitcast, s32[32]{0:T(128)} %param.19), kind=kLoop, calls=%fused_computation.2 | loop fusion | flops 33 | bytes 264 | tf_op jit(solution)/shard_map/concatenate | solution.py:366
  1.9 5.3 %fit_sums.1 = (f32[16,64]{1,0:T(8,128)}, f32[16,8192]{1,0:T(8,128)}, f32[48,8192]{1,0:T(8,128)}) custom-call(s32[33]{0:T(128)} %pad_add_fusion.scalar_ref, f32[32,8192]{1,0:T(8,128)} %data_ref.1, bf16[8,16,8192]{2,1,0:T(8,128)(2,1)} %refs_1_.3, bf16[8,16,8192]{2,1,0:T(8,128)(2,1)} %refs_1_.3), custom_call_target="tpu_custom_call" | custom-call | tf_op jit(solution)/shard_map/fit_sums/pallas_call | solution.py:386
  7.6 3.6 %collective-permute-start = (f32[16,64]{1,0:T(8,128)}, f32[16,64]{1,0:T(8,128)S(1)}, u32[]{:S(2)}, u32[]{:S(2)}) collective-permute-start(f32[16,64]{1,0:T(8,128)} %get-tuple-element.23), channel_id=1, source_target_pairs={{0,4},{1,5},{2,6},{3,7},{4,0},{5,1},{6,2},{7,3},{8,12},{9,13},{10,... | collective-permute-start | bytes 12296 | tf_op jit(solution)/shard_map/ppermute | solution.py:345
  11.3 1.8 %collective-permute-done = f32[16,64]{1,0:T(8,128)S(1)} collective-permute-done((f32[16,64]{1,0:T(8,128)}, f32[16,64]{1,0:T(8,128)S(1)}, u32[]{:S(2)}, u32[]{:S(2)}) %collective-permute-start) | collective-permute-done | bytes 4128 | tf_op jit(solution)/shard_map/ppermute | solution.py:345
  13.1 0.7 add.10
  13.8 1.9 %collective-permute-start.1 = (f32[16,64]{1,0:T(8,128)S(1)}, f32[16,64]{1,0:T(8,128)S(1)}, u32[]{:S(2)}, u32[]{:S(2)}) collective-permute-start(f32[16,64]{1,0:T(8,128)S(1)} %add.10), channel_id=1, source_target_pairs={{0,2},{1,3},{2,0},{3,1},{4,6},{5,7},{6,4},{7,5},{8,10},{9,11},{10,... | collective-permute-start | bytes 12296 | tf_op jit(solution)/shard_map/ppermute | solution.py:345
  15.7 1.7 %collective-permute-done.1 = f32[16,64]{1,0:T(8,128)S(1)} collective-permute-done((f32[16,64]{1,0:T(8,128)S(1)}, f32[16,64]{1,0:T(8,128)S(1)}, u32[]{:S(2)}, u32[]{:S(2)}) %collective-permute-start.1) | collective-permute-done | bytes 4128 | tf_op jit(solution)/shard_map/ppermute | solution.py:345
  17.5 1.2 %collective-permute-done.2 = f32[16,64]{1,0:T(8,128)S(1)} collective-permute-done((f32[16,64]{1,0:T(8,128)S(1)}, f32[16,64]{1,0:T(8,128)S(1)}, u32[]{:S(2)}, u32[]{:S(2)}) %collective-permute-start.2) | collective-permute-done | bytes 4128 | tf_op jit(solution)/shard_map/ppermute | solution.py:345
  18.7 1.0 %copy-done.3 = f32[16,8192]{1,0:T(8,128)S(1)} copy-done((f32[16,8192]{1,0:T(8,128)S(1)}, f32[16,8192]{1,0:T(8,128)}, u32[]{:S(2)}) %copy-start.3) | copy-done | bytes 524312
  19.7 3.9 %residual.1 = (f32[16,32]{1,0:T(8,128)}, f32[2,64,256]{2,1,0:T(8,128)S(1)}, f32[2,64,256]{2,1,0:T(8,128)}, f32[2,64,256]{2,1,0:T(8,128)S(1)}, f32[2,64,256]{2,1,...) custom-call(s32[33]{0:T(128)S(1)} %copy-done.5, ...), custom_call_target="tpu_custom_call" | custom-call | tf_op jit(solution)/shard_map/residual/pallas_call | solution.py:425
  23.6 1.9 %collective-permute-start.7 = (f32[2,64,256]{2,1,0:T(8,128)}, f32[2,64,256]{2,1,0:T(8,128)S(1)}, u32[]{:S(2)}, u32[]{:S(2)}) collective-permute-start(f32[2,64,256]{2,1,0:T(8,128)} %get-tuple-element.34), channel_id=1, source_target_pairs={{0,2},{1,3},{2,0},{3,1},{4,6},{5,7},{6,4},{7,5},{8,10},{9,11},{10,... | collective-permute-start | bytes 393224 | tf_op jit(solution)/shard_map/ppermute | solution.py:345
  25.4 2.6 %collective-permute-start.8 = (f32[2,64,256]{2,1,0:T(8,128)S(1)}, f32[2,64,256]{2,1,0:T(8,128)S(1)}, u32[]{:S(2)}, u32[]{:S(2)}) collective-permute-start(f32[2,64,256]{2,1,0:T(8,128)S(1)} %get-tuple-element.35), channel_id=1, source_target_pairs={{0,4},{1,5},{2,6},{3,7},{4,0},{5,1},{6,2},{7,3},{8,12},{9,13},{10,... | collective-permute-start | bytes 393224 | tf_op jit(solution)/shard_map/ppermute | solution.py:345
  28.1 0.9 %collective-permute-start.4 = (f32[2,64,256]{2,1,0:T(8,128)S(1)}, f32[2,64,256]{2,1,0:T(8,128)S(1)}, u32[]{:S(2)}, u32[]{:S(2)}) collective-permute-start(f32[2,64,256]{2,1,0:T(8,128)S(1)} %get-tuple-element.28), channel_id=1, source_target_pairs={{0,2},{1,3},{2,0},{3,1},{4,6},{5,7},{6,4},{7,5},{8,10},{9,11},{10,... | collective-permute-start | bytes 393224 | tf_op jit(solution)/shard_map/ppermute | solution.py:345
  29.0 3.5 %collective-permute-start.5 = (f32[2,64,256]{2,1,0:T(8,128)S(1)}, f32[2,64,256]{2,1,0:T(8,128)S(1)}, u32[]{:S(2)}, u32[]{:S(2)}) collective-permute-start(f32[2,64,256]{2,1,0:T(8,128)S(1)} %get-tuple-element.29), channel_id=1, source_target_pairs={{0,4},{1,5},{2,6},{3,7},{4,0},{5,1},{6,2},{7,3},{8,12},{9,13},{10,... | collective-permute-start | bytes 393224 | tf_op jit(solution)/shard_map/ppermute | solution.py:345
  32.5 1.2 %copy-done.2 = s32[4,65536]{1,0:T(4,128)S(1)} copy-done((s32[4,65536]{1,0:T(4,128)S(1)}, s32[4,65536]{1,0:T(4,128)}, u32[]{:S(2)}) %copy-start.2) | copy-done | bytes 1048600
  33.8 0.7 copy-done.4
  34.5 0.8 cells.1
  35.3 1.0 %collective-permute-start.6 = (f32[2,64,256]{2,1,0:T(8,128)S(1)}, f32[2,64,256]{2,1,0:T(8,128)S(1)}, u32[]{:S(2)}, u32[]{:S(2)}) collective-permute-start(f32[2,64,256]{2,1,0:T(8,128)S(1)} %get-tuple-element.30), channel_id=1, source_target_pairs={{0,6},{1,7},{2,4},{3,5},{4,2},{5,3},{6,0},{7,1},{8,14},{9,15},{10,... | collective-permute-start | bytes 393224 | tf_op jit(solution)/shard_map/ppermute | solution.py:345
  36.3 2.0 %collective-permute-done.8.refs_2_ = f32[2,64,256]{2,1,0:T(8,128)S(1)} collective-permute-done((f32[2,64,256]{2,1,0:T(8,128)S(1)}, f32[2,64,256]{2,1,0:T(8,128)S(1)}, u32[]{:S(2)}, u32[]{:S(2)}) %collective-permute-start.8) | collective-permute-done | bytes 131104 | tf_op jit(solution)/shard_map/ppermute | solution.py:345
  38.3 0.9 %copy-done.9 = bf16[256,512]{1,0:T(8,128)(2,1)S(1)} copy-done((bf16[256,512]{1,0:T(8,128)(2,1)S(1)}, bf16[256,512]{1,0:T(8,128)(2,1)}, u32[]{:S(2)}) %copy-start.9) | copy-done | bytes 262168
  39.3 0.9 %copy-done.11 = bf16[256,512]{1,0:T(8,128)(2,1)S(1)} copy-done((bf16[256,512]{1,0:T(8,128)(2,1)S(1)}, bf16[256,512]{1,0:T(8,128)(2,1)}, u32[]{:S(2)}) %copy-start.11) | copy-done | bytes 262168
  40.2 0.9 %copy-done.13 = f32[144,256]{1,0:T(8,128)S(1)} copy-done((f32[144,256]{1,0:T(8,128)S(1)}, f32[144,256]{1,0:T(8,128)}, u32[]{:S(2)}) %copy-start.13) | copy-done | bytes 147480
  41.1 0.9 %copy-done.15 = f32[128,256]{1,0:T(8,128)S(1)} copy-done((f32[128,256]{1,0:T(8,128)S(1)}, f32[128,256]{1,0:T(8,128)}, u32[]{:S(2)}) %copy-start.15) | copy-done | bytes 131096
  42.1 0.9 %copy-done.17 = f32[128,256]{1,0:T(8,128)S(1)} copy-done((f32[128,256]{1,0:T(8,128)S(1)}, f32[128,256]{1,0:T(8,128)}, u32[]{:S(2)}) %copy-start.17) | copy-done | bytes 131096
  43.0 0.9 %copy-done.19 = bf16[256,256]{1,0:T(8,128)(2,1)S(1)} copy-done((bf16[256,256]{1,0:T(8,128)(2,1)S(1)}, bf16[256,256]{1,0:T(8,128)(2,1)}, u32[]{:S(2)}) %copy-start.19) | copy-done | bytes 131096
  43.9 0.9 %copy-done.20 = bf16[256,256]{1,0:T(8,128)(2,1)S(1)} copy-done((bf16[256,256]{1,0:T(8,128)(2,1)S(1)}, bf16[256,256]{1,0:T(8,128)(2,1)}, u32[]{:S(2)}) %copy-start.20) | copy-done | bytes 131096
  44.8 0.9 %copy-done.21 = bf16[256,256]{1,0:T(8,128)(2,1)S(1)} copy-done((bf16[256,256]{1,0:T(8,128)(2,1)S(1)}, bf16[256,256]{1,0:T(8,128)(2,1)}, u32[]{:S(2)}) %copy-start.21) | copy-done | bytes 131096
  45.7 0.9 %copy-done.22 = bf16[256,256]{1,0:T(8,128)(2,1)S(1)} copy-done((bf16[256,256]{1,0:T(8,128)(2,1)S(1)}, bf16[256,256]{1,0:T(8,128)(2,1)}, u32[]{:S(2)}) %copy-start.22) | copy-done | bytes 131096
  46.6 9.2 %filter_and_bin.2 = (f32[2048,128]{1,0:T(8,128)S(1)}, f32[64,64]{1,0:T(8,128)S(1)}) custom-call(s32[4]{0:T(128)S(1)} %iota_xor_fusion.place_ref, s32[16]{0:T(128)S(1)} %copy-done.6, f32[4]{0:T(128)S(1)} %copy-done.7, f32[4]{0:T(128)S(1)} %copy-done.8, f32[4]{0:T(128)S(1)} %convert_convert_fusion.inverse_ref, f32[2,64,256]{2,1,0:T(8,128)S(1)} %get-tuple-element.33.refs_0_, ...), custom_call_target="tpu_custom_call" | custom-call | flops 10485760000 | bytes 2097152 | tf_op jit(solution)/shard_map/filter_and_bin/pallas_call | solution.py:483
  55.9 10.3 %filter_and_bin.3 = (bf16[4,65536]{1,0:T(4,128)(2,1)}, f32[16,128]{1,0:T(8,128)S(1)}, f32[16,128]{1,0:T(8,128)S(1)}) custom-call(s32[4]{0:T(128)S(1)} %iota_xor_fusion.place_ref, s32[16]{0:T(128)S(1)} %copy-done.6, f32[4]{0:T(128)S(1)} %copy-done.7, f32[4]{0:T(128)S(1)} %copy-done.8, f32[4]{0:T(128)S(1)} %convert_convert_fusion.inverse_ref, ...), custom_call_target="tpu_custom_call" | custom-call | flops 10485760000 | bytes 2097152 | tf_op jit(solution)/shard_map/filter_and_bin/pallas_call | solution.py:483
  66.3 19.5 %all_to_all.9 = f32[32,1,512]{2,1,0:T(1,128)S(1)} all-to-all(f32[32,1,512]{2,1,0:T(1,128)S(1)} %all_to_all.6), channel_id=1, replica_groups=mesh['det'=4,'tm'=8] {'det','tm'}, dimensions={0} | all-to-all | bytes 131072 | tf_op jit(solution)/shard_map/all_to_all | solution.py:527
  85.8 0.6 fusion
  (54 shorter events, 0.7 us)
Async XLA Ops:
  1.9 16.8 %copy-start = (bf16[8,16,8192]{2,1,0:T(8,128)(2,1)S(1)}, bf16[8,16,8192]{2,1,0:T(8,128)(2,1)}, u32[]{:S(2)}) copy-start(bf16[8,16,8192]{2,1,0:T(8,128)(2,1)} %refs_1_.3) | copy-start | bytes 6291460
  1.9 16.8 %copy-start.5 = (s32[33]{0:T(128)S(1)}, s32[33]{0:T(128)}, u32[]{:S(2)}) copy-start(s32[33]{0:T(128)} %pad_add_fusion.scalar_ref) | copy-start | bytes 400
  7.2 11.4 %collective-permute-start.3 = (f32[48,8192]{1,0:T(8,128)}, f32[48,8192]{1,0:T(8,128)S(1)}, u32[]{:S(2)}, u32[]{:S(2)}) collective-permute-start(f32[48,8192]{1,0:T(8,128)} %get-tuple-element.25), channel_id=1, source_target_pairs={{0,1},{1,0},{2,3},{3,2},{4,5},{5,4},{6,7},{7,6},{8,9},{9,8},{10,11... | collective-permute-start | bytes 4718600 | tf_op jit(solution)/shard_map/ppermute | solution.py:345
  7.6 5.5 %collective-permute-start = (f32[16,64]{1,0:T(8,128)}, f32[16,64]{1,0:T(8,128)S(1)}, u32[]{:S(2)}, u32[]{:S(2)}) collective-permute-start(f32[16,64]{1,0:T(8,128)} %get-tuple-element.23), channel_id=1, source_target_pairs={{0,4},{1,5},{2,6},{3,7},{4,0},{5,1},{6,2},{7,3},{8,12},{9,13},{10,... | collective-permute-start | bytes 12296 | tf_op jit(solution)/shard_map/ppermute | solution.py:345
  13.8 3.7 %collective-permute-start.1 = (f32[16,64]{1,0:T(8,128)S(1)}, f32[16,64]{1,0:T(8,128)S(1)}, u32[]{:S(2)}, u32[]{:S(2)}) collective-permute-start(f32[16,64]{1,0:T(8,128)S(1)} %add.10), channel_id=1, source_target_pairs={{0,2},{1,3},{2,0},{3,1},{4,6},{5,7},{6,4},{7,5},{8,10},{9,11},{10,... | collective-permute-start | bytes 12296 | tf_op jit(solution)/shard_map/ppermute | solution.py:345
  17.5 1.2 %collective-permute-start.2 = (f32[16,64]{1,0:T(8,128)S(1)}, f32[16,64]{1,0:T(8,128)S(1)}, u32[]{:S(2)}, u32[]{:S(2)}) collective-permute-start(f32[16,64]{1,0:T(8,128)S(1)} %add.11), channel_id=1, source_target_pairs={{0,1},{1,0},{2,3},{3,2},{4,5},{5,4},{6,7},{7,6},{8,9},{9,8},{10,11... | collective-permute-start | bytes 12296 | tf_op jit(solution)/shard_map/ppermute | solution.py:345
  18.6 1.0 %copy-start.3 = (f32[16,8192]{1,0:T(8,128)S(1)}, f32[16,8192]{1,0:T(8,128)}, u32[]{:S(2)}) copy-start(f32[16,8192]{1,0:T(8,128)} %get-tuple-element.24.mine_ref) | copy-start | bytes 1572868
  19.7 8.4 %copy-start.8 = (f32[4]{0:T(128)S(1)}, f32[4]{0:T(128)}, u32[]{:S(2)}) copy-start(f32[4]{0:T(128)} %white_ref.3) | copy-start | bytes 52
  19.7 12.8 %copy-start.1 = (s32[4,65536]{1,0:T(4,128)S(1)}, s32[4,65536]{1,0:T(4,128)}, u32[]{:S(2)}) copy-start(s32[4,65536]{1,0:T(4,128)} %tile_ref.1) | copy-start | bytes 3145732
  23.6 14.8 %copy-start.6 = (s32[16]{0:T(128)S(1)}, s32[16]{0:T(128)}, u32[]{:S(2)}) copy-start(s32[16]{0:T(128)} %order_ref.3) | copy-start | bytes 196
  23.6 14.8 %copy-start.7 = (f32[4]{0:T(128)S(1)}, f32[4]{0:T(128)}, u32[]{:S(2)}) copy-start(f32[4]{0:T(128)} %knee_ref.3) | copy-start | bytes 52
  23.6 11.7 %collective-permute-start.7 = (f32[2,64,256]{2,1,0:T(8,128)}, f32[2,64,256]{2,1,0:T(8,128)S(1)}, u32[]{:S(2)}, u32[]{:S(2)}) collective-permute-start(f32[2,64,256]{2,1,0:T(8,128)} %get-tuple-element.34), channel_id=1, source_target_pairs={{0,2},{1,3},{2,0},{3,1},{4,6},{5,7},{6,4},{7,5},{8,10},{9,11},{10,... | collective-permute-start | bytes 393224 | tf_op jit(solution)/shard_map/ppermute | solution.py:345
  25.4 12.9 %collective-permute-start.8 = (f32[2,64,256]{2,1,0:T(8,128)S(1)}, f32[2,64,256]{2,1,0:T(8,128)S(1)}, u32[]{:S(2)}, u32[]{:S(2)}) collective-permute-start(f32[2,64,256]{2,1,0:T(8,128)S(1)} %get-tuple-element.35), channel_id=1, source_target_pairs={{0,4},{1,5},{2,6},{3,7},{4,0},{5,1},{6,2},{7,3},{8,12},{9,13},{10,... | collective-permute-start | bytes 393224 | tf_op jit(solution)/shard_map/ppermute | solution.py:345
  28.1 10.3 %collective-permute-start.9 = (f32[2,64,256]{2,1,0:T(8,128)S(1)}, f32[2,64,256]{2,1,0:T(8,128)S(1)}, u32[]{:S(2)}, u32[]{:S(2)}) collective-permute-start(f32[2,64,256]{2,1,0:T(8,128)S(1)} %get-tuple-element.36), channel_id=1, source_target_pairs={{0,6},{1,7},{2,4},{3,5},{4,2},{5,3},{6,0},{7,1},{8,14},{9,15},{10,... | collective-permute-start | bytes 393224 | tf_op jit(solution)/shard_map/ppermute | solution.py:345
  28.1 27.7 %collective-permute-start.4 = (f32[2,64,256]{2,1,0:T(8,128)S(1)}, f32[2,64,256]{2,1,0:T(8,128)S(1)}, u32[]{:S(2)}, u32[]{:S(2)}) collective-permute-start(f32[2,64,256]{2,1,0:T(8,128)S(1)} %get-tuple-element.28), channel_id=1, source_target_pairs={{0,2},{1,3},{2,0},{3,1},{4,6},{5,7},{6,4},{7,5},{8,10},{9,11},{10,... | collective-permute-start | bytes 393224 | tf_op jit(solution)/shard_map/ppermute | solution.py:345
  29.0 26.8 %collective-permute-start.5 = (f32[2,64,256]{2,1,0:T(8,128)S(1)}, f32[2,64,256]{2,1,0:T(8,128)S(1)}, u32[]{:S(2)}, u32[]{:S(2)}) collective-permute-start(f32[2,64,256]{2,1,0:T(8,128)S(1)} %get-tuple-element.29), channel_id=1, source_target_pairs={{0,4},{1,5},{2,6},{3,7},{4,0},{5,1},{6,2},{7,3},{8,12},{9,13},{10,... | collective-permute-start | bytes 393224 | tf_op jit(solution)/shard_map/ppermute | solution.py:345
  32.5 1.2 %copy-start.2 = (s32[4,65536]{1,0:T(4,128)S(1)}, s32[4,65536]{1,0:T(4,128)}, u32[]{:S(2)}) copy-start(s32[4,65536]{1,0:T(4,128)} %pixel_ref.1) | copy-start | bytes 3145732
  35.3 20.5 %collective-permute-start.6 = (f32[2,64,256]{2,1,0:T(8,128)S(1)}, f32[2,64,256]{2,1,0:T(8,128)S(1)}, u32[]{:S(2)}, u32[]{:S(2)}) collective-permute-start(f32[2,64,256]{2,1,0:T(8,128)S(1)} %get-tuple-element.30), channel_id=1, source_target_pairs={{0,6},{1,7},{2,4},{3,5},{4,2},{5,3},{6,0},{7,1},{8,14},{9,15},{10,... | collective-permute-start | bytes 393224 | tf_op jit(solution)/shard_map/ppermute | solution.py:345
  38.3 1.0 %copy-start.9 = (bf16[256,512]{1,0:T(8,128)(2,1)S(1)}, bf16[256,512]{1,0:T(8,128)(2,1)}, u32[]{:S(2)}) copy-start(bf16[256,512]{1,0:T(8,128)(2,1)} %constant.45.clone.refs_9_) | copy-start | bytes 786436
  39.3 0.9 %copy-start.11 = (bf16[256,512]{1,0:T(8,128)(2,1)S(1)}, bf16[256,512]{1,0:T(8,128)(2,1)}, u32[]{:S(2)}) copy-start(bf16[256,512]{1,0:T(8,128)(2,1)} %constant.44.clone.refs_8_) | copy-start | bytes 786436
  40.2 0.9 %copy-start.13 = (f32[144,256]{1,0:T(8,128)S(1)}, f32[144,256]{1,0:T(8,128)}, u32[]{:S(2)}) copy-start(f32[144,256]{1,0:T(8,128)} %constant.50.clone.refs_14_) | copy-start | bytes 442372
  41.1 0.9 %copy-start.15 = (f32[128,256]{1,0:T(8,128)S(1)}, f32[128,256]{1,0:T(8,128)}, u32[]{:S(2)}) copy-start(f32[128,256]{1,0:T(8,128)} %constant.49.clone.refs_13_) | copy-start | bytes 393220
  42.1 0.9 %copy-start.17 = (f32[128,256]{1,0:T(8,128)S(1)}, f32[128,256]{1,0:T(8,128)}, u32[]{:S(2)}) copy-start(f32[128,256]{1,0:T(8,128)} %constant.48.clone.refs_12_) | copy-start | bytes 393220
  43.0 0.9 %copy-start.19 = (bf16[256,256]{1,0:T(8,128)(2,1)S(1)}, bf16[256,256]{1,0:T(8,128)(2,1)}, u32[]{:S(2)}) copy-start(bf16[256,256]{1,0:T(8,128)(2,1)} %constant.47.clone.refs_11_) | copy-start | bytes 393220
  43.9 0.9 %copy-start.20 = (bf16[256,256]{1,0:T(8,128)(2,1)S(1)}, bf16[256,256]{1,0:T(8,128)(2,1)}, u32[]{:S(2)}) copy-start(bf16[256,256]{1,0:T(8,128)(2,1)} %constant.46.clone.refs_10_) | copy-start | bytes 393220
  44.8 0.9 %copy-start.21 = (bf16[256,256]{1,0:T(8,128)(2,1)S(1)}, bf16[256,256]{1,0:T(8,128)(2,1)}, u32[]{:S(2)}) copy-start(bf16[256,256]{1,0:T(8,128)(2,1)} %constant.43.clone.refs_7_) | copy-start | bytes 393220
  45.7 0.9 %copy-start.22 = (bf16[256,256]{1,0:T(8,128)(2,1)S(1)}, bf16[256,256]{1,0:T(8,128)(2,1)}, u32[]{:S(2)}) copy-start(bf16[256,256]{1,0:T(8,128)(2,1)} %constant.42.clone.refs_6_) | copy-start | bytes 393220
  46.6 9.3 %copy-start.10 = (bf16[256,512]{1,0:T(8,128)(2,1)S(1)}, bf16[256,512]{1,0:T(8,128)(2,1)}, u32[]{:S(2)}) copy-start(bf16[256,512]{1,0:T(8,128)(2,1)} %constant.45.clone.refs_9_) | copy-start | bytes 786436
  46.6 9.3 %copy-start.12 = (bf16[256,512]{1,0:T(8,128)(2,1)S(1)}, bf16[256,512]{1,0:T(8,128)(2,1)}, u32[]{:S(2)}) copy-start(bf16[256,512]{1,0:T(8,128)(2,1)} %constant.44.clone.refs_8_) | copy-start | bytes 786436
  46.6 9.3 %copy-start.14 = (f32[144,256]{1,0:T(8,128)S(1)}, f32[144,256]{1,0:T(8,128)}, u32[]{:S(2)}) copy-start(f32[144,256]{1,0:T(8,128)} %constant.50.clone.refs_14_) | copy-start | bytes 442372
  46.6 9.3 %copy-start.16 = (f32[128,256]{1,0:T(8,128)S(1)}, f32[128,256]{1,0:T(8,128)}, u32[]{:S(2)}) copy-start(f32[128,256]{1,0:T(8,128)} %constant.49.clone.refs_13_) | copy-start | bytes 393220
  46.6 9.3 %copy-start.18 = (f32[128,256]{1,0:T(8,128)S(1)}, f32[128,256]{1,0:T(8,128)}, u32[]{:S(2)}) copy-start(f32[128,256]{1,0:T(8,128)} %constant.48.clone.refs_12_) | copy-start | bytes 393220
  (1 other events, 0.7 us)

commit v2 on v1

v2 whole, which is shorter than its diff:
```python
import functools
import math

import jax
import jax.numpy as jnp
import numpy as np
from jax import lax
from jax.experimental import pallas as pl
from jax.experimental.pallas import tpu as pltpu
from jax.sharding import PartitionSpec as P

PIX = 128
COLS = 256
LANES = 128
HALVES = COLS // LANES
LOW = 64
SAMPLE_RATE = 200.0
MIB = 1024 * 1024
STEP = 8192
NT = (((1,), (1,)), ((), ()))
f32 = jnp.float32
bf16 = jnp.bfloat16


def split2(x):
    high = x.astype(bf16)
    return high, (x - high.astype(f32)).astype(bf16)


def split3(x):
    high = x.astype(bf16)
    rest = x - high.astype(f32)
    mid = rest.astype(bf16)
    return high, mid, (rest - mid.astype(f32)).astype(bf16)


@functools.lru_cache(maxsize=None)
def tables(rows):
    total = rows * COLS
    half = rows // 2
    slots = np.arange(half)
    slots[0] = half
    ramp = np.arange(rows)
    angle = 2.0 * np.pi * (slots[:, None] * ramp[None, :] % rows) / rows
    first = np.concatenate([np.cos(angle), -np.sin(angle)], axis=0)
    first[half] = 1.0
    weight = np.full((half,), 2.0)
    weight[0] = 1.0
    last = np.concatenate([weight[:, None] * np.cos(angle), -2.0 * np.sin(angle)], axis=0)
    last[half] = 1.0
    last = last.T / total
    col = np.arange(COLS)
    phase = 2.0 * np.pi * (col[:, None] * col[None, :] % COLS) / COLS
    turn = 2.0 * np.pi * (slots[:, None] * col[None, :] % total) / total
    bins = np.concatenate([slots, np.zeros((16,), np.int64)])[:, None] + rows * col[None, :]
    freq = np.minimum(bins, total - bins).astype(np.float32) * np.float32(SAMPLE_RATE / total)
    made = [first, np.cos(phase), np.sin(phase), last, np.cos(turn), np.sin(turn), freq * freq]
    return np.concatenate([table.astype(np.float32) for table in made], axis=0)


def dot3(left, right):
    (lh, ll), (rh, rl) = left, right
    return jnp.dot(
        jnp.concatenate([lh, ll, lh], axis=1),
        jnp.concatenate([rh, rh, rl], axis=0),
        preferred_element_type=f32,
    )


def fit_kernel(runs, run_len, paired, wafer_ref, data_ref, *refs):
    template_refs, out_ref = refs[:runs], refs[runs]
    parts = []
    for run in range(runs):
        temp = template_refs[run][0]
        modes = temp.shape[0]
        high, mid, low = split3(data_ref[run * run_len : (run + 1) * run_len, :])
        both = lax.dot_general(
            temp, jnp.concatenate([temp, high, mid, low], axis=0), NT, preferred_element_type=f32
        )
        ends = [modes + i * run_len for i in range(4)]
        parts.append(both[:, :modes])
        parts.append(
            both[:, ends[0] : ends[1]] + both[:, ends[1] : ends[2]] + both[:, ends[2] : ends[3]]
        )
        if paired:
            refs[runs + 1][run * modes : (run + 1) * modes, :] = temp.astype(f32)
    part = jnp.concatenate(parts, axis=1)

    @pl.when(pl.program_id(0) == 0)
    def _():
        out_ref[...] = part

    @pl.when(pl.program_id(0) > 0)
    def _():
        out_ref[...] += part


def eliminate(sums, runs, run_len, modes):
    width = modes + run_len
    row_index = lax.broadcasted_iota(jnp.int32, (modes, width), 0)
    joined = [sums[:, run * width : (run + 1) * width] for run in range(runs)]
    for column in range(modes):
        for run in range(runs):
            now = joined[run]
            pivot_row = now[column : column + 1, :] / now[column : column + 1, column : column + 1]
            rest = now - now[:, column : column + 1] * pivot_row
            joined[run] = jnp.where(row_index == column, pivot_row, rest)
    return [now[:, modes:] for now in joined]


def paired_kernel(
    runs, run_len, local_dets, chunks, wafer_ref, data_ref, got_ref, wide_ref, temp_ref, *refs
):
    chips = data_ref.shape[0] // (2 * local_dets)
    terms, refs = [ref[...] for ref in refs[:chips]], refs[chips:]
    while len(terms) > 1:
        terms = [a + b for a, b in zip(terms[0::2], terms[1::2])]
    amps_ref, out_refs, rows_ref = refs[0], refs[1:-1], refs[-1]
    modes = temp_ref.shape[1]
    row_count, time_local = data_ref.shape
    kept = row_count // 2
    pieces = time_local // COLS
    amps = eliminate(terms[0], runs, run_len, modes)
    amps_ref[...] = jnp.concatenate(amps, axis=1)
    me = lax.axis_index("tm")
    core, chip = jnp.bitwise_and(me, 1), jnp.right_shift(me, 1)
    per_run = run_len // 2
    shard_rows = HALVES * pieces * kept

    def mine(rows):
        groups = [rows[start : start + local_dets] for start in range(0, run_len, local_dets)]
        even, odd = jnp.concatenate(groups[0::2], axis=0), jnp.concatenate(groups[1::2], axis=0)
        return jnp.where(core == 0, even, odd)

    for run in range(runs):
        left = jnp.concatenate(split3(mine(amps[run].T)), axis=1)
        own = temp_ref[wafer_ref[run * run_len]]
        other = wide_ref[run * modes : (run + 1) * modes, :].astype(bf16)
        for side, (temp, source) in enumerate([(own, data_ref), (other, got_ref)]):
            fitted = jnp.dot(left, jnp.concatenate([temp] * 3, axis=0), preferred_element_type=f32)
            kept_rows = mine(source[run * run_len : (run + 1) * run_len, :]) - fitted
            for lane in range(time_local // LANES):
                start = side * shard_rows + run * per_run
                start += (lane % HALVES * pieces + lane // HALVES) * kept
                rows_ref[start : start + per_run, :] = kept_rows[:, lane * LANES : (lane + 1) * LANES]
    per_chunk = local_dets // chunks
    for chunk in range(chunks):
        for step in range(chips):
            base = jnp.bitwise_xor(chip, step) * local_dets + chunk * per_chunk
            for det in range(per_chunk):
                for side in range(2):
                    place = pl.multiple_of(jnp.bitwise_xor(core, side) * pieces, pieces)
                    out_refs[chunk * chips + step][det, pl.ds(place, pieces), :] = take_rows(
                        rows_ref, side * shard_rows + base + det, pieces, kept
                    )


def residual_kernel(runs, run_len, owners, wafer_ref, data_ref, temp_ref, sums_ref, *refs):
    amps_ref, out_ref, rows_ref = refs
    modes = temp_ref.shape[1]
    row_count, time_local = data_ref.shape
    pieces = time_local // COLS
    amps = eliminate(sums_ref[...], runs, run_len, modes)
    amps_ref[...] = jnp.concatenate(amps, axis=1)
    for run in range(runs):
        temp = temp_ref[wafer_ref[run * run_len]]
        left = jnp.concatenate(split3(amps[run].T), axis=1)
        fitted = jnp.dot(left, jnp.concatenate([temp] * 3, axis=0), preferred_element_type=f32)
        rows = slice(run * run_len, (run + 1) * run_len)
        for lane in range(time_local // LANES):
            cols = slice(lane * LANES, (lane + 1) * LANES)
            start = (lane % HALVES * pieces + lane // HALVES) * row_count + run * run_len
            rows_ref[start : start + run_len, :] = data_ref[rows, cols] - fitted[:, cols]
    local_dets = row_count // owners
    for owner in range(owners):
        for det in range(local_dets):
            out_ref[owner, det] = take_rows(rows_ref, owner * local_dets + det, pieces, row_count)


def take_rows(ref, start, count, stride):
    return jnp.concatenate(
        [
            ref[pl.ds(side * count * stride + start, count, stride=stride), :]
            for side in range(HALVES)
        ],
        axis=1,
    )


def binned(high_rows, low_rows, value_rows, weight_row, tall):
    high_ramp = lax.broadcasted_iota(jnp.int32, (tall, COLS), 0).astype(f32).astype(bf16)
    low_ramp = lax.broadcasted_iota(jnp.int32, (LOW, COLS), 0).astype(f32).astype(bf16)
    weight = jnp.broadcast_to(weight_row, (tall, COLS)).astype(bf16)
    zero, one = jnp.zeros((tall, COLS), bf16), jnp.ones((LOW, COLS), bf16)
    lefts, rights = [], []
    for row in range(high_rows.shape[0]):
        high = jnp.broadcast_to(high_rows[row : row + 1], (tall, COLS)).astype(bf16)
        low = jnp.broadcast_to(low_rows[row : row + 1], (LOW, COLS)).astype(bf16)
        value = jnp.broadcast_to(value_rows[row : row + 1], (tall, COLS)).astype(bf16)
        hot = high == high_ramp
        lefts.append(
            jnp.concatenate([jnp.where(hot, value, zero), jnp.where(hot, weight, zero)], axis=0)
        )
        rights.append(jnp.where(low == low_ramp, one, jnp.zeros_like(one)))
    return lax.dot_general(
        jnp.concatenate(lefts, axis=1),
        jnp.concatenate(rights, axis=1),
        NT,
        preferred_element_type=f32,
    )


def prepare_kernel(knee_ref, white_ref, after_ref, table_ref, tile_ref, pixel_ref, *refs):
    outs, (turn_cos, turn_sin, gain_ref, inverse_ref, high_ref, low_ref, hi_s, lo_s) = refs[:6], refs[6:]
    local_dets, rows = high_ref.shape[0], high_ref.shape[1]
    half = rows // 2
    tables_at = [0]
    for height in (rows, COLS, COLS, rows, half, half):
        tables_at.append(tables_at[-1] + height)
    first, cosine, sine, last, turn_c, turn_s = (
        table_ref[start:end, :] for start, end in zip(tables_at[:-1], tables_at[1:])
    )
    for i, table in enumerate((first, jnp.concatenate([cosine, sine], axis=1), last)):
        outs[2 * i][...], outs[2 * i + 1][...] = split2(table)
    turn_cos[...], turn_sin[...] = turn_c, turn_s
    squared = table_ref[tables_at[-1] :, :]
    cell = tile_ref[...] * PIX + pixel_ref[...]
    high = jnp.right_shift(cell, LOW.bit_length() - 1).astype(f32)
    low = jnp.bitwise_and(cell, LOW - 1).astype(f32)
    for lane in range(rows * HALVES):
        cols = slice(lane * LANES, (lane + 1) * LANES)
        start = (lane % HALVES * rows + lane // HALVES) * local_dets
        hi_s[start : start + local_dets, :] = high[:, cols]
        lo_s[start : start + local_dets, :] = low[:, cols]
    for det in range(local_dets):
        high_ref[det] = take_rows(hi_s, det, rows, local_dets)
        low_ref[det] = take_rows(lo_s, det, rows, local_dets)
        knee = knee_ref[det]
        gain_ref[det] = squared / (white_ref[det] * (squared + knee * knee))
        inverse_ref[det] = 1.0 / jnp.full((1, COLS), white_ref[det], f32)


def filter_kernel(parts, first_det, count, dets, final, order_ref, *refs):
    part_refs = refs[:parts]
    (f_h, f_l, s_h, s_l, l_h, l_l, tc_ref, ts_ref, gain_ref, inverse_ref, high_ref, low_ref) = refs[
        parts : parts + 12
    ]
    refs = refs[parts + 12 :]
    if first_det > 0:
        before_ref, sums_ref, refs = refs[0], refs[1], refs[2:]
    if final:
        out_ref, sky_ref, weight_ref, signal, stacked, totals = refs
    else:
        stacked, totals, signal = refs
    rows = signal.shape[0]
    half = rows // 2
    totals[...] = sums_ref[...] if first_det > 0 else jnp.zeros_like(totals)
    tall = totals.shape[0] // 2
    row_index = lax.broadcasted_iota(jnp.int32, (half, COLS), 0)
    chip = jnp.right_shift(lax.axis_index("tm"), 1)

    def one(turn):
        det = turn + first_det
        for part in range(parts):
            height = part_refs[part].shape[1]
            start = 0
            if parts > 1:
                start = pl.multiple_of(jnp.bitwise_xor(chip, part) * height, height)
            signal[pl.ds(start, height), :] = part_refs[part][turn]
        turn_cos, turn_sin = tc_ref[...], ts_ref[...]
        side = (s_h[...], s_l[...])
        first = dot3((f_h[...], f_l[...]), split2(signal[...]))
        real_y, low_y = first[:half], first[half:]
        imag_y = jnp.where(row_index == 0, 0.0, low_y)
        zero_y = jnp.broadcast_to(low_y[0:1], (16, COLS))
        real_z = real_y * turn_cos + imag_y * turn_sin
        imag_z = imag_y * turn_cos - real_y * turn_sin
        forward = dot3(split2(jnp.concatenate([real_z, imag_z, zero_y], axis=0)), side)
        cos_f, sin_f = forward[:, :COLS], forward[:, COLS:]
        gain = gain_ref[det]
        gain_main, gain_zero = gain[:half], gain[half:]
        real_x = (cos_f[:half] + sin_f[half : 2 * half]) * gain_main
        imag_x = (cos_f[half : 2 * half] - sin_f[:half]) * gain_main
        zero_r = cos_f[2 * half :] * gain_zero
        zero_i = -sin_f[2 * half :] * gain_zero
        back = dot3(split2(jnp.concatenate([real_x, imag_x, zero_r, zero_i], axis=0)), side)
        cos_b, sin_b = back[:, :COLS], back[:, COLS:]
        real_u = cos_b[:half] - sin_b[half : 2 * half]
        imag_u = sin_b[:half] + cos_b[half : 2 * half]
        zero_o = cos_b[2 * half : 2 * half + 16] - sin_b[2 * half + 16 :]
        real_v = real_u * turn_cos - imag_u * turn_sin
        imag_v = real_u * turn_sin + imag_u * turn_cos
        imag_v = jnp.where(row_index == 0, zero_o[0:1], imag_v)
        result = dot3((l_h[...], l_l[...]), split2(jnp.concatenate([real_v, imag_v], axis=0)))
        signal[...] = result
        for half_index in range(HALVES):
            cols = slice(half_index * LANES, (half_index + 1) * LANES)
            stacked[pl.ds(half_index * rows * dets + det, rows, stride=dets), :] = result[:, cols]
        totals[...] += binned(high_ref[det], low_ref[det], result, inverse_ref[det], tall)

    for turn in range(count):
        one(turn)
    if final:
        det_index = lax.broadcasted_iota(jnp.int32, (dets, LANES), 0)
        for lane in range(rows * HALVES):
            start = (lane % HALVES * rows + lane // HALVES) * dets
            here = stacked[start : start + dets, :]
            if first_det > 0:
                here = jnp.where(det_index < first_det, before_ref[start : start + dets, :], here)
            out_ref[:, lane * LANES : (lane + 1) * LANES] = here.astype(bf16)
        per_tile = PIX // LOW
        for tile in range(sky_ref.shape[0]):
            source = order_ref[tile] * per_tile
            for piece in range(per_tile):
                cols = slice(piece * LOW, (piece + 1) * LOW)
                sky_ref[tile : tile + 1, cols] = totals[pl.ds(source + piece, 1), :]
                weight_ref[tile : tile + 1, cols] = totals[pl.ds(tall + source + piece, 1), :]


def swap(x, step, axis):
    size = lax.axis_size(axis)
    return lax.ppermute(x, axis, [(i, i ^ step) for i in range(size)])


def vmem(limit):
    return pltpu.CompilerParams(vmem_limit_bytes=limit * MIB)


def shards(
    detector_data, templates, wafer_of, knee_freq, white_level, tile_id, pixel_id, tile_order
):
    row_count, time_local = detector_data.shape
    wafer_count, modes, _ = templates.shape
    owners, groups = lax.axis_size("tm"), lax.axis_size("det")
    run_len = min(row_count, row_count * groups // wafer_count)
    runs = row_count // run_len
    width = runs * (modes + run_len)
    local_dets = row_count // owners
    full_length = time_local * owners
    rows = full_length // COLS
    pieces = time_local // COLS
    paired = owners & (owners - 1) == 0 and 4 <= owners <= 8 and run_len % (2 * local_dets) == 0
    step_len = min(STEP, time_local)
    smem = pl.BlockSpec(memory_space=pltpu.SMEM)
    whole = pl.BlockSpec(memory_space=pltpu.VMEM)
    anywhere = pl.BlockSpec(memory_space=pl.ANY)

    def template_spec(run):
        return pl.BlockSpec((1, modes, step_len), lambda i, w, run=run: (w[run * run_len], 0, i))

    def by_step(height):
        return pl.BlockSpec((height, step_len), lambda i, w: (0, i))

    if paired:
        got = swap(detector_data, 1, "tm")
    sums, *wide = pl.pallas_call(
        functools.partial(fit_kernel, runs, run_len, paired),
        out_shape=[jax.ShapeDtypeStruct((modes, width), f32)]
        + [jax.ShapeDtypeStruct((runs * modes, time_local), f32)] * paired,
        grid_spec=pltpu.PrefetchScalarGridSpec(
            num_scalar_prefetch=1,
            grid=(time_local // step_len,),
            in_specs=[by_step(row_count)] + [template_spec(run) for run in range(runs)],
            out_specs=[pl.BlockSpec((modes, width), lambda i, w: (0, 0))]
            + [by_step(runs * modes)] * paired,
        ),
        compiler_params=vmem(60),
        name="fit_sums",
    )(wafer_of, detector_data, *[templates] * runs)
    if paired:
        wide = swap(wide[0], 1, "tm")
    if paired:
        sums = sums + swap(sums, 1, "tm")
        sums = [sums] + [swap(sums, step, "tm") for step in range(2, owners, 2)]
    else:
        sums = [lax.psum(sums, "tm")]

    chunks = 2 if paired and local_dets % 2 == 0 else 1
    per_chunk = local_dets // chunks
    if paired:
        chips = owners // 2
        blocks_out = [(per_chunk, 2 * pieces, COLS)] * (chunks * chips)
        kernel = functools.partial(paired_kernel, runs, run_len, local_dets, chunks)
        operands = [detector_data, got, wide, templates]
        scratch = pltpu.VMEM((HALVES * pieces * row_count, LANES), f32)
    else:
        blocks_out = [(owners, local_dets, pieces, COLS)]
        kernel = functools.partial(residual_kernel, runs, run_len, owners)
        operands = [detector_data, templates]
        scratch = pltpu.VMEM((HALVES * pieces * row_count, LANES), f32)
    fit_amps, *blocks = pl.pallas_call(
        kernel,
        out_shape=[jax.ShapeDtypeStruct(shape, f32) for shape in [(modes, row_count), *blocks_out]],
        in_specs=[smem] + [whole] * (len(sums) + len(operands)),
        out_specs=[whole] * (1 + len(blocks_out)),
        scratch_shapes=[scratch],
        compiler_params=vmem(32),
        name="residual",
    )(wafer_of, *operands, *sums)

    if paired:
        received = [blocks[chunk * chips : (chunk + 1) * chips] for chunk in range(chunks)]
        for step in reversed(range(1, chips)):
            received[0][step] = swap(received[0][step], 2 * step, "tm")
    else:
        moved = lax.all_to_all(blocks[0], "tm", split_axis=0, concat_axis=0, tiled=True)
        received = [[jnp.swapaxes(moved, 0, 1).reshape(local_dets, rows, COLS)]]

    tile_count = tile_order.shape[0]
    tall = tile_count * PIX // LOW
    table = jnp.asarray(tables(rows))
    half = rows // 2
    grid_shape = (local_dets, rows, COLS)
    pair_shapes = [(rows, rows), (COLS, 2 * COLS), (rows, rows)]
    pairs = [jax.ShapeDtypeStruct(shape, bf16) for shape in pair_shapes for _ in range(2)]
    prepared_shapes = [
        (half, COLS),
        (half, COLS),
        (local_dets, half + 16, COLS),
        (local_dets, 1, COLS),
        grid_shape,
        grid_shape,
    ]
    prepared = pl.pallas_call(
        prepare_kernel,
        out_shape=pairs + [jax.ShapeDtypeStruct(shape, f32) for shape in prepared_shapes],
        in_specs=[smem, smem, anywhere, whole, whole, whole],
        out_specs=[whole] * 12,
        scratch_shapes=[pltpu.VMEM((HALVES * rows * local_dets, LANES), f32)] * 2,
        compiler_params=vmem(32),
        cost_estimate=pl.CostEstimate(
            flops=0, bytes_accessed=32 * local_dets * full_length, transcendentals=0
        ),
        name="prepare",
    )(knee_freq, white_level, fit_amps, table, tile_id, pixel_id)

    for chunk in range(1, chunks):
        received, prepared = lax.optimization_barrier((received, prepared))
        for step in reversed(range(1, chips)):
            received[chunk][step] = swap(received[chunk][step], 2 * step, "tm")

    stacked_shape = (HALVES * rows * local_dets, LANES)
    carried = []
    for chunk in range(chunks):
        final = chunk == chunks - 1
        first_det = chunk * per_chunk
        parts = len(received[chunk])
        if final:
            outs = [((local_dets, full_length), bf16)] + [((tile_count, PIX), f32)] * 2
            scratch = [pltpu.VMEM(s, f32) for s in ((rows, COLS), stacked_shape, (2 * tall, LOW))]
        else:
            outs = [(stacked_shape, f32), ((2 * tall, LOW), f32)]
            scratch = [pltpu.VMEM((rows, COLS), f32)]
        operands = [*received[chunk], *prepared, *carried]
        carried = pl.pallas_call(
            functools.partial(filter_kernel, parts, first_det, per_chunk, local_dets, final),
            out_shape=[jax.ShapeDtypeStruct(*o) for o in outs],
            in_specs=[smem] + [whole] * len(operands),
            out_specs=[whole] * len(outs),
            scratch_shapes=scratch,
            compiler_params=vmem(32),
            cost_estimate=pl.CostEstimate(
                flops=80000 * per_chunk * full_length,
                bytes_accessed=16 * per_chunk * full_length,
                transcendentals=0,
            ),
            name="filter_and_bin",
        )(tile_order, *operands)
    weighted_data, sky_part, weight_part = carried

    owned = tile_count * PIX // owners
    both = jnp.concatenate(
        [sky_part.reshape(owners, owned), weight_part.reshape(owners, owned)], axis=1
    )
    spread = jnp.broadcast_to(both[None], (groups, *both.shape)).reshape(groups * owners, 2 * owned)
    spread = lax.all_to_all(spread, ("det", "tm"), split_axis=0, concat_axis=0, tiled=True)
    scale = float(tile_count * PIX) / float(local_dets * groups * owners * full_length)
    summed = jnp.sum(spread, axis=0) * scale
    return (fit_amps, weighted_data, summed[:owned], summed[owned:])


def solution(mesh):
    in_specs = (
        P("det", "tm"),
        P(None, None, "tm"),
        P("det"),
        P(("det", "tm")),
        P(("det", "tm")),
        P(("det", "tm"), None),
        P(("det", "tm"), None),
        P(),
    )
    out_specs = (P(None, "det"), P(("det", "tm"), None), P("tm"), P("tm"))
    return jax.shard_map(shards, mesh=mesh, in_specs=in_specs, out_specs=out_specs, check_vma=False)
```

time: 87 us -> 71.7 us (0.82)
  local copies, waits for them, and re-layouts: 11.9 us -> 1.39 us
  blocking collectives: 19.5 us -> 12.3 us
  waiting for transfers between devices: 6.82 us -> 13 us
  Pallas kernels: 29.5 us -> 27.4 us
  other arithmetic: 2.03 us -> 0.78 us
    unnamed x46 -> x20, local copies, waits for them, and re-layouts: 11.2 us -> 0.73 us
    all_to_all x1, blocking collectives: 19.5 us -> 12.3 us  [shards(): lax.all_to_all(spread, ('det', 'tm'), split_axis=0, concat_axis=0, tiled=...]
    ppermute x10 -> x12, waiting for transfers between devices: 6.82 us -> 13 us  [swap(): return lax.ppermute(x, axis, [(i, i ^ step) for i in range(size)])]
    pallas_call x4, Pallas kernels: 25.6 us -> 23.7 us  [the longest x2 18.4 us: shards(): pl.pallas_call(functools.partial(filter_kernel, parts, first_det, per_chu...]
    concatenate x1 -> x0, other arithmetic: 1.24 us -> none  [shards(): scalars = jnp.concatenate([wafer_of, me[None]])]
    ppermute x10 -> x12, starting transfers between devices: 15.9 us -> 15.7 us  [swap(): return lax.ppermute(x, axis, [(i, i ^ step) for i in range(size)])]
  transfers between devices with their start and end apart: 10 -> 12, of which waited for: 4 -> 5; matrix products, arithmetic and copies ran while one was open for 1% -> 1% of each run, Pallas kernels for 12% -> 14%
where the time goes in v2:
time: 71.7 us; the launch traced here: 71.4 us
  Pallas kernels  27.4 us (38%)
  starting transfers between devices  15.7 us (22%)
  waiting for transfers between devices  13 us (18%)
  blocking collectives  12.3 us (17%)
  local copies, waits for them, and re-layouts  1.39 us (2%)
  other arithmetic  0.78 us (1%)
  between operations  0.77 us (1%)
    pallas_call x2, Pallas kernels, shards(): pl.pallas_call(functools.partial(filter_kernel, parts, first_det, per_chu...  18.4 us
    ppermute x12, starting transfers between devices, swap(): return lax.ppermute(x, axis, [(i, i ^ step) for i in range(size)])  15.7 us
    ppermute x12, waiting for transfers between devices, swap(): return lax.ppermute(x, axis, [(i, i ^ step) for i in range(size)])  13 us
    all_to_all x1, blocking collectives, shards(): lax.all_to_all(spread, ('det', 'tm'), split_axis=0, concat_axis=0, tiled=...  12.3 us
    pallas_call x1, Pallas kernels, shards(): pl.pallas_call(functools.partial(fit_kernel, runs, run_len, paired), out_...  3.73 us
    pallas_call x1, Pallas kernels, shards(): pl.pallas_call(kernel, out_shape=[jax.ShapeDtypeStruct(shape, f32) for sh...  3.72 us
    pallas_call x1, Pallas kernels, shards(): pl.pallas_call(prepare_kernel, out_shape=pairs + [jax.ShapeDtypeStruct(sh...  1.56 us
  transfers between devices with their start and end apart: 12, of which 5 were waited for; matrix products, arithmetic and copies ran while one was open for 1% of the time, Pallas kernels for 14%

profile of v2, /device:TPU:0, one launch (start us, length us, event | category | flops | bytes accessed | tf_op | source)
XLA Modules:
  0.0 71.4 jit_solution(5894661243626075255)
XLA Ops:
  0.7 3.7 %fit_sums.1 = (f32[16,64]{1,0:T(8,128)}, f32[32,8192]{1,0:T(8,128)}) custom-call(s32[32]{0:T(128)} %wafer_ref.3, f32[32,8192]{1,0:T(8,128)} %data_ref.3, bf16[8,16,8192]{2,1,0:T(8,128)(2,1)} %temp_ref.1, bf16[8,16,8192]{2,1,0:T(8,128)(2,1)} %temp_ref.1), custom_call_target="tpu_custom_call" | custom-call | tf_op jit(solution)/shard_map/fit_sums/pallas_call | solution.py:356
  4.4 0.5 collective-permute-start.1
  4.8 0.1 collective-permute-start
  4.9 0.5 collective-permute-start.2
  5.4 2.9 %collective-permute-done.2 = f32[16,64]{1,0:T(8,128)S(1)} collective-permute-done((f32[16,64]{1,0:T(8,128)}, f32[16,64]{1,0:T(8,128)S(1)}, u32[]{:S(2)}, u32[]{:S(2)}) %collective-permute-start.2) | collective-permute-done | bytes 4128 | tf_op jit(solution)/shard_map/ppermute | solution.py:322
  8.3 0.7 add.3.refs_0_
  9.0 0.0 copy-start.8
  9.0 5.1 %collective-permute-start.5 = (f32[16,64]{1,0:T(8,128)S(1)}, f32[16,64]{1,0:T(8,128)S(1)}, u32[]{:S(2)}, u32[]{:S(2)}) collective-permute-start(f32[16,64]{1,0:T(8,128)S(1)} %add.3.refs_0_), channel_id=1, source_target_pairs={{0,6},{1,7},{2,4},{3,5},{4,2},{5,3},{6,0},{7,1},{8,14},{9,15},{10,... | collective-permute-start | bytes 12296 | tf_op jit(solution)/shard_map/ppermute | solution.py:322
  14.1 0.6 collective-permute-start.3
  14.7 1.0 %collective-permute-done.5.refs_3_ = f32[16,64]{1,0:T(8,128)S(1)} collective-permute-done((f32[16,64]{1,0:T(8,128)S(1)}, f32[16,64]{1,0:T(8,128)S(1)}, u32[]{:S(2)}, u32[]{:S(2)}) %collective-permute-start.5) | collective-permute-done | bytes 4128 | tf_op jit(solution)/shard_map/ppermute | solution.py:322
  15.7 2.9 %collective-permute-done.4.refs_2_ = f32[16,64]{1,0:T(8,128)S(1)} collective-permute-done((f32[16,64]{1,0:T(8,128)S(1)}, f32[16,64]{1,0:T(8,128)S(1)}, u32[]{:S(2)}, u32[]{:S(2)}) %collective-permute-start.4) | collective-permute-done | bytes 4128 | tf_op jit(solution)/shard_map/ppermute | solution.py:322
  18.7 0.0 collective-permute-done.3.refs_1_
  18.7 0.0 collective-permute-done.1.wide_ref
  18.7 3.7 %residual.1 = (f32[16,32]{1,0:T(8,128)}, f32[2,64,256]{2,1,0:T(8,128)S(1)}, f32[2,64,256]{2,1,0:T(8,128)S(1)}, f32[2,64,256]{2,1,0:T(8,128)S(1)}, f32[2,64,256]{...) custom-call(s32[32]{0:T(128)S(1)} %copy-done.6, ...), custom_call_target="tpu_custom_call" | custom-call | tf_op jit(solution)/shard_map/residual/pallas_call | solution.py:391
  22.4 2.0 %collective-permute-start.7 = (f32[2,64,256]{2,1,0:T(8,128)S(1)}, f32[2,64,256]{2,1,0:T(8,128)S(1)}, u32[]{:S(2)}, u32[]{:S(2)}) collective-permute-start(f32[2,64,256]{2,1,0:T(8,128)S(1)} %get-tuple-element.57), channel_id=1, source_target_pairs={{0,4},{1,5},{2,6},{3,7},{4,0},{5,1},{6,2},{7,3},{8,12},{9,13},{10,... | collective-permute-start | bytes 393224 | tf_op jit(solution)/shard_map/ppermute | solution.py:322
  24.4 2.4 %collective-permute-start.8 = (f32[2,64,256]{2,1,0:T(8,128)S(1)}, f32[2,64,256]{2,1,0:T(8,128)S(1)}, u32[]{:S(2)}, u32[]{:S(2)}) collective-permute-start(f32[2,64,256]{2,1,0:T(8,128)S(1)} %get-tuple-element.58), channel_id=1, source_target_pairs={{0,6},{1,7},{2,4},{3,5},{4,2},{5,3},{6,0},{7,1},{8,14},{9,15},{10,... | collective-permute-start | bytes 393224 | tf_op jit(solution)/shard_map/ppermute | solution.py:322
  26.8 0.0 copy-start.5
  26.8 0.7 copy-done.5
  27.5 1.6 %prepare.1 = (bf16[256,256]{1,0:T(8,128)(2,1)S(1)}, bf16[256,256]{1,0:T(8,128)(2,1)S(1)}, bf16[256,512]{1,0:T(8,128)(2,1)S(1)}, bf16[256,512]{1,0:T(8,128)(2,1)S...) custom-call(f32[4]{0:T(128)S(1)} %copy-done.7, ...), custom_call_target="tpu_custom_call" | custom-call | bytes 8388608 | tf_op jit(solution)/shard_map/prepare/pallas_call | solution.py:424
  29.1 0.0 collective-permute-done.6.refs_1_
  29.1 5.6 %collective-permute-done.7.refs_2_ = f32[2,64,256]{2,1,0:T(8,128)S(1)} collective-permute-done((f32[2,64,256]{2,1,0:T(8,128)S(1)}, f32[2,64,256]{2,1,0:T(8,128)S(1)}, u32[]{:S(2)}, u32[]{:S(2)}) %collective-permute-start.7) | collective-permute-done | bytes 131104 | tf_op jit(solution)/shard_map/ppermute | solution.py:322
  34.7 2.0 %collective-permute-start.9 = (f32[2,64,256]{2,1,0:T(8,128)S(1)}, f32[2,64,256]{2,1,0:T(8,128)S(1)}, u32[]{:S(2)}, u32[]{:S(2)}) collective-permute-start(f32[2,64,256]{2,1,0:T(8,128)S(1)} %get-tuple-element.76), channel_id=1, source_target_pairs={{0,2},{1,3},{2,0},{3,1},{4,6},{5,7},{6,4},{7,5},{8,10},{9,11},{10,... | collective-permute-start | bytes 393224 | tf_op jit(solution)/shard_map/ppermute | solution.py:322
  36.7 1.2 %collective-permute-start.10 = (f32[2,64,256]{2,1,0:T(8,128)S(1)}, f32[2,64,256]{2,1,0:T(8,128)S(1)}, u32[]{:S(2)}, u32[]{:S(2)}) collective-permute-start(f32[2,64,256]{2,1,0:T(8,128)S(1)} %get-tuple-element.77), channel_id=1, source_target_pairs={{0,4},{1,5},{2,6},{3,7},{4,0},{5,1},{6,2},{7,3},{8,12},{9,13},{10,... | collective-permute-start | bytes 393224 | tf_op jit(solution)/shard_map/ppermute | solution.py:322
  37.9 1.5 %collective-permute-start.11 = (f32[2,64,256]{2,1,0:T(8,128)S(1)}, f32[2,64,256]{2,1,0:T(8,128)S(1)}, u32[]{:S(2)}, u32[]{:S(2)}) collective-permute-start(f32[2,64,256]{2,1,0:T(8,128)S(1)} %get-tuple-element.78), channel_id=1, source_target_pairs={{0,6},{1,7},{2,4},{3,5},{4,2},{5,3},{6,0},{7,1},{8,14},{9,15},{10,... | collective-permute-start | bytes 393224 | tf_op jit(solution)/shard_map/ppermute | solution.py:322
  39.3 8.6 %filter_and_bin.2 = (f32[2048,128]{1,0:T(8,128)S(1)}, f32[64,64]{1,0:T(8,128)S(1)}) custom-call(s32[16]{0:T(128)S(1)} %copy-done.9, f32[2,64,256]{2,1,0:T(8,128)S(1)} %get-tuple-element.91.refs_0_, f32[2,64,256]{2,1,0:T(8,128)S(1)} %collective-permute-done.6.refs_1_, f32[2,64,256]{2,1,0:T(8,128)S(1)} %collective-permute-done.7.refs_2_, ...), custom_call_target="tpu_custom_call" | custom-call | flops 10485760000 | bytes 2097152 | tf_op jit(solution)/shard_map/filter_and_bin/pallas_call | solution.py:455
  47.9 0.0 collective-permute-done.9.refs_1_
  47.9 0.6 collective-permute-done.10.refs_2_
  48.5 9.8 %filter_and_bin.3 = (bf16[4,65536]{1,0:T(4,128)(2,1)}, f32[16,128]{1,0:T(8,128)S(1)}, f32[16,128]{1,0:T(8,128)S(1)}) custom-call(s32[16]{0:T(128)S(1)} %copy-done.9, f32[2,64,256]{2,1,0:T(8,128)S(1)} %get-tuple-element.75.refs_0_, f32[2,64,256]{2,1,0:T(8,128)S(1)} %collective-permute-done.9.refs_1_, f32[2,64,256]{2,1,0:T(8,128)S(1)} %collective-permute-done.10.refs_2_, ...), custom_call_target="tpu_custom_call" | custom-call | flops 10485760000 | bytes 2097152 | tf_op jit(solution)/shard_map/filter_and_bin/pallas_call | solution.py:455
  58.4 0.1 all_to_all.6
  58.4 12.3 %all_to_all.9 = f32[32,1,512]{2,1,0:T(1,128)S(1)} all-to-all(f32[32,1,512]{2,1,0:T(1,128)S(1)} %all_to_all.6), channel_id=1, replica_groups=mesh['det'=4,'tm'=8] {'det','tm'}, dimensions={0} | all-to-all | bytes 131072 | tf_op jit(solution)/shard_map/all_to_all | solution.py:476
  70.7 0.1 reduce_sum.9
  70.8 0.6 fusion
  (27 shorter events, 0.1 us)
Async XLA Ops:
  0.6 4.2 %copy-start.1 = (f32[32,8192]{1,0:T(8,128)S(1)}, f32[32,8192]{1,0:T(8,128)}, u32[]{:S(2)}) copy-start(f32[32,8192]{1,0:T(8,128)} %data_ref.3) | copy-start | bytes 3145732
  0.6 18.0 %copy-start.6 = (s32[32]{0:T(128)S(1)}, s32[32]{0:T(128)}, u32[]{:S(2)}) copy-start(s32[32]{0:T(128)} %wafer_ref.3) | copy-start | bytes 388
  0.7 18.0 %copy-start = (bf16[8,16,8192]{2,1,0:T(8,128)(2,1)S(1)}, bf16[8,16,8192]{2,1,0:T(8,128)(2,1)}, u32[]{:S(2)}) copy-start(bf16[8,16,8192]{2,1,0:T(8,128)(2,1)} %temp_ref.1) | copy-start | bytes 6291460
  4.4 14.3 %collective-permute-start.1 = (f32[32,8192]{1,0:T(8,128)}, f32[32,8192]{1,0:T(8,128)S(1)}, u32[]{:S(2)}, u32[]{:S(2)}) collective-permute-start(f32[32,8192]{1,0:T(8,128)} %get-tuple-element.52), channel_id=1, source_target_pairs={{0,1},{1,0},{2,3},{3,2},{4,5},{5,4},{6,7},{7,6},{8,9},{9,8},{10,11... | collective-permute-start | bytes 3145736 | tf_op jit(solution)/shard_map/ppermute | solution.py:322
  4.8 13.8 %collective-permute-start = (f32[32,8192]{1,0:T(8,128)S(1)}, f32[32,8192]{1,0:T(8,128)S(1)}, u32[]{:S(2)}, u32[]{:S(2)}) collective-permute-start(f32[32,8192]{1,0:T(8,128)S(1)} %copy-done.1), channel_id=1, source_target_pairs={{0,1},{1,0},{2,3},{3,2},{4,5},{5,4},{6,7},{7,6},{8,9},{9,8},{10,11... | collective-permute-start | bytes 3145736 | tf_op jit(solution)/shard_map/ppermute | solution.py:322
  4.9 3.4 %collective-permute-start.2 = (f32[16,64]{1,0:T(8,128)}, f32[16,64]{1,0:T(8,128)S(1)}, u32[]{:S(2)}, u32[]{:S(2)}) collective-permute-start(f32[16,64]{1,0:T(8,128)} %get-tuple-element.53), channel_id=1, source_target_pairs={{0,1},{1,0},{2,3},{3,2},{4,5},{5,4},{6,7},{7,6},{8,9},{9,8},{10,11... | collective-permute-start | bytes 12296 | tf_op jit(solution)/shard_map/ppermute | solution.py:322
  9.0 17.8 %copy-start.2 = (f32[1424,256]{1,0:T(8,128)S(1)}, f32[1424,256]{1,0:T(8,128)}, u32[]{:S(2)}) copy-start(f32[1424,256]{1,0:T(8,128)} %constant.6.clone.table_ref) | copy-start | bytes 4374532
  9.0 17.8 %copy-start.3 = (s32[4,65536]{1,0:T(4,128)S(1)}, s32[4,65536]{1,0:T(4,128)}, u32[]{:S(2)}) copy-start(s32[4,65536]{1,0:T(4,128)} %tile_ref.1) | copy-start | bytes 3145732
  9.0 17.8 %copy-start.4 = (s32[4,65536]{1,0:T(4,128)S(1)}, s32[4,65536]{1,0:T(4,128)}, u32[]{:S(2)}) copy-start(s32[4,65536]{1,0:T(4,128)} %pixel_ref.1) | copy-start | bytes 3145732
  9.0 17.8 %copy-start.7 = (f32[4]{0:T(128)S(1)}, f32[4]{0:T(128)}, u32[]{:S(2)}) copy-start(f32[4]{0:T(128)} %knee_ref.1) | copy-start | bytes 52
  9.0 17.8 %copy-start.8 = (f32[4]{0:T(128)S(1)}, f32[4]{0:T(128)}, u32[]{:S(2)}) copy-start(f32[4]{0:T(128)} %white_ref.1) | copy-start | bytes 52
  9.0 6.8 %collective-permute-start.5 = (f32[16,64]{1,0:T(8,128)S(1)}, f32[16,64]{1,0:T(8,128)S(1)}, u32[]{:S(2)}, u32[]{:S(2)}) collective-permute-start(f32[16,64]{1,0:T(8,128)S(1)} %add.3.refs_0_), channel_id=1, source_target_pairs={{0,6},{1,7},{2,4},{3,5},{4,2},{5,3},{6,0},{7,1},{8,14},{9,15},{10,... | collective-permute-start | bytes 12296 | tf_op jit(solution)/shard_map/ppermute | solution.py:322
  14.1 4.5 %collective-permute-start.4 = (f32[16,64]{1,0:T(8,128)S(1)}, f32[16,64]{1,0:T(8,128)S(1)}, u32[]{:S(2)}, u32[]{:S(2)}) collective-permute-start(f32[16,64]{1,0:T(8,128)S(1)} %add.3.refs_0_), channel_id=1, source_target_pairs={{0,4},{1,5},{2,6},{3,7},{4,0},{5,1},{6,2},{7,3},{8,12},{9,13},{10,... | collective-permute-start | bytes 12296 | tf_op jit(solution)/shard_map/ppermute | solution.py:322
  14.1 4.5 %collective-permute-start.3 = (f32[16,64]{1,0:T(8,128)S(1)}, f32[16,64]{1,0:T(8,128)S(1)}, u32[]{:S(2)}, u32[]{:S(2)}) collective-permute-start(f32[16,64]{1,0:T(8,128)S(1)} %add.3.refs_0_), channel_id=1, source_target_pairs={{0,2},{1,3},{2,0},{3,1},{4,6},{5,7},{6,4},{7,5},{8,10},{9,11},{10,... | collective-permute-start | bytes 12296 | tf_op jit(solution)/shard_map/ppermute | solution.py:322
  22.4 16.9 %copy-start.9 = (s32[16]{0:T(128)S(1)}, s32[16]{0:T(128)}, u32[]{:S(2)}) copy-start(s32[16]{0:T(128)} %order_ref.3) | copy-start | bytes 196
  22.4 6.7 %collective-permute-start.6 = (f32[2,64,256]{2,1,0:T(8,128)S(1)}, f32[2,64,256]{2,1,0:T(8,128)S(1)}, u32[]{:S(2)}, u32[]{:S(2)}) collective-permute-start(f32[2,64,256]{2,1,0:T(8,128)S(1)} %get-tuple-element.56), channel_id=1, source_target_pairs={{0,2},{1,3},{2,0},{3,1},{4,6},{5,7},{6,4},{7,5},{8,10},{9,11},{10,... | collective-permute-start | bytes 393224 | tf_op jit(solution)/shard_map/ppermute | solution.py:322
  22.4 12.3 %collective-permute-start.7 = (f32[2,64,256]{2,1,0:T(8,128)S(1)}, f32[2,64,256]{2,1,0:T(8,128)S(1)}, u32[]{:S(2)}, u32[]{:S(2)}) collective-permute-start(f32[2,64,256]{2,1,0:T(8,128)S(1)} %get-tuple-element.57), channel_id=1, source_target_pairs={{0,4},{1,5},{2,6},{3,7},{4,0},{5,1},{6,2},{7,3},{8,12},{9,13},{10,... | collective-permute-start | bytes 393224 | tf_op jit(solution)/shard_map/ppermute | solution.py:322
  24.4 10.3 %collective-permute-start.8 = (f32[2,64,256]{2,1,0:T(8,128)S(1)}, f32[2,64,256]{2,1,0:T(8,128)S(1)}, u32[]{:S(2)}, u32[]{:S(2)}) collective-permute-start(f32[2,64,256]{2,1,0:T(8,128)S(1)} %get-tuple-element.58), channel_id=1, source_target_pairs={{0,6},{1,7},{2,4},{3,5},{4,2},{5,3},{6,0},{7,1},{8,14},{9,15},{10,... | collective-permute-start | bytes 393224 | tf_op jit(solution)/shard_map/ppermute | solution.py:322
  26.8 0.7 copy-start.5
  34.7 13.2 %collective-permute-start.9 = (f32[2,64,256]{2,1,0:T(8,128)S(1)}, f32[2,64,256]{2,1,0:T(8,128)S(1)}, u32[]{:S(2)}, u32[]{:S(2)}) collective-permute-start(f32[2,64,256]{2,1,0:T(8,128)S(1)} %get-tuple-element.76), channel_id=1, source_target_pairs={{0,2},{1,3},{2,0},{3,1},{4,6},{5,7},{6,4},{7,5},{8,10},{9,11},{10,... | collective-permute-start | bytes 393224 | tf_op jit(solution)/shard_map/ppermute | solution.py:322
  36.7 11.8 %collective-permute-start.10 = (f32[2,64,256]{2,1,0:T(8,128)S(1)}, f32[2,64,256]{2,1,0:T(8,128)S(1)}, u32[]{:S(2)}, u32[]{:S(2)}) collective-permute-start(f32[2,64,256]{2,1,0:T(8,128)S(1)} %get-tuple-element.77), channel_id=1, source_target_pairs={{0,4},{1,5},{2,6},{3,7},{4,0},{5,1},{6,2},{7,3},{8,12},{9,13},{10,... | collective-permute-start | bytes 393224 | tf_op jit(solution)/shard_map/ppermute | solution.py:322
  37.9 10.6 %collective-permute-start.11 = (f32[2,64,256]{2,1,0:T(8,128)S(1)}, f32[2,64,256]{2,1,0:T(8,128)S(1)}, u32[]{:S(2)}, u32[]{:S(2)}) collective-permute-start(f32[2,64,256]{2,1,0:T(8,128)S(1)} %get-tuple-element.78), channel_id=1, source_target_pairs={{0,6},{1,7},{2,4},{3,5},{4,2},{5,3},{6,0},{7,1},{8,14},{9,15},{10,... | collective-permute-start | bytes 393224 | tf_op jit(solution)/shard_map/ppermute | solution.py:322

commit v3 on v2

--- a/solution.py
+++ b/solution.py
@@ -112,15 +112,13 @@
     runs, run_len, local_dets, chunks, wafer_ref, data_ref, got_ref, wide_ref, temp_ref, *refs
 ):
     chips = data_ref.shape[0] // (2 * local_dets)
-    terms, refs = [ref[...] for ref in refs[:chips]], refs[chips:]
-    while len(terms) > 1:
-        terms = [a + b for a, b in zip(terms[0::2], terms[1::2])]
+    sums, refs = refs[0][...] + refs[1][...], refs[2:]
     amps_ref, out_refs, rows_ref = refs[0], refs[1:-1], refs[-1]
     modes = temp_ref.shape[1]
     row_count, time_local = data_ref.shape
     kept = row_count // 2
     pieces = time_local // COLS
-    amps = eliminate(terms[0], runs, run_len, modes)
+    amps = eliminate(sums, runs, run_len, modes)
     amps_ref[...] = jnp.concatenate(amps, axis=1)
     me = lax.axis_index("tm")
     core, chip = jnp.bitwise_and(me, 1), jnp.right_shift(me, 1)
@@ -292,14 +290,12 @@
         imag_v = real_u * turn_sin + imag_u * turn_cos
         imag_v = jnp.where(row_index == 0, zero_o[0:1], imag_v)
         result = dot3((l_h[...], l_l[...]), split2(jnp.concatenate([real_v, imag_v], axis=0)))
-        signal[...] = result
         for half_index in range(HALVES):
             cols = slice(half_index * LANES, (half_index + 1) * LANES)
             stacked[pl.ds(half_index * rows * dets + det, rows, stride=dets), :] = result[:, cols]
-        totals[...] += binned(high_ref[det], low_ref[det], result, inverse_ref[det], tall)
-
-    for turn in range(count):
-        one(turn)
+        return result
+
+    results = [one(turn) for turn in range(count)]
     if final:
         det_index = lax.broadcasted_iota(jnp.int32, (dets, LANES), 0)
         for lane in range(rows * HALVES):
@@ -308,6 +304,10 @@
             if first_det > 0:
                 here = jnp.where(det_index < first_det, before_ref[start : start + dets, :], here)
             out_ref[:, lane * LANES : (lane + 1) * LANES] = here.astype(bf16)
+    for turn, result in enumerate(results):
+        det = turn + first_det
+        totals[...] += binned(high_ref[det], low_ref[det], result, inverse_ref[det], tall)
+    if final:
         per_tile = PIX // LOW
         for tile in range(sky_ref.shape[0]):
             source = order_ref[tile] * per_tile
@@ -370,8 +370,10 @@
     if paired:
         wide = swap(wide[0], 1, "tm")
     if paired:
-        sums = sums + swap(sums, 1, "tm")
-        sums = [sums] + [swap(sums, step, "tm") for step in range(2, owners, 2)]
+        terms = [sums] + [swap(sums, step, "tm") for step in range(2, owners, 2)]
+        while len(terms) > 1:
+            terms = [a + b for a, b in zip(terms[0::2], terms[1::2])]
+        sums = [terms[0], swap(terms[0], 1, "tm")]
     else:
         sums = [lax.psum(sums, "tm")]
 
@@ -435,7 +437,9 @@
     )(knee_freq, white_level, fit_amps, table, tile_id, pixel_id)
 
     for chunk in range(1, chunks):
-        received, prepared = lax.optimization_barrier((received, prepared))
+        near = [received[chunk - 1][:-1], received[chunk], prepared]
+        near = lax.optimization_barrier(near)
+        received[chunk - 1][:-1], received[chunk], prepared = near
         for step in reversed(range(1, chips)):
             received[chunk][step] = swap(received[chunk][step], 2 * step, "tm")
 

time: 71.7 us -> 69.4 us (0.968)
  waiting for transfers between devices: 13 us -> 11.6 us
    ppermute x12, waiting for transfers between devices: 13 us -> 11.6 us  [swap(): return lax.ppermute(x, axis, [(i, i ^ step) for i in range(size)])]
    ppermute x12, starting transfers between devices: 15.7 us -> 15 us  [swap(): return lax.ppermute(x, axis, [(i, i ^ step) for i in range(size)])]
where the time goes in v3:
time: 69.4 us; the launch traced here: 69.1 us
  Pallas kernels  27 us (39%)
  starting transfers between devices  15 us (22%)
  blocking collectives  12.5 us (18%)
  waiting for transfers between devices  11.6 us (17%)
  local copies, waits for them, and re-layouts  1.39 us (2%)
  other arithmetic  0.78 us (1%)
  between operations  0.78 us (1%)
    pallas_call x2, Pallas kernels, shards(): pl.pallas_call(functools.partial(filter_kernel, parts, first_det, per_chu...  18 us
    ppermute x12, starting transfers between devices, swap(): return lax.ppermute(x, axis, [(i, i ^ step) for i in range(size)])  15 us
    all_to_all x1, blocking collectives, shards(): lax.all_to_all(spread, ('det', 'tm'), split_axis=0, concat_axis=0, tiled=...  12.5 us
    ppermute x12, waiting for transfers between devices, swap(): return lax.ppermute(x, axis, [(i, i ^ step) for i in range(size)])  11.6 us
    pallas_call x1, Pallas kernels, shards(): pl.pallas_call(functools.partial(fit_kernel, runs, run_len, paired), out_...  3.73 us
    pallas_call x1, Pallas kernels, shards(): pl.pallas_call(kernel, out_shape=[jax.ShapeDtypeStruct(shape, f32) for sh...  3.72 us
    pallas_call x1, Pallas kernels, shards(): pl.pallas_call(prepare_kernel, out_shape=pairs + [jax.ShapeDtypeStruct(sh...  1.56 us
  transfers between devices with their start and end apart: 12, of which 5 were waited for; matrix products, arithmetic and copies ran while one was open for 1% of the time, Pallas kernels for 14%

profile of v3, /device:TPU:0, one launch (start us, length us, event | category | flops | bytes accessed | tf_op | source)
XLA Modules:
  0.0 69.1 jit_solution(11094966041885615590)
XLA Ops:
  0.7 3.7 %fit_sums.1 = (f32[16,64]{1,0:T(8,128)}, f32[32,8192]{1,0:T(8,128)}) custom-call(s32[32]{0:T(128)} %wafer_ref.3, f32[32,8192]{1,0:T(8,128)} %data_ref.3, bf16[8,16,8192]{2,1,0:T(8,128)(2,1)} %temp_ref.1, bf16[8,16,8192]{2,1,0:T(8,128)(2,1)} %temp_ref.1), custom_call_target="tpu_custom_call" | custom-call | tf_op jit(solution)/shard_map/fit_sums/pallas_call | solution.py:356
  4.4 0.5 collective-permute-start.1
  4.8 0.1 collective-permute-start
  4.9 5.0 %collective-permute-start.4 = (f32[16,64]{1,0:T(8,128)}, f32[16,64]{1,0:T(8,128)S(1)}, u32[]{:S(2)}, u32[]{:S(2)}) collective-permute-start(f32[16,64]{1,0:T(8,128)} %get-tuple-element.52), channel_id=1, source_target_pairs={{0,6},{1,7},{2,4},{3,5},{4,2},{5,3},{6,0},{7,1},{8,14},{9,15},{10,... | collective-permute-start | bytes 12296 | tf_op jit(solution)/shard_map/ppermute | solution.py:322
  10.0 0.0 collective-permute-start.3
  10.0 0.6 collective-permute-start.2
  10.5 1.3 %collective-permute-done.4 = f32[16,64]{1,0:T(8,128)S(1)} collective-permute-done((f32[16,64]{1,0:T(8,128)}, f32[16,64]{1,0:T(8,128)S(1)}, u32[]{:S(2)}, u32[]{:S(2)}) %collective-permute-start.4) | collective-permute-done | bytes 4128 | tf_op jit(solution)/shard_map/ppermute | solution.py:322
  11.8 2.9 %collective-permute-done.3 = f32[16,64]{1,0:T(8,128)S(1)} collective-permute-done((f32[16,64]{1,0:T(8,128)}, f32[16,64]{1,0:T(8,128)S(1)}, u32[]{:S(2)}, u32[]{:S(2)}) %collective-permute-start.3) | collective-permute-done | bytes 4128 | tf_op jit(solution)/shard_map/ppermute | solution.py:322
  14.7 0.7 %add_add_fusion.refs_0_ = f32[16,64]{1,0:T(8,128)S(1)} fusion(f32[16,64]{1,0:T(8,128)S(1)} %collective-permute-done.3, f32[16,64]{1,0:T(8,128)S(1)} %collective-permute-done.4, f32[16,64]{1,0:T(8,128)} %get-tuple-element.52, f32[16,64]{1,0:T(8,128)S(1)} %collective-permute-done.2), kind=kLoop, calls=%fused_computation.1 | loop fusion | flops 3072 | bytes 20480 | tf_op jit(solution)/shard_map/add | solution.py:375
  15.4 0.0 copy-start.7
  15.4 0.0 copy-start.8
  15.5 0.1 collective-permute-start.5
  15.5 1.2 %collective-permute-done.5.refs_1_ = f32[16,64]{1,0:T(8,128)S(1)} collective-permute-done((f32[16,64]{1,0:T(8,128)S(1)}, f32[16,64]{1,0:T(8,128)S(1)}, u32[]{:S(2)}, u32[]{:S(2)}) %collective-permute-start.5) | collective-permute-done | bytes 4128 | tf_op jit(solution)/shard_map/ppermute | solution.py:322
  16.7 0.0 collective-permute-done.1.wide_ref
  16.7 0.0 collective-permute-done.got_ref
  16.7 3.7 %residual.1 = (f32[16,32]{1,0:T(8,128)}, f32[2,64,256]{2,1,0:T(8,128)S(1)}, f32[2,64,256]{2,1,0:T(8,128)S(1)}, f32[2,64,256]{2,1,0:T(8,128)S(1)}, f32[2,64,256]{...) custom-call(s32[32]{0:T(128)S(1)} %copy-done.6, ...), custom_call_target="tpu_custom_call" | custom-call | tf_op jit(solution)/shard_map/residual/pallas_call | solution.py:393
  20.4 2.0 %collective-permute-start.7 = (f32[2,64,256]{2,1,0:T(8,128)S(1)}, f32[2,64,256]{2,1,0:T(8,128)S(1)}, u32[]{:S(2)}, u32[]{:S(2)}) collective-permute-start(f32[2,64,256]{2,1,0:T(8,128)S(1)} %get-tuple-element.56), channel_id=1, source_target_pairs={{0,4},{1,5},{2,6},{3,7},{4,0},{5,1},{6,2},{7,3},{8,12},{9,13},{10,... | collective-permute-start | bytes 393224 | tf_op jit(solution)/shard_map/ppermute | solution.py:322
  22.5 2.3 %collective-permute-start.11 = (f32[2,64,256]{2,1,0:T(8,128)S(1)}, f32[2,64,256]{2,1,0:T(8,128)S(1)}, u32[]{:S(2)}, u32[]{:S(2)}) collective-permute-start(f32[2,64,256]{2,1,0:T(8,128)S(1)} %get-tuple-element.92), channel_id=1, source_target_pairs={{0,6},{1,7},{2,4},{3,5},{4,2},{5,3},{6,0},{7,1},{8,14},{9,15},{10,... | collective-permute-start | bytes 393224 | tf_op jit(solution)/shard_map/ppermute | solution.py:322
  24.9 0.0 copy-start.5
  24.9 0.7 copy-done.5
  25.6 1.6 %prepare.1 = (bf16[256,256]{1,0:T(8,128)(2,1)S(1)}, bf16[256,256]{1,0:T(8,128)(2,1)S(1)}, bf16[256,512]{1,0:T(8,128)(2,1)S(1)}, bf16[256,512]{1,0:T(8,128)(2,1)S...) custom-call(f32[4]{0:T(128)S(1)} %copy-done.7, ...), custom_call_target="tpu_custom_call" | custom-call | bytes 8388608 | tf_op jit(solution)/shard_map/prepare/pallas_call | solution.py:426
  27.1 1.6 %collective-permute-done.6.refs_1_ = f32[2,64,256]{2,1,0:T(8,128)S(1)} collective-permute-done((f32[2,64,256]{2,1,0:T(8,128)S(1)}, f32[2,64,256]{2,1,0:T(8,128)S(1)}, u32[]{:S(2)}, u32[]{:S(2)}) %collective-permute-start.6) | collective-permute-done | bytes 131104 | tf_op jit(solution)/shard_map/ppermute | solution.py:322
  28.7 4.6 %collective-permute-done.7.refs_2_ = f32[2,64,256]{2,1,0:T(8,128)S(1)} collective-permute-done((f32[2,64,256]{2,1,0:T(8,128)S(1)}, f32[2,64,256]{2,1,0:T(8,128)S(1)}, u32[]{:S(2)}, u32[]{:S(2)}) %collective-permute-start.7) | collective-permute-done | bytes 131104 | tf_op jit(solution)/shard_map/ppermute | solution.py:322
  33.3 0.3 collective-permute-start.8
  33.6 3.4 %collective-permute-start.9 = (f32[2,64,256]{2,1,0:T(8,128)S(1)}, f32[2,64,256]{2,1,0:T(8,128)S(1)}, u32[]{:S(2)}, u32[]{:S(2)}) collective-permute-start(f32[2,64,256]{2,1,0:T(8,128)S(1)} %get-tuple-element.75), channel_id=1, source_target_pairs={{0,4},{1,5},{2,6},{3,7},{4,0},{5,1},{6,2},{7,3},{8,12},{9,13},{10,... | collective-permute-start | bytes 393224 | tf_op jit(solution)/shard_map/ppermute | solution.py:322
  37.0 0.7 %collective-permute-start.10 = (f32[2,64,256]{2,1,0:T(8,128)S(1)}, f32[2,64,256]{2,1,0:T(8,128)S(1)}, u32[]{:S(2)}, u32[]{:S(2)}) collective-permute-start(f32[2,64,256]{2,1,0:T(8,128)S(1)} %get-tuple-element.76), channel_id=1, source_target_pairs={{0,6},{1,7},{2,4},{3,5},{4,2},{5,3},{6,0},{7,1},{8,14},{9,15},{10,... | collective-permute-start | bytes 393224 | tf_op jit(solution)/shard_map/ppermute | solution.py:322
  37.7 8.4 %filter_and_bin.2 = (f32[2048,128]{1,0:T(8,128)S(1)}, f32[64,64]{1,0:T(8,128)S(1)}) custom-call(s32[16]{0:T(128)S(1)} %copy-done.9, f32[2,64,256]{2,1,0:T(8,128)S(1)} %get-tuple-element.89.refs_0_, f32[2,64,256]{2,1,0:T(8,128)S(1)} %collective-permute-done.6.refs_1_, f32[2,64,256]{2,1,0:T(8,128)S(1)} %collective-permute-done.7.refs_2_, ...), custom_call_target="tpu_custom_call" | custom-call | flops 10485760000 | bytes 2097152 | tf_op jit(solution)/shard_map/filter_and_bin/pallas_call | solution.py:459
  46.1 9.6 %filter_and_bin.3 = (bf16[4,65536]{1,0:T(4,128)(2,1)}, f32[16,128]{1,0:T(8,128)S(1)}, f32[16,128]{1,0:T(8,128)S(1)}) custom-call(s32[16]{0:T(128)S(1)} %copy-done.9, f32[2,64,256]{2,1,0:T(8,128)S(1)} %get-tuple-element.73.refs_0_, f32[2,64,256]{2,1,0:T(8,128)S(1)} %collective-permute-done.8.refs_1_, f32[2,64,256]{2,1,0:T(8,128)S(1)} %collective-permute-done.9.refs_2_, ...), custom_call_target="tpu_custom_call" | custom-call | flops 10485760000 | bytes 2097152 | tf_op jit(solution)/shard_map/filter_and_bin/pallas_call | solution.py:459
  55.8 0.1 all_to_all.6
  55.9 12.5 %all_to_all.9 = f32[32,1,512]{2,1,0:T(1,128)S(1)} all-to-all(f32[32,1,512]{2,1,0:T(1,128)S(1)} %all_to_all.6), channel_id=1, replica_groups=mesh['det'=4,'tm'=8] {'det','tm'}, dimensions={0} | all-to-all | bytes 131072 | tf_op jit(solution)/shard_map/all_to_all | solution.py:480
  68.4 0.1 reduce_sum.9
  68.5 0.6 fusion
  (27 shorter events, 0.1 us)
Async XLA Ops:
  0.6 4.2 %copy-start.1 = (f32[32,8192]{1,0:T(8,128)S(1)}, f32[32,8192]{1,0:T(8,128)}, u32[]{:S(2)}) copy-start(f32[32,8192]{1,0:T(8,128)} %data_ref.3) | copy-start | bytes 3145732
  0.6 16.1 %copy-start.6 = (s32[32]{0:T(128)S(1)}, s32[32]{0:T(128)}, u32[]{:S(2)}) copy-start(s32[32]{0:T(128)} %wafer_ref.3) | copy-start | bytes 388
  0.7 16.1 %copy-start = (bf16[8,16,8192]{2,1,0:T(8,128)(2,1)S(1)}, bf16[8,16,8192]{2,1,0:T(8,128)(2,1)}, u32[]{:S(2)}) copy-start(bf16[8,16,8192]{2,1,0:T(8,128)(2,1)} %temp_ref.1) | copy-start | bytes 6291460
  4.4 12.3 %collective-permute-start.1 = (f32[32,8192]{1,0:T(8,128)}, f32[32,8192]{1,0:T(8,128)S(1)}, u32[]{:S(2)}, u32[]{:S(2)}) collective-permute-start(f32[32,8192]{1,0:T(8,128)} %get-tuple-element.51), channel_id=1, source_target_pairs={{0,1},{1,0},{2,3},{3,2},{4,5},{5,4},{6,7},{7,6},{8,9},{9,8},{10,11... | collective-permute-start | bytes 3145736 | tf_op jit(solution)/shard_map/ppermute | solution.py:322
  4.8 11.9 %collective-permute-start = (f32[32,8192]{1,0:T(8,128)S(1)}, f32[32,8192]{1,0:T(8,128)S(1)}, u32[]{:S(2)}, u32[]{:S(2)}) collective-permute-start(f32[32,8192]{1,0:T(8,128)S(1)} %copy-done.1), channel_id=1, source_target_pairs={{0,1},{1,0},{2,3},{3,2},{4,5},{5,4},{6,7},{7,6},{8,9},{9,8},{10,11... | collective-permute-start | bytes 3145736 | tf_op jit(solution)/shard_map/ppermute | solution.py:322
  4.9 6.9 %collective-permute-start.4 = (f32[16,64]{1,0:T(8,128)}, f32[16,64]{1,0:T(8,128)S(1)}, u32[]{:S(2)}, u32[]{:S(2)}) collective-permute-start(f32[16,64]{1,0:T(8,128)} %get-tuple-element.52), channel_id=1, source_target_pairs={{0,6},{1,7},{2,4},{3,5},{4,2},{5,3},{6,0},{7,1},{8,14},{9,15},{10,... | collective-permute-start | bytes 12296 | tf_op jit(solution)/shard_map/ppermute | solution.py:322
  10.0 4.8 %collective-permute-start.3 = (f32[16,64]{1,0:T(8,128)}, f32[16,64]{1,0:T(8,128)S(1)}, u32[]{:S(2)}, u32[]{:S(2)}) collective-permute-start(f32[16,64]{1,0:T(8,128)} %get-tuple-element.52), channel_id=1, source_target_pairs={{0,4},{1,5},{2,6},{3,7},{4,0},{5,1},{6,2},{7,3},{8,12},{9,13},{10,... | collective-permute-start | bytes 12296 | tf_op jit(solution)/shard_map/ppermute | solution.py:322
  10.0 4.8 %collective-permute-start.2 = (f32[16,64]{1,0:T(8,128)}, f32[16,64]{1,0:T(8,128)S(1)}, u32[]{:S(2)}, u32[]{:S(2)}) collective-permute-start(f32[16,64]{1,0:T(8,128)} %get-tuple-element.52), channel_id=1, source_target_pairs={{0,2},{1,3},{2,0},{3,1},{4,6},{5,7},{6,4},{7,5},{8,10},{9,11},{10,... | collective-permute-start | bytes 12296 | tf_op jit(solution)/shard_map/ppermute | solution.py:322
  15.4 9.4 %copy-start.2 = (f32[1424,256]{1,0:T(8,128)S(1)}, f32[1424,256]{1,0:T(8,128)}, u32[]{:S(2)}) copy-start(f32[1424,256]{1,0:T(8,128)} %constant.6.clone.table_ref) | copy-start | bytes 4374532
  15.4 9.4 %copy-start.3 = (s32[4,65536]{1,0:T(4,128)S(1)}, s32[4,65536]{1,0:T(4,128)}, u32[]{:S(2)}) copy-start(s32[4,65536]{1,0:T(4,128)} %tile_ref.1) | copy-start | bytes 3145732
  15.4 9.4 %copy-start.4 = (s32[4,65536]{1,0:T(4,128)S(1)}, s32[4,65536]{1,0:T(4,128)}, u32[]{:S(2)}) copy-start(s32[4,65536]{1,0:T(4,128)} %pixel_ref.1) | copy-start | bytes 3145732
  15.4 9.4 %copy-start.7 = (f32[4]{0:T(128)S(1)}, f32[4]{0:T(128)}, u32[]{:S(2)}) copy-start(f32[4]{0:T(128)} %knee_ref.1) | copy-start | bytes 52
  15.4 9.4 %copy-start.8 = (f32[4]{0:T(128)S(1)}, f32[4]{0:T(128)}, u32[]{:S(2)}) copy-start(f32[4]{0:T(128)} %white_ref.1) | copy-start | bytes 52
  15.5 1.2 %collective-permute-start.5 = (f32[16,64]{1,0:T(8,128)S(1)}, f32[16,64]{1,0:T(8,128)S(1)}, u32[]{:S(2)}, u32[]{:S(2)}) collective-permute-start(f32[16,64]{1,0:T(8,128)S(1)} %add_add_fusion.refs_0_), channel_id=1, source_target_pairs={{0,1},{1,0},{2,3},{3,2},{4,5},{5,4},{6,7},{7,6},{8,9},{9,8},{10,11... | collective-permute-start | bytes 12296 | tf_op jit(solution)/shard_map/ppermute | solution.py:322
  20.4 17.3 %copy-start.9 = (s32[16]{0:T(128)S(1)}, s32[16]{0:T(128)}, u32[]{:S(2)}) copy-start(s32[16]{0:T(128)} %order_ref.3) | copy-start | bytes 196
  20.4 8.3 %collective-permute-start.6 = (f32[2,64,256]{2,1,0:T(8,128)S(1)}, f32[2,64,256]{2,1,0:T(8,128)S(1)}, u32[]{:S(2)}, u32[]{:S(2)}) collective-permute-start(f32[2,64,256]{2,1,0:T(8,128)S(1)} %get-tuple-element.55), channel_id=1, source_target_pairs={{0,2},{1,3},{2,0},{3,1},{4,6},{5,7},{6,4},{7,5},{8,10},{9,11},{10,... | collective-permute-start | bytes 393224 | tf_op jit(solution)/shard_map/ppermute | solution.py:322
  20.4 12.9 %collective-permute-start.7 = (f32[2,64,256]{2,1,0:T(8,128)S(1)}, f32[2,64,256]{2,1,0:T(8,128)S(1)}, u32[]{:S(2)}, u32[]{:S(2)}) collective-permute-start(f32[2,64,256]{2,1,0:T(8,128)S(1)} %get-tuple-element.56), channel_id=1, source_target_pairs={{0,4},{1,5},{2,6},{3,7},{4,0},{5,1},{6,2},{7,3},{8,12},{9,13},{10,... | collective-permute-start | bytes 393224 | tf_op jit(solution)/shard_map/ppermute | solution.py:322
  22.5 15.2 %collective-permute-start.11 = (f32[2,64,256]{2,1,0:T(8,128)S(1)}, f32[2,64,256]{2,1,0:T(8,128)S(1)}, u32[]{:S(2)}, u32[]{:S(2)}) collective-permute-start(f32[2,64,256]{2,1,0:T(8,128)S(1)} %get-tuple-element.92), channel_id=1, source_target_pairs={{0,6},{1,7},{2,4},{3,5},{4,2},{5,3},{6,0},{7,1},{8,14},{9,15},{10,... | collective-permute-start | bytes 393224 | tf_op jit(solution)/shard_map/ppermute | solution.py:322
  24.9 0.7 %copy-start.5 = (f32[16,32]{1,0:T(8,128)S(1)}, f32[16,32]{1,0:T(8,128)}, u32[]{:S(2)}) copy-start(f32[16,32]{1,0:T(8,128)} %get-tuple-element.47.after_ref) | copy-start | bytes 6148
  33.3 12.8 %collective-permute-start.8 = (f32[2,64,256]{2,1,0:T(8,128)S(1)}, f32[2,64,256]{2,1,0:T(8,128)S(1)}, u32[]{:S(2)}, u32[]{:S(2)}) collective-permute-start(f32[2,64,256]{2,1,0:T(8,128)S(1)} %get-tuple-element.74), channel_id=1, source_target_pairs={{0,2},{1,3},{2,0},{3,1},{4,6},{5,7},{6,4},{7,5},{8,10},{9,11},{10,... | collective-permute-start | bytes 393224 | tf_op jit(solution)/shard_map/ppermute | solution.py:322
  33.6 12.5 %collective-permute-start.9 = (f32[2,64,256]{2,1,0:T(8,128)S(1)}, f32[2,64,256]{2,1,0:T(8,128)S(1)}, u32[]{:S(2)}, u32[]{:S(2)}) collective-permute-start(f32[2,64,256]{2,1,0:T(8,128)S(1)} %get-tuple-element.75), channel_id=1, source_target_pairs={{0,4},{1,5},{2,6},{3,7},{4,0},{5,1},{6,2},{7,3},{8,12},{9,13},{10,... | collective-permute-start | bytes 393224 | tf_op jit(solution)/shard_map/ppermute | solution.py:322
  37.0 9.1 %collective-permute-start.10 = (f32[2,64,256]{2,1,0:T(8,128)S(1)}, f32[2,64,256]{2,1,0:T(8,128)S(1)}, u32[]{:S(2)}, u32[]{:S(2)}) collective-permute-start(f32[2,64,256]{2,1,0:T(8,128)S(1)} %get-tuple-element.76), channel_id=1, source_target_pairs={{0,6},{1,7},{2,4},{3,5},{4,2},{5,3},{6,0},{7,1},{8,14},{9,15},{10,... | collective-permute-start | bytes 393224 | tf_op jit(solution)/shard_map/ppermute | solution.py:322

commit v4 on v3

--- a/solution.py
+++ b/solution.py
@@ -257,45 +257,56 @@
     row_index = lax.broadcasted_iota(jnp.int32, (half, COLS), 0)
     chip = jnp.right_shift(lax.axis_index("tm"), 1)
 
-    def one(turn):
-        det = turn + first_det
+    turn_cos, turn_sin = tc_ref[...], ts_ref[...]
+    side = (s_h[...], s_l[...])
+    turns = range(count)
+    slabs = []
+    for turn in turns:
         for part in range(parts):
             height = part_refs[part].shape[1]
             start = 0
             if parts > 1:
                 start = pl.multiple_of(jnp.bitwise_xor(chip, part) * height, height)
-            signal[pl.ds(start, height), :] = part_refs[part][turn]
-        turn_cos, turn_sin = tc_ref[...], ts_ref[...]
-        side = (s_h[...], s_l[...])
-        first = dot3((f_h[...], f_l[...]), split2(signal[...]))
-        real_y, low_y = first[:half], first[half:]
+            signal[pl.ds(start, height), turn * COLS : (turn + 1) * COLS] = part_refs[part][turn]
+    first = dot3((f_h[...], f_l[...]), split2(signal[...]))
+    for turn in turns:
+        cols = slice(turn * COLS, (turn + 1) * COLS)
+        real_y, low_y = first[:half, cols], first[half:, cols]
         imag_y = jnp.where(row_index == 0, 0.0, low_y)
-        zero_y = jnp.broadcast_to(low_y[0:1], (16, COLS))
-        real_z = real_y * turn_cos + imag_y * turn_sin
-        imag_z = imag_y * turn_cos - real_y * turn_sin
-        forward = dot3(split2(jnp.concatenate([real_z, imag_z, zero_y], axis=0)), side)
-        cos_f, sin_f = forward[:, :COLS], forward[:, COLS:]
-        gain = gain_ref[det]
+        slabs.append(real_y * turn_cos + imag_y * turn_sin)
+        slabs.append(imag_y * turn_cos - real_y * turn_sin)
+        slabs.append(jnp.broadcast_to(low_y[0:1], (16, COLS)))
+    forward = dot3(split2(jnp.concatenate(slabs, axis=0)), side)
+    height = 2 * half + 16
+    slabs = []
+    for turn in turns:
+        cos_f = forward[turn * height : (turn + 1) * height, :COLS]
+        sin_f = forward[turn * height : (turn + 1) * height, COLS:]
+        gain = gain_ref[turn + first_det]
         gain_main, gain_zero = gain[:half], gain[half:]
-        real_x = (cos_f[:half] + sin_f[half : 2 * half]) * gain_main
-        imag_x = (cos_f[half : 2 * half] - sin_f[:half]) * gain_main
-        zero_r = cos_f[2 * half :] * gain_zero
-        zero_i = -sin_f[2 * half :] * gain_zero
-        back = dot3(split2(jnp.concatenate([real_x, imag_x, zero_r, zero_i], axis=0)), side)
-        cos_b, sin_b = back[:, :COLS], back[:, COLS:]
+        slabs.append((cos_f[:half] + sin_f[half : 2 * half]) * gain_main)
+        slabs.append((cos_f[half : 2 * half] - sin_f[:half]) * gain_main)
+        slabs.append(cos_f[2 * half :] * gain_zero)
+        slabs.append(-sin_f[2 * half :] * gain_zero)
+    back = dot3(split2(jnp.concatenate(slabs, axis=0)), side)
+    height = 2 * half + 32
+    slabs = []
+    for turn in turns:
+        cos_b = back[turn * height : (turn + 1) * height, :COLS]
+        sin_b = back[turn * height : (turn + 1) * height, COLS:]
         real_u = cos_b[:half] - sin_b[half : 2 * half]
         imag_u = sin_b[:half] + cos_b[half : 2 * half]
         zero_o = cos_b[2 * half : 2 * half + 16] - sin_b[2 * half + 16 :]
-        real_v = real_u * turn_cos - imag_u * turn_sin
         imag_v = real_u * turn_sin + imag_u * turn_cos
         imag_v = jnp.where(row_index == 0, zero_o[0:1], imag_v)
-        result = dot3((l_h[...], l_l[...]), split2(jnp.concatenate([real_v, imag_v], axis=0)))
+        slabs.append(jnp.concatenate([real_u * turn_cos - imag_u * turn_sin, imag_v], axis=0))
+    result = dot3((l_h[...], l_l[...]), split2(jnp.concatenate(slabs, axis=1)))
+    results = [result[:, turn * COLS : (turn + 1) * COLS] for turn in turns]
+    for turn in turns:
         for half_index in range(HALVES):
             cols = slice(half_index * LANES, (half_index + 1) * LANES)
-            stacked[pl.ds(half_index * rows * dets + det, rows, stride=dets), :] = result[:, cols]
-        return result
-
-    results = [one(turn) for turn in range(count)]
+            start = half_index * rows * dets + first_det + turn
+            stacked[pl.ds(start, rows, stride=dets), :] = results[turn][:, cols]
     if final:
         det_index = lax.broadcasted_iota(jnp.int32, (dets, LANES), 0)
         for lane in range(rows * HALVES):
@@ -451,10 +462,10 @@
         parts = len(received[chunk])
         if final:
             outs = [((local_dets, full_length), bf16)] + [((tile_count, PIX), f32)] * 2
-            scratch = [pltpu.VMEM(s, f32) for s in ((rows, COLS), stacked_shape, (2 * tall, LOW))]
+            scratch = [pltpu.VMEM(s, f32) for s in ((rows, per_chunk * COLS), stacked_shape, (2 * tall, LOW))]
         else:
             outs = [(stacked_shape, f32), ((2 * tall, LOW), f32)]
-            scratch = [pltpu.VMEM((rows, COLS), f32)]
+            scratch = [pltpu.VMEM((rows, per_chunk * COLS), f32)]
         operands = [*received[chunk], *prepared, *carried]
         carried = pl.pallas_call(
             functools.partial(filter_kernel, parts, first_det, per_chunk, local_dets, final),

time: 69.4 us -> 68.5 us (0.987)
  Pallas kernels: 27 us -> 25.6 us
    pallas_call x2, Pallas kernels: 18 us -> 16.6 us  [shards(): pl.pallas_call(functools.partial(filter_kernel, parts, first_det, per_chu...]
  transfers between devices with their start and end apart: 12 -> 12, of which waited for: 5 -> 6; matrix products, arithmetic and copies ran while one was open for 1% -> 1% of each run, Pallas kernels for 14% -> 14%
where the time goes in v4:
time: 68.5 us; the launch traced here: 68.2 us
  Pallas kernels  25.6 us (37%)
  starting transfers between devices  15 us (22%)
  blocking collectives  12.4 us (18%)
  waiting for transfers between devices  12.2 us (18%)
  local copies, waits for them, and re-layouts  1.39 us (2%)
  other arithmetic  0.78 us (1%)
  between operations  0.76 us (1%)
    pallas_call x2, Pallas kernels, shards(): pl.pallas_call(functools.partial(filter_kernel, parts, first_det, per_chu...  16.6 us
    ppermute x12, starting transfers between devices, swap(): return lax.ppermute(x, axis, [(i, i ^ step) for i in range(size)])  15 us
    all_to_all x1, blocking collectives, shards(): lax.all_to_all(spread, ('det', 'tm'), split_axis=0, concat_axis=0, tiled=...  12.4 us
    ppermute x12, waiting for transfers between devices, swap(): return lax.ppermute(x, axis, [(i, i ^ step) for i in range(size)])  12.2 us
    pallas_call x1, Pallas kernels, shards(): pl.pallas_call(functools.partial(fit_kernel, runs, run_len, paired), out_...  3.73 us
    pallas_call x1, Pallas kernels, shards(): pl.pallas_call(kernel, out_shape=[jax.ShapeDtypeStruct(shape, f32) for sh...  3.72 us
    pallas_call x1, Pallas kernels, shards(): pl.pallas_call(prepare_kernel, out_shape=pairs + [jax.ShapeDtypeStruct(sh...  1.56 us
  transfers between devices with their start and end apart: 12, of which 6 were waited for; matrix products, arithmetic and copies ran while one was open for 1% of the time, Pallas kernels for 14%

profile of v4, /device:TPU:0, one launch (start us, length us, event | category | flops | bytes accessed | tf_op | source)
XLA Modules:
  0.0 68.2 jit_solution(13736726464115750142)
XLA Ops:
  0.7 3.7 %fit_sums.1 = (f32[16,64]{1,0:T(8,128)}, f32[32,8192]{1,0:T(8,128)}) custom-call(s32[32]{0:T(128)} %wafer_ref.3, f32[32,8192]{1,0:T(8,128)} %data_ref.3, bf16[8,16,8192]{2,1,0:T(8,128)(2,1)} %temp_ref.1, bf16[8,16,8192]{2,1,0:T(8,128)(2,1)} %temp_ref.1), custom_call_target="tpu_custom_call" | custom-call | tf_op jit(solution)/shard_map/fit_sums/pallas_call | solution.py:367
  4.4 0.5 collective-permute-start.1
  4.8 0.1 collective-permute-start
  4.9 5.0 %collective-permute-start.4 = (f32[16,64]{1,0:T(8,128)}, f32[16,64]{1,0:T(8,128)S(1)}, u32[]{:S(2)}, u32[]{:S(2)}) collective-permute-start(f32[16,64]{1,0:T(8,128)} %get-tuple-element.52), channel_id=1, source_target_pairs={{0,6},{1,7},{2,4},{3,5},{4,2},{5,3},{6,0},{7,1},{8,14},{9,15},{10,... | collective-permute-start | bytes 12296 | tf_op jit(solution)/shard_map/ppermute | solution.py:333
  10.0 0.0 collective-permute-start.3
  10.0 0.6 collective-permute-start.2
  10.5 1.3 %collective-permute-done.4 = f32[16,64]{1,0:T(8,128)S(1)} collective-permute-done((f32[16,64]{1,0:T(8,128)}, f32[16,64]{1,0:T(8,128)S(1)}, u32[]{:S(2)}, u32[]{:S(2)}) %collective-permute-start.4) | collective-permute-done | bytes 4128 | tf_op jit(solution)/shard_map/ppermute | solution.py:333
  11.8 2.9 %collective-permute-done.3 = f32[16,64]{1,0:T(8,128)S(1)} collective-permute-done((f32[16,64]{1,0:T(8,128)}, f32[16,64]{1,0:T(8,128)S(1)}, u32[]{:S(2)}, u32[]{:S(2)}) %collective-permute-start.3) | collective-permute-done | bytes 4128 | tf_op jit(solution)/shard_map/ppermute | solution.py:333
  14.7 0.7 %add_add_fusion.refs_0_ = f32[16,64]{1,0:T(8,128)S(1)} fusion(f32[16,64]{1,0:T(8,128)S(1)} %collective-permute-done.3, f32[16,64]{1,0:T(8,128)S(1)} %collective-permute-done.4, f32[16,64]{1,0:T(8,128)} %get-tuple-element.52, f32[16,64]{1,0:T(8,128)S(1)} %collective-permute-done.2), kind=kLoop, calls=%fused_computation.1 | loop fusion | flops 3072 | bytes 20480 | tf_op jit(solution)/shard_map/add | solution.py:386
  15.4 0.0 copy-start.7
  15.4 0.0 copy-start.8
  15.5 0.1 collective-permute-start.5
  15.5 1.2 %collective-permute-done.5.refs_1_ = f32[16,64]{1,0:T(8,128)S(1)} collective-permute-done((f32[16,64]{1,0:T(8,128)S(1)}, f32[16,64]{1,0:T(8,128)S(1)}, u32[]{:S(2)}, u32[]{:S(2)}) %collective-permute-start.5) | collective-permute-done | bytes 4128 | tf_op jit(solution)/shard_map/ppermute | solution.py:333
  16.7 0.0 collective-permute-done.1.wide_ref
  16.7 3.7 %residual.1 = (f32[16,32]{1,0:T(8,128)}, f32[2,64,256]{2,1,0:T(8,128)S(1)}, f32[2,64,256]{2,1,0:T(8,128)S(1)}, f32[2,64,256]{2,1,0:T(8,128)S(1)}, f32[2,64,256]{...) custom-call(s32[32]{0:T(128)S(1)} %copy-done.6, ...), custom_call_target="tpu_custom_call" | custom-call | tf_op jit(solution)/shard_map/residual/pallas_call | solution.py:404
  20.4 2.0 %collective-permute-start.7 = (f32[2,64,256]{2,1,0:T(8,128)S(1)}, f32[2,64,256]{2,1,0:T(8,128)S(1)}, u32[]{:S(2)}, u32[]{:S(2)}) collective-permute-start(f32[2,64,256]{2,1,0:T(8,128)S(1)} %get-tuple-element.56), channel_id=1, source_target_pairs={{0,4},{1,5},{2,6},{3,7},{4,0},{5,1},{6,2},{7,3},{8,12},{9,13},{10,... | collective-permute-start | bytes 393224 | tf_op jit(solution)/shard_map/ppermute | solution.py:333
  22.5 2.3 %collective-permute-start.11 = (f32[2,64,256]{2,1,0:T(8,128)S(1)}, f32[2,64,256]{2,1,0:T(8,128)S(1)}, u32[]{:S(2)}, u32[]{:S(2)}) collective-permute-start(f32[2,64,256]{2,1,0:T(8,128)S(1)} %get-tuple-element.92), channel_id=1, source_target_pairs={{0,6},{1,7},{2,4},{3,5},{4,2},{5,3},{6,0},{7,1},{8,14},{9,15},{10,... | collective-permute-start | bytes 393224 | tf_op jit(solution)/shard_map/ppermute | solution.py:333
  24.9 0.0 copy-start.5
  24.9 0.7 %copy-done.5 = f32[16,32]{1,0:T(8,128)S(1)} copy-done((f32[16,32]{1,0:T(8,128)S(1)}, f32[16,32]{1,0:T(8,128)}, u32[]{:S(2)}) %copy-start.5) | copy-done | bytes 2072
  25.6 1.6 %prepare.1 = (bf16[256,256]{1,0:T(8,128)(2,1)S(1)}, bf16[256,256]{1,0:T(8,128)(2,1)S(1)}, bf16[256,512]{1,0:T(8,128)(2,1)S(1)}, bf16[256,512]{1,0:T(8,128)(2,1)S...) custom-call(f32[4]{0:T(128)S(1)} %copy-done.7, ...), custom_call_target="tpu_custom_call" | custom-call | bytes 8388608 | tf_op jit(solution)/shard_map/prepare/pallas_call | solution.py:437
  27.1 1.6 %collective-permute-done.6.refs_1_ = f32[2,64,256]{2,1,0:T(8,128)S(1)} collective-permute-done((f32[2,64,256]{2,1,0:T(8,128)S(1)}, f32[2,64,256]{2,1,0:T(8,128)S(1)}, u32[]{:S(2)}, u32[]{:S(2)}) %collective-permute-start.6) | collective-permute-done | bytes 131104 | tf_op jit(solution)/shard_map/ppermute | solution.py:333
  28.7 4.6 %collective-permute-done.7.refs_2_ = f32[2,64,256]{2,1,0:T(8,128)S(1)} collective-permute-done((f32[2,64,256]{2,1,0:T(8,128)S(1)}, f32[2,64,256]{2,1,0:T(8,128)S(1)}, u32[]{:S(2)}, u32[]{:S(2)}) %collective-permute-start.7) | collective-permute-done | bytes 131104 | tf_op jit(solution)/shard_map/ppermute | solution.py:333
  33.3 0.3 collective-permute-start.8
  33.6 3.4 %collective-permute-start.9 = (f32[2,64,256]{2,1,0:T(8,128)S(1)}, f32[2,64,256]{2,1,0:T(8,128)S(1)}, u32[]{:S(2)}, u32[]{:S(2)}) collective-permute-start(f32[2,64,256]{2,1,0:T(8,128)S(1)} %get-tuple-element.75), channel_id=1, source_target_pairs={{0,4},{1,5},{2,6},{3,7},{4,0},{5,1},{6,2},{7,3},{8,12},{9,13},{10,... | collective-permute-start | bytes 393224 | tf_op jit(solution)/shard_map/ppermute | solution.py:333
  37.0 0.7 %collective-permute-start.10 = (f32[2,64,256]{2,1,0:T(8,128)S(1)}, f32[2,64,256]{2,1,0:T(8,128)S(1)}, u32[]{:S(2)}, u32[]{:S(2)}) collective-permute-start(f32[2,64,256]{2,1,0:T(8,128)S(1)} %get-tuple-element.76), channel_id=1, source_target_pairs={{0,6},{1,7},{2,4},{3,5},{4,2},{5,3},{6,0},{7,1},{8,14},{9,15},{10,... | collective-permute-start | bytes 393224 | tf_op jit(solution)/shard_map/ppermute | solution.py:333
  37.7 7.7 %filter_and_bin.2 = (f32[2048,128]{1,0:T(8,128)S(1)}, f32[64,64]{1,0:T(8,128)S(1)}) custom-call(s32[16]{0:T(128)S(1)} %copy-done.9, f32[2,64,256]{2,1,0:T(8,128)S(1)} %get-tuple-element.89.refs_0_, f32[2,64,256]{2,1,0:T(8,128)S(1)} %collective-permute-done.6.refs_1_, f32[2,64,256]{2,1,0:T(8,128)S(1)} %collective-permute-done.7.refs_2_, ...), custom_call_target="tpu_custom_call" | custom-call | flops 10485760000 | bytes 2097152 | tf_op jit(solution)/shard_map/filter_and_bin/pallas_call | solution.py:470
  45.4 0.6 collective-permute-done.9.refs_2_
  46.1 8.9 %filter_and_bin.3 = (bf16[4,65536]{1,0:T(4,128)(2,1)}, f32[16,128]{1,0:T(8,128)S(1)}, f32[16,128]{1,0:T(8,128)S(1)}) custom-call(s32[16]{0:T(128)S(1)} %copy-done.9, f32[2,64,256]{2,1,0:T(8,128)S(1)} %get-tuple-element.73.refs_0_, f32[2,64,256]{2,1,0:T(8,128)S(1)} %collective-permute-done.8.refs_1_, f32[2,64,256]{2,1,0:T(8,128)S(1)} %collective-permute-done.9.refs_2_, ...), custom_call_target="tpu_custom_call" | custom-call | flops 10485760000 | bytes 2097152 | tf_op jit(solution)/shard_map/filter_and_bin/pallas_call | solution.py:470
  55.0 0.1 all_to_all.6
  55.1 12.4 %all_to_all.9 = f32[32,1,512]{2,1,0:T(1,128)S(1)} all-to-all(f32[32,1,512]{2,1,0:T(1,128)S(1)} %all_to_all.6), channel_id=1, replica_groups=mesh['det'=4,'tm'=8] {'det','tm'}, dimensions={0} | all-to-all | bytes 131072 | tf_op jit(solution)/shard_map/all_to_all | solution.py:491
  67.5 0.1 reduce_sum.9
  67.6 0.6 fusion
  (27 shorter events, 0.1 us)
Async XLA Ops:
  0.6 4.2 %copy-start.1 = (f32[32,8192]{1,0:T(8,128)S(1)}, f32[32,8192]{1,0:T(8,128)}, u32[]{:S(2)}) copy-start(f32[32,8192]{1,0:T(8,128)} %data_ref.3) | copy-start | bytes 3145732
  0.6 16.1 %copy-start.6 = (s32[32]{0:T(128)S(1)}, s32[32]{0:T(128)}, u32[]{:S(2)}) copy-start(s32[32]{0:T(128)} %wafer_ref.3) | copy-start | bytes 388
  0.7 16.1 %copy-start = (bf16[8,16,8192]{2,1,0:T(8,128)(2,1)S(1)}, bf16[8,16,8192]{2,1,0:T(8,128)(2,1)}, u32[]{:S(2)}) copy-start(bf16[8,16,8192]{2,1,0:T(8,128)(2,1)} %temp_ref.1) | copy-start | bytes 6291460
  4.4 12.3 %collective-permute-start.1 = (f32[32,8192]{1,0:T(8,128)}, f32[32,8192]{1,0:T(8,128)S(1)}, u32[]{:S(2)}, u32[]{:S(2)}) collective-permute-start(f32[32,8192]{1,0:T(8,128)} %get-tuple-element.51), channel_id=1, source_target_pairs={{0,1},{1,0},{2,3},{3,2},{4,5},{5,4},{6,7},{7,6},{8,9},{9,8},{10,11... | collective-permute-start | bytes 3145736 | tf_op jit(solution)/shard_map/ppermute | solution.py:333
  4.8 11.9 %collective-permute-start = (f32[32,8192]{1,0:T(8,128)S(1)}, f32[32,8192]{1,0:T(8,128)S(1)}, u32[]{:S(2)}, u32[]{:S(2)}) collective-permute-start(f32[32,8192]{1,0:T(8,128)S(1)} %copy-done.1), channel_id=1, source_target_pairs={{0,1},{1,0},{2,3},{3,2},{4,5},{5,4},{6,7},{7,6},{8,9},{9,8},{10,11... | collective-permute-start | bytes 3145736 | tf_op jit(solution)/shard_map/ppermute | solution.py:333
  4.9 6.9 %collective-permute-start.4 = (f32[16,64]{1,0:T(8,128)}, f32[16,64]{1,0:T(8,128)S(1)}, u32[]{:S(2)}, u32[]{:S(2)}) collective-permute-start(f32[16,64]{1,0:T(8,128)} %get-tuple-element.52), channel_id=1, source_target_pairs={{0,6},{1,7},{2,4},{3,5},{4,2},{5,3},{6,0},{7,1},{8,14},{9,15},{10,... | collective-permute-start | bytes 12296 | tf_op jit(solution)/shard_map/ppermute | solution.py:333
  10.0 4.8 %collective-permute-start.3 = (f32[16,64]{1,0:T(8,128)}, f32[16,64]{1,0:T(8,128)S(1)}, u32[]{:S(2)}, u32[]{:S(2)}) collective-permute-start(f32[16,64]{1,0:T(8,128)} %get-tuple-element.52), channel_id=1, source_target_pairs={{0,4},{1,5},{2,6},{3,7},{4,0},{5,1},{6,2},{7,3},{8,12},{9,13},{10,... | collective-permute-start | bytes 12296 | tf_op jit(solution)/shard_map/ppermute | solution.py:333
  10.0 4.8 %collective-permute-start.2 = (f32[16,64]{1,0:T(8,128)}, f32[16,64]{1,0:T(8,128)S(1)}, u32[]{:S(2)}, u32[]{:S(2)}) collective-permute-start(f32[16,64]{1,0:T(8,128)} %get-tuple-element.52), channel_id=1, source_target_pairs={{0,2},{1,3},{2,0},{3,1},{4,6},{5,7},{6,4},{7,5},{8,10},{9,11},{10,... | collective-permute-start | bytes 12296 | tf_op jit(solution)/shard_map/ppermute | solution.py:333
  15.4 9.4 %copy-start.2 = (f32[1424,256]{1,0:T(8,128)S(1)}, f32[1424,256]{1,0:T(8,128)}, u32[]{:S(2)}) copy-start(f32[1424,256]{1,0:T(8,128)} %constant.6.clone.table_ref) | copy-start | bytes 4374532
  15.4 9.4 %copy-start.3 = (s32[4,65536]{1,0:T(4,128)S(1)}, s32[4,65536]{1,0:T(4,128)}, u32[]{:S(2)}) copy-start(s32[4,65536]{1,0:T(4,128)} %tile_ref.1) | copy-start | bytes 3145732
  15.4 9.4 %copy-start.4 = (s32[4,65536]{1,0:T(4,128)S(1)}, s32[4,65536]{1,0:T(4,128)}, u32[]{:S(2)}) copy-start(s32[4,65536]{1,0:T(4,128)} %pixel_ref.1) | copy-start | bytes 3145732
  15.4 9.4 %copy-start.7 = (f32[4]{0:T(128)S(1)}, f32[4]{0:T(128)}, u32[]{:S(2)}) copy-start(f32[4]{0:T(128)} %knee_ref.1) | copy-start | bytes 52
  15.4 9.4 %copy-start.8 = (f32[4]{0:T(128)S(1)}, f32[4]{0:T(128)}, u32[]{:S(2)}) copy-start(f32[4]{0:T(128)} %white_ref.1) | copy-start | bytes 52
  15.5 1.2 %collective-permute-start.5 = (f32[16,64]{1,0:T(8,128)S(1)}, f32[16,64]{1,0:T(8,128)S(1)}, u32[]{:S(2)}, u32[]{:S(2)}) collective-permute-start(f32[16,64]{1,0:T(8,128)S(1)} %add_add_fusion.refs_0_), channel_id=1, source_target_pairs={{0,1},{1,0},{2,3},{3,2},{4,5},{5,4},{6,7},{7,6},{8,9},{9,8},{10,11... | collective-permute-start | bytes 12296 | tf_op jit(solution)/shard_map/ppermute | solution.py:333
  20.4 17.3 %copy-start.9 = (s32[16]{0:T(128)S(1)}, s32[16]{0:T(128)}, u32[]{:S(2)}) copy-start(s32[16]{0:T(128)} %order_ref.3) | copy-start | bytes 196
  20.4 8.3 %collective-permute-start.6 = (f32[2,64,256]{2,1,0:T(8,128)S(1)}, f32[2,64,256]{2,1,0:T(8,128)S(1)}, u32[]{:S(2)}, u32[]{:S(2)}) collective-permute-start(f32[2,64,256]{2,1,0:T(8,128)S(1)} %get-tuple-element.55), channel_id=1, source_target_pairs={{0,2},{1,3},{2,0},{3,1},{4,6},{5,7},{6,4},{7,5},{8,10},{9,11},{10,... | collective-permute-start | bytes 393224 | tf_op jit(solution)/shard_map/ppermute | solution.py:333
  20.4 12.9 %collective-permute-start.7 = (f32[2,64,256]{2,1,0:T(8,128)S(1)}, f32[2,64,256]{2,1,0:T(8,128)S(1)}, u32[]{:S(2)}, u32[]{:S(2)}) collective-permute-start(f32[2,64,256]{2,1,0:T(8,128)S(1)} %get-tuple-element.56), channel_id=1, source_target_pairs={{0,4},{1,5},{2,6},{3,7},{4,0},{5,1},{6,2},{7,3},{8,12},{9,13},{10,... | collective-permute-start | bytes 393224 | tf_op jit(solution)/shard_map/ppermute | solution.py:333
  22.5 15.2 %collective-permute-start.11 = (f32[2,64,256]{2,1,0:T(8,128)S(1)}, f32[2,64,256]{2,1,0:T(8,128)S(1)}, u32[]{:S(2)}, u32[]{:S(2)}) collective-permute-start(f32[2,64,256]{2,1,0:T(8,128)S(1)} %get-tuple-element.92), channel_id=1, source_target_pairs={{0,6},{1,7},{2,4},{3,5},{4,2},{5,3},{6,0},{7,1},{8,14},{9,15},{10,... | collective-permute-start | bytes 393224 | tf_op jit(solution)/shard_map/ppermute | solution.py:333
  24.9 0.7 %copy-start.5 = (f32[16,32]{1,0:T(8,128)S(1)}, f32[16,32]{1,0:T(8,128)}, u32[]{:S(2)}) copy-start(f32[16,32]{1,0:T(8,128)} %get-tuple-element.47.after_ref) | copy-start | bytes 6148
  33.3 12.1 %collective-permute-start.8 = (f32[2,64,256]{2,1,0:T(8,128)S(1)}, f32[2,64,256]{2,1,0:T(8,128)S(1)}, u32[]{:S(2)}, u32[]{:S(2)}) collective-permute-start(f32[2,64,256]{2,1,0:T(8,128)S(1)} %get-tuple-element.74), channel_id=1, source_target_pairs={{0,2},{1,3},{2,0},{3,1},{4,6},{5,7},{6,4},{7,5},{8,10},{9,11},{10,... | collective-permute-start | bytes 393224 | tf_op jit(solution)/shard_map/ppermute | solution.py:333
  33.6 12.4 %collective-permute-start.9 = (f32[2,64,256]{2,1,0:T(8,128)S(1)}, f32[2,64,256]{2,1,0:T(8,128)S(1)}, u32[]{:S(2)}, u32[]{:S(2)}) collective-permute-start(f32[2,64,256]{2,1,0:T(8,128)S(1)} %get-tuple-element.75), channel_id=1, source_target_pairs={{0,4},{1,5},{2,6},{3,7},{4,0},{5,1},{6,2},{7,3},{8,12},{9,13},{10,... | collective-permute-start | bytes 393224 | tf_op jit(solution)/shard_map/ppermute | solution.py:333
  37.0 9.1 %collective-permute-start.10 = (f32[2,64,256]{2,1,0:T(8,128)S(1)}, f32[2,64,256]{2,1,0:T(8,128)S(1)}, u32[]{:S(2)}, u32[]{:S(2)}) collective-permute-start(f32[2,64,256]{2,1,0:T(8,128)S(1)} %get-tuple-element.76), channel_id=1, source_target_pairs={{0,6},{1,7},{2,4},{3,5},{4,2},{5,3},{6,0},{7,1},{8,14},{9,15},{10,... | collective-permute-start | bytes 393224 | tf_op jit(solution)/shard_map/ppermute | solution.py:333

commit v5 on v4

--- a/solution.py
+++ b/solution.py
@@ -413,7 +413,7 @@
 
     if paired:
         received = [blocks[chunk * chips : (chunk + 1) * chips] for chunk in range(chunks)]
-        for step in reversed(range(1, chips)):
+        for step in range(1, chips):
             received[0][step] = swap(received[0][step], 2 * step, "tm")
     else:
         moved = lax.all_to_all(blocks[0], "tm", split_axis=0, concat_axis=0, tiled=True)
@@ -448,10 +448,10 @@
     )(knee_freq, white_level, fit_amps, table, tile_id, pixel_id)
 
     for chunk in range(1, chunks):
-        near = [received[chunk - 1][:-1], received[chunk], prepared]
+        near = [received[chunk - 1][2:3], received[chunk], prepared]
         near = lax.optimization_barrier(near)
-        received[chunk - 1][:-1], received[chunk], prepared = near
-        for step in reversed(range(1, chips)):
+        received[chunk - 1][2:3], received[chunk], prepared = near
+        for step in range(1, chips):
             received[chunk][step] = swap(received[chunk][step], 2 * step, "tm")
 
     stacked_shape = (HALVES * rows * local_dets, LANES)

time: 68.5 us -> 66.6 us (0.972)
  waiting for transfers between devices: 12.2 us -> 9.74 us
    ppermute x12, waiting for transfers between devices: 12.2 us -> 9.74 us  [swap(): return lax.ppermute(x, axis, [(i, i ^ step) for i in range(size)])]
  transfers between devices with their start and end apart: 12 -> 12, of which waited for: 6 -> 4; matrix products, arithmetic and copies ran while one was open for 1% -> 1% of each run, Pallas kernels for 14% -> 14%
where the time goes in v5:
time: 66.6 us; the launch traced here: 66.3 us
  Pallas kernels  25.6 us (38%)
  starting transfers between devices  15 us (23%)
  blocking collectives  13 us (20%)
  waiting for transfers between devices  9.74 us (15%)
  local copies, waits for them, and re-layouts  1.39 us (2%)
  other arithmetic  0.78 us (1%)
  between operations  0.78 us (1%)
    pallas_call x2, Pallas kernels, shards(): pl.pallas_call(functools.partial(filter_kernel, parts, first_det, per_chu...  16.6 us
    ppermute x12, starting transfers between devices, swap(): return lax.ppermute(x, axis, [(i, i ^ step) for i in range(size)])  15 us
    all_to_all x1, blocking collectives, shards(): lax.all_to_all(spread, ('det', 'tm'), split_axis=0, concat_axis=0, tiled=...  13 us
    ppermute x12, waiting for transfers between devices, swap(): return lax.ppermute(x, axis, [(i, i ^ step) for i in range(size)])  9.74 us
    pallas_call x1, Pallas kernels, shards(): pl.pallas_call(functools.partial(fit_kernel, runs, run_len, paired), out_...  3.73 us
    pallas_call x1, Pallas kernels, shards(): pl.pallas_call(kernel, out_shape=[jax.ShapeDtypeStruct(shape, f32) for sh...  3.72 us
    pallas_call x1, Pallas kernels, shards(): pl.pallas_call(prepare_kernel, out_shape=pairs + [jax.ShapeDtypeStruct(sh...  1.56 us
  transfers between devices with their start and end apart: 12, of which 4 were waited for; matrix products, arithmetic and copies ran while one was open for 1% of the time, Pallas kernels for 14%

profile of v5, /device:TPU:0, one launch (start us, length us, event | category | flops | bytes accessed | tf_op | source)
XLA Modules:
  0.0 66.3 jit_solution(13821838488378097599)
XLA Ops:
  0.7 3.7 %fit_sums.1 = (f32[16,64]{1,0:T(8,128)}, f32[32,8192]{1,0:T(8,128)}) custom-call(s32[32]{0:T(128)} %wafer_ref.3, f32[32,8192]{1,0:T(8,128)} %data_ref.3, bf16[8,16,8192]{2,1,0:T(8,128)(2,1)} %temp_ref.1, bf16[8,16,8192]{2,1,0:T(8,128)(2,1)} %temp_ref.1), custom_call_target="tpu_custom_call" | custom-call | tf_op jit(solution)/shard_map/fit_sums/pallas_call | solution.py:367
  4.4 0.5 collective-permute-start.1
  4.8 0.1 collective-permute-start
  4.9 5.0 %collective-permute-start.4 = (f32[16,64]{1,0:T(8,128)}, f32[16,64]{1,0:T(8,128)S(1)}, u32[]{:S(2)}, u32[]{:S(2)}) collective-permute-start(f32[16,64]{1,0:T(8,128)} %get-tuple-element.50), channel_id=1, source_target_pairs={{0,6},{1,7},{2,4},{3,5},{4,2},{5,3},{6,0},{7,1},{8,14},{9,15},{10,... | collective-permute-start | bytes 12296 | tf_op jit(solution)/shard_map/ppermute | solution.py:333
  10.0 0.0 collective-permute-start.3
  10.0 0.6 collective-permute-start.2
  10.5 1.3 %collective-permute-done.4 = f32[16,64]{1,0:T(8,128)S(1)} collective-permute-done((f32[16,64]{1,0:T(8,128)}, f32[16,64]{1,0:T(8,128)S(1)}, u32[]{:S(2)}, u32[]{:S(2)}) %collective-permute-start.4) | collective-permute-done | bytes 4128 | tf_op jit(solution)/shard_map/ppermute | solution.py:333
  11.8 2.9 %collective-permute-done.3 = f32[16,64]{1,0:T(8,128)S(1)} collective-permute-done((f32[16,64]{1,0:T(8,128)}, f32[16,64]{1,0:T(8,128)S(1)}, u32[]{:S(2)}, u32[]{:S(2)}) %collective-permute-start.3) | collective-permute-done | bytes 4128 | tf_op jit(solution)/shard_map/ppermute | solution.py:333
  14.7 0.7 %add_add_fusion.refs_0_ = f32[16,64]{1,0:T(8,128)S(1)} fusion(f32[16,64]{1,0:T(8,128)S(1)} %collective-permute-done.3, f32[16,64]{1,0:T(8,128)S(1)} %collective-permute-done.4, f32[16,64]{1,0:T(8,128)} %get-tuple-element.50, f32[16,64]{1,0:T(8,128)S(1)} %collective-permute-done.2), kind=kLoop, calls=%fused_computation.1 | loop fusion | flops 3072 | bytes 20480 | tf_op jit(solution)/shard_map/add | solution.py:386
  15.4 0.0 copy-start.7
  15.4 0.0 copy-start.8
  15.5 0.1 collective-permute-start.5
  15.5 1.2 %collective-permute-done.5.refs_1_ = f32[16,64]{1,0:T(8,128)S(1)} collective-permute-done((f32[16,64]{1,0:T(8,128)S(1)}, f32[16,64]{1,0:T(8,128)S(1)}, u32[]{:S(2)}, u32[]{:S(2)}) %collective-permute-start.5) | collective-permute-done | bytes 4128 | tf_op jit(solution)/shard_map/ppermute | solution.py:333
  16.7 0.0 collective-permute-done.1.wide_ref
  16.7 0.0 collective-permute-done.got_ref
  16.7 3.7 %residual.1 = (f32[16,32]{1,0:T(8,128)}, f32[2,64,256]{2,1,0:T(8,128)S(1)}, f32[2,64,256]{2,1,0:T(8,128)S(1)}, f32[2,64,256]{2,1,0:T(8,128)S(1)}, f32[2,64,256]{...) custom-call(s32[32]{0:T(128)S(1)} %copy-done.6, ...), custom_call_target="tpu_custom_call" | custom-call | tf_op jit(solution)/shard_map/residual/pallas_call | solution.py:404
  20.4 2.0 %collective-permute-start.6 = (f32[2,64,256]{2,1,0:T(8,128)S(1)}, f32[2,64,256]{2,1,0:T(8,128)S(1)}, u32[]{:S(2)}, u32[]{:S(2)}) collective-permute-start(f32[2,64,256]{2,1,0:T(8,128)S(1)} %get-tuple-element.52), channel_id=1, source_target_pairs={{0,4},{1,5},{2,6},{3,7},{4,0},{5,1},{6,2},{7,3},{8,12},{9,13},{10,... | collective-permute-start | bytes 393224 | tf_op jit(solution)/shard_map/ppermute | solution.py:333
  22.4 0.0 collective-permute-start.10
  22.5 2.3 %collective-permute-start.11 = (f32[2,64,256]{2,1,0:T(8,128)S(1)}, f32[2,64,256]{2,1,0:T(8,128)S(1)}, u32[]{:S(2)}, u32[]{:S(2)}) collective-permute-start(f32[2,64,256]{2,1,0:T(8,128)S(1)} %get-tuple-element.88), channel_id=1, source_target_pairs={{0,6},{1,7},{2,4},{3,5},{4,2},{5,3},{6,0},{7,1},{8,14},{9,15},{10,... | collective-permute-start | bytes 393224 | tf_op jit(solution)/shard_map/ppermute | solution.py:333
  24.9 0.0 copy-start.5
  24.9 0.7 %copy-done.5 = f32[16,32]{1,0:T(8,128)S(1)} copy-done((f32[16,32]{1,0:T(8,128)S(1)}, f32[16,32]{1,0:T(8,128)}, u32[]{:S(2)}) %copy-start.5) | copy-done | bytes 2072
  25.6 1.6 %prepare.1 = (bf16[256,256]{1,0:T(8,128)(2,1)S(1)}, bf16[256,256]{1,0:T(8,128)(2,1)S(1)}, bf16[256,512]{1,0:T(8,128)(2,1)S(1)}, bf16[256,512]{1,0:T(8,128)(2,1)S...) custom-call(f32[4]{0:T(128)S(1)} %copy-done.7, ...), custom_call_target="tpu_custom_call" | custom-call | bytes 8388608 | tf_op jit(solution)/shard_map/prepare/pallas_call | solution.py:437
  27.1 4.4 %collective-permute-done.6.refs_2_ = f32[2,64,256]{2,1,0:T(8,128)S(1)} collective-permute-done((f32[2,64,256]{2,1,0:T(8,128)S(1)}, f32[2,64,256]{2,1,0:T(8,128)S(1)}, u32[]{:S(2)}, u32[]{:S(2)}) %collective-permute-start.6) | collective-permute-done | bytes 131104 | tf_op jit(solution)/shard_map/ppermute | solution.py:333
  31.5 1.2 %collective-permute-start.8 = (f32[2,64,256]{2,1,0:T(8,128)S(1)}, f32[2,64,256]{2,1,0:T(8,128)S(1)}, u32[]{:S(2)}, u32[]{:S(2)}) collective-permute-start(f32[2,64,256]{2,1,0:T(8,128)S(1)} %get-tuple-element.71), channel_id=1, source_target_pairs={{0,4},{1,5},{2,6},{3,7},{4,0},{5,1},{6,2},{7,3},{8,12},{9,13},{10,... | collective-permute-start | bytes 393224 | tf_op jit(solution)/shard_map/ppermute | solution.py:333
  32.7 3.2 %collective-permute-start.9 = (f32[2,64,256]{2,1,0:T(8,128)S(1)}, f32[2,64,256]{2,1,0:T(8,128)S(1)}, u32[]{:S(2)}, u32[]{:S(2)}) collective-permute-start(f32[2,64,256]{2,1,0:T(8,128)S(1)} %get-tuple-element.72), channel_id=1, source_target_pairs={{0,6},{1,7},{2,4},{3,5},{4,2},{5,3},{6,0},{7,1},{8,14},{9,15},{10,... | collective-permute-start | bytes 393224 | tf_op jit(solution)/shard_map/ppermute | solution.py:333
  35.9 7.7 %filter_and_bin.2 = (f32[2048,128]{1,0:T(8,128)S(1)}, f32[64,64]{1,0:T(8,128)S(1)}) custom-call(s32[16]{0:T(128)S(1)} %copy-done.9, f32[2,64,256]{2,1,0:T(8,128)S(1)} %get-tuple-element.85.refs_0_, f32[2,64,256]{2,1,0:T(8,128)S(1)} %collective-permute-done.10.refs_1_, f32[2,64,256]{2,1,0:T(8,128)S(1)} %collective-permute-done.6.refs_2_, ...), custom_call_target="tpu_custom_call" | custom-call | flops 10485760000 | bytes 2097152 | tf_op jit(solution)/shard_map/filter_and_bin/pallas_call | solution.py:470
  43.6 0.0 collective-permute-done.8.refs_2_
  43.6 8.9 %filter_and_bin.3 = (bf16[4,65536]{1,0:T(4,128)(2,1)}, f32[16,128]{1,0:T(8,128)S(1)}, f32[16,128]{1,0:T(8,128)S(1)}) custom-call(s32[16]{0:T(128)S(1)} %copy-done.9, f32[2,64,256]{2,1,0:T(8,128)S(1)} %get-tuple-element.69.refs_0_, f32[2,64,256]{2,1,0:T(8,128)S(1)} %collective-permute-done.7.refs_1_, f32[2,64,256]{2,1,0:T(8,128)S(1)} %collective-permute-done.8.refs_2_, ...), custom_call_target="tpu_custom_call" | custom-call | flops 10485760000 | bytes 2097152 | tf_op jit(solution)/shard_map/filter_and_bin/pallas_call | solution.py:470
  52.6 0.1 all_to_all.6
  52.6 13.0 %all_to_all.9 = f32[32,1,512]{2,1,0:T(1,128)S(1)} all-to-all(f32[32,1,512]{2,1,0:T(1,128)S(1)} %all_to_all.6), channel_id=1, replica_groups=mesh['det'=4,'tm'=8] {'det','tm'}, dimensions={0} | all-to-all | bytes 131072 | tf_op jit(solution)/shard_map/all_to_all | solution.py:491
  65.7 0.1 reduce_sum.9
  65.7 0.6 fusion
  (27 shorter events, 0.1 us)
Async XLA Ops:
  0.6 4.2 %copy-start.1 = (f32[32,8192]{1,0:T(8,128)S(1)}, f32[32,8192]{1,0:T(8,128)}, u32[]{:S(2)}) copy-start(f32[32,8192]{1,0:T(8,128)} %data_ref.3) | copy-start | bytes 3145732
  0.6 16.1 %copy-start.6 = (s32[32]{0:T(128)S(1)}, s32[32]{0:T(128)}, u32[]{:S(2)}) copy-start(s32[32]{0:T(128)} %wafer_ref.3) | copy-start | bytes 388
  0.7 16.1 %copy-start = (bf16[8,16,8192]{2,1,0:T(8,128)(2,1)S(1)}, bf16[8,16,8192]{2,1,0:T(8,128)(2,1)}, u32[]{:S(2)}) copy-start(bf16[8,16,8192]{2,1,0:T(8,128)(2,1)} %temp_ref.1) | copy-start | bytes 6291460
  4.4 12.3 %collective-permute-start.1 = (f32[32,8192]{1,0:T(8,128)}, f32[32,8192]{1,0:T(8,128)S(1)}, u32[]{:S(2)}, u32[]{:S(2)}) collective-permute-start(f32[32,8192]{1,0:T(8,128)} %get-tuple-element.49), channel_id=1, source_target_pairs={{0,1},{1,0},{2,3},{3,2},{4,5},{5,4},{6,7},{7,6},{8,9},{9,8},{10,11... | collective-permute-start | bytes 3145736 | tf_op jit(solution)/shard_map/ppermute | solution.py:333
  4.8 11.9 %collective-permute-start = (f32[32,8192]{1,0:T(8,128)S(1)}, f32[32,8192]{1,0:T(8,128)S(1)}, u32[]{:S(2)}, u32[]{:S(2)}) collective-permute-start(f32[32,8192]{1,0:T(8,128)S(1)} %copy-done.1), channel_id=1, source_target_pairs={{0,1},{1,0},{2,3},{3,2},{4,5},{5,4},{6,7},{7,6},{8,9},{9,8},{10,11... | collective-permute-start | bytes 3145736 | tf_op jit(solution)/shard_map/ppermute | solution.py:333
  4.9 6.9 %collective-permute-start.4 = (f32[16,64]{1,0:T(8,128)}, f32[16,64]{1,0:T(8,128)S(1)}, u32[]{:S(2)}, u32[]{:S(2)}) collective-permute-start(f32[16,64]{1,0:T(8,128)} %get-tuple-element.50), channel_id=1, source_target_pairs={{0,6},{1,7},{2,4},{3,5},{4,2},{5,3},{6,0},{7,1},{8,14},{9,15},{10,... | collective-permute-start | bytes 12296 | tf_op jit(solution)/shard_map/ppermute | solution.py:333
  10.0 4.8 %collective-permute-start.3 = (f32[16,64]{1,0:T(8,128)}, f32[16,64]{1,0:T(8,128)S(1)}, u32[]{:S(2)}, u32[]{:S(2)}) collective-permute-start(f32[16,64]{1,0:T(8,128)} %get-tuple-element.50), channel_id=1, source_target_pairs={{0,4},{1,5},{2,6},{3,7},{4,0},{5,1},{6,2},{7,3},{8,12},{9,13},{10,... | collective-permute-start | bytes 12296 | tf_op jit(solution)/shard_map/ppermute | solution.py:333
  10.0 4.8 %collective-permute-start.2 = (f32[16,64]{1,0:T(8,128)}, f32[16,64]{1,0:T(8,128)S(1)}, u32[]{:S(2)}, u32[]{:S(2)}) collective-permute-start(f32[16,64]{1,0:T(8,128)} %get-tuple-element.50), channel_id=1, source_target_pairs={{0,2},{1,3},{2,0},{3,1},{4,6},{5,7},{6,4},{7,5},{8,10},{9,11},{10,... | collective-permute-start | bytes 12296 | tf_op jit(solution)/shard_map/ppermute | solution.py:333
  15.4 9.4 %copy-start.2 = (f32[1424,256]{1,0:T(8,128)S(1)}, f32[1424,256]{1,0:T(8,128)}, u32[]{:S(2)}) copy-start(f32[1424,256]{1,0:T(8,128)} %constant.6.clone.table_ref) | copy-start | bytes 4374532
  15.4 9.4 %copy-start.3 = (s32[4,65536]{1,0:T(4,128)S(1)}, s32[4,65536]{1,0:T(4,128)}, u32[]{:S(2)}) copy-start(s32[4,65536]{1,0:T(4,128)} %tile_ref.1) | copy-start | bytes 3145732
  15.4 9.4 %copy-start.4 = (s32[4,65536]{1,0:T(4,128)S(1)}, s32[4,65536]{1,0:T(4,128)}, u32[]{:S(2)}) copy-start(s32[4,65536]{1,0:T(4,128)} %pixel_ref.1) | copy-start | bytes 3145732
  15.4 9.4 %copy-start.7 = (f32[4]{0:T(128)S(1)}, f32[4]{0:T(128)}, u32[]{:S(2)}) copy-start(f32[4]{0:T(128)} %knee_ref.1) | copy-start | bytes 52
  15.4 9.4 %copy-start.8 = (f32[4]{0:T(128)S(1)}, f32[4]{0:T(128)}, u32[]{:S(2)}) copy-start(f32[4]{0:T(128)} %white_ref.1) | copy-start | bytes 52
  15.5 1.2 %collective-permute-start.5 = (f32[16,64]{1,0:T(8,128)S(1)}, f32[16,64]{1,0:T(8,128)S(1)}, u32[]{:S(2)}, u32[]{:S(2)}) collective-permute-start(f32[16,64]{1,0:T(8,128)S(1)} %add_add_fusion.refs_0_), channel_id=1, source_target_pairs={{0,1},{1,0},{2,3},{3,2},{4,5},{5,4},{6,7},{7,6},{8,9},{9,8},{10,11... | collective-permute-start | bytes 12296 | tf_op jit(solution)/shard_map/ppermute | solution.py:333
  20.4 15.4 %copy-start.9 = (s32[16]{0:T(128)S(1)}, s32[16]{0:T(128)}, u32[]{:S(2)}) copy-start(s32[16]{0:T(128)} %order_ref.3) | copy-start | bytes 196
  20.4 11.0 %collective-permute-start.6 = (f32[2,64,256]{2,1,0:T(8,128)S(1)}, f32[2,64,256]{2,1,0:T(8,128)S(1)}, u32[]{:S(2)}, u32[]{:S(2)}) collective-permute-start(f32[2,64,256]{2,1,0:T(8,128)S(1)} %get-tuple-element.52), channel_id=1, source_target_pairs={{0,4},{1,5},{2,6},{3,7},{4,0},{5,1},{6,2},{7,3},{8,12},{9,13},{10,... | collective-permute-start | bytes 393224 | tf_op jit(solution)/shard_map/ppermute | solution.py:333
  22.4 13.4 %collective-permute-start.10 = (f32[2,64,256]{2,1,0:T(8,128)S(1)}, f32[2,64,256]{2,1,0:T(8,128)S(1)}, u32[]{:S(2)}, u32[]{:S(2)}) collective-permute-start(f32[2,64,256]{2,1,0:T(8,128)S(1)} %get-tuple-element.86), channel_id=1, source_target_pairs={{0,2},{1,3},{2,0},{3,1},{4,6},{5,7},{6,4},{7,5},{8,10},{9,11},{10,... | collective-permute-start | bytes 393224 | tf_op jit(solution)/shard_map/ppermute | solution.py:333
  22.5 13.4 %collective-permute-start.11 = (f32[2,64,256]{2,1,0:T(8,128)S(1)}, f32[2,64,256]{2,1,0:T(8,128)S(1)}, u32[]{:S(2)}, u32[]{:S(2)}) collective-permute-start(f32[2,64,256]{2,1,0:T(8,128)S(1)} %get-tuple-element.88), channel_id=1, source_target_pairs={{0,6},{1,7},{2,4},{3,5},{4,2},{5,3},{6,0},{7,1},{8,14},{9,15},{10,... | collective-permute-start | bytes 393224 | tf_op jit(solution)/shard_map/ppermute | solution.py:333
  24.9 0.7 %copy-start.5 = (f32[16,32]{1,0:T(8,128)S(1)}, f32[16,32]{1,0:T(8,128)}, u32[]{:S(2)}) copy-start(f32[16,32]{1,0:T(8,128)} %get-tuple-element.45.after_ref) | copy-start | bytes 6148
  31.5 12.1 %collective-permute-start.7 = (f32[2,64,256]{2,1,0:T(8,128)S(1)}, f32[2,64,256]{2,1,0:T(8,128)S(1)}, u32[]{:S(2)}, u32[]{:S(2)}) collective-permute-start(f32[2,64,256]{2,1,0:T(8,128)S(1)} %get-tuple-element.70), channel_id=1, source_target_pairs={{0,2},{1,3},{2,0},{3,1},{4,6},{5,7},{6,4},{7,5},{8,10},{9,11},{10,... | collective-permute-start | bytes 393224 | tf_op jit(solution)/shard_map/ppermute | solution.py:333
  31.5 12.1 %collective-permute-start.8 = (f32[2,64,256]{2,1,0:T(8,128)S(1)}, f32[2,64,256]{2,1,0:T(8,128)S(1)}, u32[]{:S(2)}, u32[]{:S(2)}) collective-permute-start(f32[2,64,256]{2,1,0:T(8,128)S(1)} %get-tuple-element.71), channel_id=1, source_target_pairs={{0,4},{1,5},{2,6},{3,7},{4,0},{5,1},{6,2},{7,3},{8,12},{9,13},{10,... | collective-permute-start | bytes 393224 | tf_op jit(solution)/shard_map/ppermute | solution.py:333
  32.7 10.9 %collective-permute-start.9 = (f32[2,64,256]{2,1,0:T(8,128)S(1)}, f32[2,64,256]{2,1,0:T(8,128)S(1)}, u32[]{:S(2)}, u32[]{:S(2)}) collective-permute-start(f32[2,64,256]{2,1,0:T(8,128)S(1)} %get-tuple-element.72), channel_id=1, source_target_pairs={{0,6},{1,7},{2,4},{3,5},{4,2},{5,3},{6,0},{7,1},{8,14},{9,15},{10,... | collective-permute-start | bytes 393224 | tf_op jit(solution)/shard_map/ppermute | solution.py:333

commit v6 on v5

--- a/solution.py
+++ b/solution.py
@@ -102,8 +102,9 @@
     for column in range(modes):
         for run in range(runs):
             now = joined[run]
-            pivot_row = now[column : column + 1, :] / now[column : column + 1, column : column + 1]
-            rest = now - now[:, column : column + 1] * pivot_row
+            factor = jnp.broadcast_to(now[:, column : column + 1], now.shape)
+            pivot_row = now[column : column + 1, :] / factor[column : column + 1, :]
+            rest = now - factor * pivot_row
             joined[run] = jnp.where(row_index == column, pivot_row, rest)
     return [now[:, modes:] for now in joined]
 

time: 66.6 us -> 66.6 us (level)
  no operation moved by 1% of the time
where the time goes in v6:
time: 66.6 us; the launch traced here: 66.3 us
  Pallas kernels  25.6 us (38%)
  starting transfers between devices  15 us (23%)
  blocking collectives  13 us (20%)
  waiting for transfers between devices  9.74 us (15%)
  local copies, waits for them, and re-layouts  1.39 us (2%)
  other arithmetic  0.78 us (1%)
  between operations  0.78 us (1%)
    pallas_call x2, Pallas kernels, shards(): pl.pallas_call(functools.partial(filter_kernel, parts, first_det, per_chu...  16.6 us
    ppermute x12, starting transfers between devices, swap(): return lax.ppermute(x, axis, [(i, i ^ step) for i in range(size)])  15 us
    all_to_all x1, blocking collectives, shards(): lax.all_to_all(spread, ('det', 'tm'), split_axis=0, concat_axis=0, tiled=...  13 us
    ppermute x12, waiting for transfers between devices, swap(): return lax.ppermute(x, axis, [(i, i ^ step) for i in range(size)])  9.74 us
    pallas_call x1, Pallas kernels, shards(): pl.pallas_call(functools.partial(fit_kernel, runs, run_len, paired), out_...  3.73 us
    pallas_call x1, Pallas kernels, shards(): pl.pallas_call(kernel, out_shape=[jax.ShapeDtypeStruct(shape, f32) for sh...  3.72 us
    pallas_call x1, Pallas kernels, shards(): pl.pallas_call(prepare_kernel, out_shape=pairs + [jax.ShapeDtypeStruct(sh...  1.56 us
  transfers between devices with their start and end apart: 12, of which 4 were waited for; matrix products, arithmetic and copies ran while one was open for 1% of the time, Pallas kernels for 14%

profile of v6, /device:TPU:0, one launch (start us, length us, event | category | flops | bytes accessed | tf_op | source)
XLA Modules:
  0.0 66.3 jit_solution(13821838488378097599)
XLA Ops:
  0.7 3.7 %fit_sums.1 = (f32[16,64]{1,0:T(8,128)}, f32[32,8192]{1,0:T(8,128)}) custom-call(s32[32]{0:T(128)} %wafer_ref.3, f32[32,8192]{1,0:T(8,128)} %data_ref.3, bf16[8,16,8192]{2,1,0:T(8,128)(2,1)} %temp_ref.1, bf16[8,16,8192]{2,1,0:T(8,128)(2,1)} %temp_ref.1), custom_call_target="tpu_custom_call" | custom-call | tf_op jit(solution)/shard_map/fit_sums/pallas_call | solution.py:368
  4.4 0.5 collective-permute-start.1
  4.8 0.1 collective-permute-start
  4.9 5.0 %collective-permute-start.4 = (f32[16,64]{1,0:T(8,128)}, f32[16,64]{1,0:T(8,128)S(1)}, u32[]{:S(2)}, u32[]{:S(2)}) collective-permute-start(f32[16,64]{1,0:T(8,128)} %get-tuple-element.50), channel_id=1, source_target_pairs={{0,6},{1,7},{2,4},{3,5},{4,2},{5,3},{6,0},{7,1},{8,14},{9,15},{10,... | collective-permute-start | bytes 12296 | tf_op jit(solution)/shard_map/ppermute | solution.py:334
  10.0 0.0 collective-permute-start.3
  10.0 0.6 collective-permute-start.2
  10.5 1.3 %collective-permute-done.4 = f32[16,64]{1,0:T(8,128)S(1)} collective-permute-done((f32[16,64]{1,0:T(8,128)}, f32[16,64]{1,0:T(8,128)S(1)}, u32[]{:S(2)}, u32[]{:S(2)}) %collective-permute-start.4) | collective-permute-done | bytes 4128 | tf_op jit(solution)/shard_map/ppermute | solution.py:334
  11.8 2.9 %collective-permute-done.3 = f32[16,64]{1,0:T(8,128)S(1)} collective-permute-done((f32[16,64]{1,0:T(8,128)}, f32[16,64]{1,0:T(8,128)S(1)}, u32[]{:S(2)}, u32[]{:S(2)}) %collective-permute-start.3) | collective-permute-done | bytes 4128 | tf_op jit(solution)/shard_map/ppermute | solution.py:334
  14.7 0.7 %add_add_fusion.refs_0_ = f32[16,64]{1,0:T(8,128)S(1)} fusion(f32[16,64]{1,0:T(8,128)S(1)} %collective-permute-done.3, f32[16,64]{1,0:T(8,128)S(1)} %collective-permute-done.4, f32[16,64]{1,0:T(8,128)} %get-tuple-element.50, f32[16,64]{1,0:T(8,128)S(1)} %collective-permute-done.2), kind=kLoop, calls=%fused_computation.1 | loop fusion | flops 3072 | bytes 20480 | tf_op jit(solution)/shard_map/add | solution.py:387
  15.4 0.0 copy-start.7
  15.4 0.0 copy-start.8
  15.5 0.1 collective-permute-start.5
  15.5 1.2 %collective-permute-done.5.refs_1_ = f32[16,64]{1,0:T(8,128)S(1)} collective-permute-done((f32[16,64]{1,0:T(8,128)S(1)}, f32[16,64]{1,0:T(8,128)S(1)}, u32[]{:S(2)}, u32[]{:S(2)}) %collective-permute-start.5) | collective-permute-done | bytes 4128 | tf_op jit(solution)/shard_map/ppermute | solution.py:334
  16.7 0.0 collective-permute-done.1.wide_ref
  16.7 0.0 collective-permute-done.got_ref
  16.7 3.7 %residual.1 = (f32[16,32]{1,0:T(8,128)}, f32[2,64,256]{2,1,0:T(8,128)S(1)}, f32[2,64,256]{2,1,0:T(8,128)S(1)}, f32[2,64,256]{2,1,0:T(8,128)S(1)}, f32[2,64,256]{...) custom-call(s32[32]{0:T(128)S(1)} %copy-done.6, ...), custom_call_target="tpu_custom_call" | custom-call | tf_op jit(solution)/shard_map/residual/pallas_call | solution.py:405
  20.4 2.0 %collective-permute-start.6 = (f32[2,64,256]{2,1,0:T(8,128)S(1)}, f32[2,64,256]{2,1,0:T(8,128)S(1)}, u32[]{:S(2)}, u32[]{:S(2)}) collective-permute-start(f32[2,64,256]{2,1,0:T(8,128)S(1)} %get-tuple-element.52), channel_id=1, source_target_pairs={{0,4},{1,5},{2,6},{3,7},{4,0},{5,1},{6,2},{7,3},{8,12},{9,13},{10,... | collective-permute-start | bytes 393224 | tf_op jit(solution)/shard_map/ppermute | solution.py:334
  22.4 0.0 collective-permute-start.10
  22.5 2.3 %collective-permute-start.11 = (f32[2,64,256]{2,1,0:T(8,128)S(1)}, f32[2,64,256]{2,1,0:T(8,128)S(1)}, u32[]{:S(2)}, u32[]{:S(2)}) collective-permute-start(f32[2,64,256]{2,1,0:T(8,128)S(1)} %get-tuple-element.88), channel_id=1, source_target_pairs={{0,6},{1,7},{2,4},{3,5},{4,2},{5,3},{6,0},{7,1},{8,14},{9,15},{10,... | collective-permute-start | bytes 393224 | tf_op jit(solution)/shard_map/ppermute | solution.py:334
  24.9 0.0 copy-start.5
  24.9 0.7 %copy-done.5 = f32[16,32]{1,0:T(8,128)S(1)} copy-done((f32[16,32]{1,0:T(8,128)S(1)}, f32[16,32]{1,0:T(8,128)}, u32[]{:S(2)}) %copy-start.5) | copy-done | bytes 2072
  25.6 1.6 %prepare.1 = (bf16[256,256]{1,0:T(8,128)(2,1)S(1)}, bf16[256,256]{1,0:T(8,128)(2,1)S(1)}, bf16[256,512]{1,0:T(8,128)(2,1)S(1)}, bf16[256,512]{1,0:T(8,128)(2,1)S...) custom-call(f32[4]{0:T(128)S(1)} %copy-done.7, ...), custom_call_target="tpu_custom_call" | custom-call | bytes 8388608 | tf_op jit(solution)/shard_map/prepare/pallas_call | solution.py:438
  27.1 4.4 %collective-permute-done.6.refs_2_ = f32[2,64,256]{2,1,0:T(8,128)S(1)} collective-permute-done((f32[2,64,256]{2,1,0:T(8,128)S(1)}, f32[2,64,256]{2,1,0:T(8,128)S(1)}, u32[]{:S(2)}, u32[]{:S(2)}) %collective-permute-start.6) | collective-permute-done | bytes 131104 | tf_op jit(solution)/shard_map/ppermute | solution.py:334
  31.5 1.2 %collective-permute-start.8 = (f32[2,64,256]{2,1,0:T(8,128)S(1)}, f32[2,64,256]{2,1,0:T(8,128)S(1)}, u32[]{:S(2)}, u32[]{:S(2)}) collective-permute-start(f32[2,64,256]{2,1,0:T(8,128)S(1)} %get-tuple-element.71), channel_id=1, source_target_pairs={{0,4},{1,5},{2,6},{3,7},{4,0},{5,1},{6,2},{7,3},{8,12},{9,13},{10,... | collective-permute-start | bytes 393224 | tf_op jit(solution)/shard_map/ppermute | solution.py:334
  32.7 3.2 %collective-permute-start.9 = (f32[2,64,256]{2,1,0:T(8,128)S(1)}, f32[2,64,256]{2,1,0:T(8,128)S(1)}, u32[]{:S(2)}, u32[]{:S(2)}) collective-permute-start(f32[2,64,256]{2,1,0:T(8,128)S(1)} %get-tuple-element.72), channel_id=1, source_target_pairs={{0,6},{1,7},{2,4},{3,5},{4,2},{5,3},{6,0},{7,1},{8,14},{9,15},{10,... | collective-permute-start | bytes 393224 | tf_op jit(solution)/shard_map/ppermute | solution.py:334
  35.9 7.7 %filter_and_bin.2 = (f32[2048,128]{1,0:T(8,128)S(1)}, f32[64,64]{1,0:T(8,128)S(1)}) custom-call(s32[16]{0:T(128)S(1)} %copy-done.9, f32[2,64,256]{2,1,0:T(8,128)S(1)} %get-tuple-element.85.refs_0_, f32[2,64,256]{2,1,0:T(8,128)S(1)} %collective-permute-done.10.refs_1_, f32[2,64,256]{2,1,0:T(8,128)S(1)} %collective-permute-done.6.refs_2_, ...), custom_call_target="tpu_custom_call" | custom-call | flops 10485760000 | bytes 2097152 | tf_op jit(solution)/shard_map/filter_and_bin/pallas_call | solution.py:471
  43.6 0.0 collective-permute-done.8.refs_2_
  43.6 8.9 %filter_and_bin.3 = (bf16[4,65536]{1,0:T(4,128)(2,1)}, f32[16,128]{1,0:T(8,128)S(1)}, f32[16,128]{1,0:T(8,128)S(1)}) custom-call(s32[16]{0:T(128)S(1)} %copy-done.9, f32[2,64,256]{2,1,0:T(8,128)S(1)} %get-tuple-element.69.refs_0_, f32[2,64,256]{2,1,0:T(8,128)S(1)} %collective-permute-done.7.refs_1_, f32[2,64,256]{2,1,0:T(8,128)S(1)} %collective-permute-done.8.refs_2_, ...), custom_call_target="tpu_custom_call" | custom-call | flops 10485760000 | bytes 2097152 | tf_op jit(solution)/shard_map/filter_and_bin/pallas_call | solution.py:471
  52.6 0.1 all_to_all.6
  52.6 13.0 %all_to_all.9 = f32[32,1,512]{2,1,0:T(1,128)S(1)} all-to-all(f32[32,1,512]{2,1,0:T(1,128)S(1)} %all_to_all.6), channel_id=1, replica_groups=mesh['det'=4,'tm'=8] {'det','tm'}, dimensions={0} | all-to-all | bytes 131072 | tf_op jit(solution)/shard_map/all_to_all | solution.py:492
  65.7 0.1 reduce_sum.9
  65.8 0.6 fusion
  (27 shorter events, 0.1 us)
Async XLA Ops:
  0.6 4.2 %copy-start.1 = (f32[32,8192]{1,0:T(8,128)S(1)}, f32[32,8192]{1,0:T(8,128)}, u32[]{:S(2)}) copy-start(f32[32,8192]{1,0:T(8,128)} %data_ref.3) | copy-start | bytes 3145732
  0.6 16.1 %copy-start.6 = (s32[32]{0:T(128)S(1)}, s32[32]{0:T(128)}, u32[]{:S(2)}) copy-start(s32[32]{0:T(128)} %wafer_ref.3) | copy-start | bytes 388
  0.7 16.1 %copy-start = (bf16[8,16,8192]{2,1,0:T(8,128)(2,1)S(1)}, bf16[8,16,8192]{2,1,0:T(8,128)(2,1)}, u32[]{:S(2)}) copy-start(bf16[8,16,8192]{2,1,0:T(8,128)(2,1)} %temp_ref.1) | copy-start | bytes 6291460
  4.4 12.3 %collective-permute-start.1 = (f32[32,8192]{1,0:T(8,128)}, f32[32,8192]{1,0:T(8,128)S(1)}, u32[]{:S(2)}, u32[]{:S(2)}) collective-permute-start(f32[32,8192]{1,0:T(8,128)} %get-tuple-element.49), channel_id=1, source_target_pairs={{0,1},{1,0},{2,3},{3,2},{4,5},{5,4},{6,7},{7,6},{8,9},{9,8},{10,11... | collective-permute-start | bytes 3145736 | tf_op jit(solution)/shard_map/ppermute | solution.py:334
  4.8 11.9 %collective-permute-start = (f32[32,8192]{1,0:T(8,128)S(1)}, f32[32,8192]{1,0:T(8,128)S(1)}, u32[]{:S(2)}, u32[]{:S(2)}) collective-permute-start(f32[32,8192]{1,0:T(8,128)S(1)} %copy-done.1), channel_id=1, source_target_pairs={{0,1},{1,0},{2,3},{3,2},{4,5},{5,4},{6,7},{7,6},{8,9},{9,8},{10,11... | collective-permute-start | bytes 3145736 | tf_op jit(solution)/shard_map/ppermute | solution.py:334
  4.9 6.9 %collective-permute-start.4 = (f32[16,64]{1,0:T(8,128)}, f32[16,64]{1,0:T(8,128)S(1)}, u32[]{:S(2)}, u32[]{:S(2)}) collective-permute-start(f32[16,64]{1,0:T(8,128)} %get-tuple-element.50), channel_id=1, source_target_pairs={{0,6},{1,7},{2,4},{3,5},{4,2},{5,3},{6,0},{7,1},{8,14},{9,15},{10,... | collective-permute-start | bytes 12296 | tf_op jit(solution)/shard_map/ppermute | solution.py:334
  10.0 4.8 %collective-permute-start.3 = (f32[16,64]{1,0:T(8,128)}, f32[16,64]{1,0:T(8,128)S(1)}, u32[]{:S(2)}, u32[]{:S(2)}) collective-permute-start(f32[16,64]{1,0:T(8,128)} %get-tuple-element.50), channel_id=1, source_target_pairs={{0,4},{1,5},{2,6},{3,7},{4,0},{5,1},{6,2},{7,3},{8,12},{9,13},{10,... | collective-permute-start | bytes 12296 | tf_op jit(solution)/shard_map/ppermute | solution.py:334
  10.0 4.8 %collective-permute-start.2 = (f32[16,64]{1,0:T(8,128)}, f32[16,64]{1,0:T(8,128)S(1)}, u32[]{:S(2)}, u32[]{:S(2)}) collective-permute-start(f32[16,64]{1,0:T(8,128)} %get-tuple-element.50), channel_id=1, source_target_pairs={{0,2},{1,3},{2,0},{3,1},{4,6},{5,7},{6,4},{7,5},{8,10},{9,11},{10,... | collective-permute-start | bytes 12296 | tf_op jit(solution)/shard_map/ppermute | solution.py:334
  15.4 9.4 %copy-start.2 = (f32[1424,256]{1,0:T(8,128)S(1)}, f32[1424,256]{1,0:T(8,128)}, u32[]{:S(2)}) copy-start(f32[1424,256]{1,0:T(8,128)} %constant.6.clone.table_ref) | copy-start | bytes 4374532
  15.4 9.4 %copy-start.3 = (s32[4,65536]{1,0:T(4,128)S(1)}, s32[4,65536]{1,0:T(4,128)}, u32[]{:S(2)}) copy-start(s32[4,65536]{1,0:T(4,128)} %tile_ref.1) | copy-start | bytes 3145732
  15.4 9.4 %copy-start.4 = (s32[4,65536]{1,0:T(4,128)S(1)}, s32[4,65536]{1,0:T(4,128)}, u32[]{:S(2)}) copy-start(s32[4,65536]{1,0:T(4,128)} %pixel_ref.1) | copy-start | bytes 3145732
  15.4 9.4 %copy-start.7 = (f32[4]{0:T(128)S(1)}, f32[4]{0:T(128)}, u32[]{:S(2)}) copy-start(f32[4]{0:T(128)} %knee_ref.1) | copy-start | bytes 52
  15.4 9.4 %copy-start.8 = (f32[4]{0:T(128)S(1)}, f32[4]{0:T(128)}, u32[]{:S(2)}) copy-start(f32[4]{0:T(128)} %white_ref.1) | copy-start | bytes 52
  15.5 1.2 %collective-permute-start.5 = (f32[16,64]{1,0:T(8,128)S(1)}, f32[16,64]{1,0:T(8,128)S(1)}, u32[]{:S(2)}, u32[]{:S(2)}) collective-permute-start(f32[16,64]{1,0:T(8,128)S(1)} %add_add_fusion.refs_0_), channel_id=1, source_target_pairs={{0,1},{1,0},{2,3},{3,2},{4,5},{5,4},{6,7},{7,6},{8,9},{9,8},{10,11... | collective-permute-start | bytes 12296 | tf_op jit(solution)/shard_map/ppermute | solution.py:334
  20.4 15.4 %copy-start.9 = (s32[16]{0:T(128)S(1)}, s32[16]{0:T(128)}, u32[]{:S(2)}) copy-start(s32[16]{0:T(128)} %order_ref.3) | copy-start | bytes 196
  20.4 11.0 %collective-permute-start.6 = (f32[2,64,256]{2,1,0:T(8,128)S(1)}, f32[2,64,256]{2,1,0:T(8,128)S(1)}, u32[]{:S(2)}, u32[]{:S(2)}) collective-permute-start(f32[2,64,256]{2,1,0:T(8,128)S(1)} %get-tuple-element.52), channel_id=1, source_target_pairs={{0,4},{1,5},{2,6},{3,7},{4,0},{5,1},{6,2},{7,3},{8,12},{9,13},{10,... | collective-permute-start | bytes 393224 | tf_op jit(solution)/shard_map/ppermute | solution.py:334
  22.4 13.4 %collective-permute-start.10 = (f32[2,64,256]{2,1,0:T(8,128)S(1)}, f32[2,64,256]{2,1,0:T(8,128)S(1)}, u32[]{:S(2)}, u32[]{:S(2)}) collective-permute-start(f32[2,64,256]{2,1,0:T(8,128)S(1)} %get-tuple-element.86), channel_id=1, source_target_pairs={{0,2},{1,3},{2,0},{3,1},{4,6},{5,7},{6,4},{7,5},{8,10},{9,11},{10,... | collective-permute-start | bytes 393224 | tf_op jit(solution)/shard_map/ppermute | solution.py:334
  22.5 13.4 %collective-permute-start.11 = (f32[2,64,256]{2,1,0:T(8,128)S(1)}, f32[2,64,256]{2,1,0:T(8,128)S(1)}, u32[]{:S(2)}, u32[]{:S(2)}) collective-permute-start(f32[2,64,256]{2,1,0:T(8,128)S(1)} %get-tuple-element.88), channel_id=1, source_target_pairs={{0,6},{1,7},{2,4},{3,5},{4,2},{5,3},{6,0},{7,1},{8,14},{9,15},{10,... | collective-permute-start | bytes 393224 | tf_op jit(solution)/shard_map/ppermute | solution.py:334
  24.9 0.7 %copy-start.5 = (f32[16,32]{1,0:T(8,128)S(1)}, f32[16,32]{1,0:T(8,128)}, u32[]{:S(2)}) copy-start(f32[16,32]{1,0:T(8,128)} %get-tuple-element.45.after_ref) | copy-start | bytes 6148
  31.5 12.1 %collective-permute-start.7 = (f32[2,64,256]{2,1,0:T(8,128)S(1)}, f32[2,64,256]{2,1,0:T(8,128)S(1)}, u32[]{:S(2)}, u32[]{:S(2)}) collective-permute-start(f32[2,64,256]{2,1,0:T(8,128)S(1)} %get-tuple-element.70), channel_id=1, source_target_pairs={{0,2},{1,3},{2,0},{3,1},{4,6},{5,7},{6,4},{7,5},{8,10},{9,11},{10,... | collective-permute-start | bytes 393224 | tf_op jit(solution)/shard_map/ppermute | solution.py:334
  31.5 12.1 %collective-permute-start.8 = (f32[2,64,256]{2,1,0:T(8,128)S(1)}, f32[2,64,256]{2,1,0:T(8,128)S(1)}, u32[]{:S(2)}, u32[]{:S(2)}) collective-permute-start(f32[2,64,256]{2,1,0:T(8,128)S(1)} %get-tuple-element.71), channel_id=1, source_target_pairs={{0,4},{1,5},{2,6},{3,7},{4,0},{5,1},{6,2},{7,3},{8,12},{9,13},{10,... | collective-permute-start | bytes 393224 | tf_op jit(solution)/shard_map/ppermute | solution.py:334
  32.7 10.9 %collective-permute-start.9 = (f32[2,64,256]{2,1,0:T(8,128)S(1)}, f32[2,64,256]{2,1,0:T(8,128)S(1)}, u32[]{:S(2)}, u32[]{:S(2)}) collective-permute-start(f32[2,64,256]{2,1,0:T(8,128)S(1)} %get-tuple-element.72), channel_id=1, source_target_pairs={{0,6},{1,7},{2,4},{3,5},{4,2},{5,3},{6,0},{7,1},{8,14},{9,15},{10,... | collective-permute-start | bytes 393224 | tf_op jit(solution)/shard_map/ppermute | solution.py:334
